TPU v7x, 32 devices: a whole 2x2x4 slice. The times are simulated.
32 devices in a mesh: rows: 4 (over z), cols: 4 (over x, core), layers: 2 (over y).
Axes of the slice: x: 2, y: 2, z: 4, core: 2. Of those that a mesh axis runs over, the one named last changes fastest.
Arguments:
- term_now: bfloat16 [96, 128, 2048], P('rows', 'layers', 'cols'), may hold values from -6 to 6
- term_prev: bfloat16 [96, 128, 2048], P('rows', 'layers', 'cols'), may hold values from -6 to 6
- cotangent: bfloat16 [96, 128, 2048], P('rows', None, 'cols'), may hold values from -6 to 6
- ham_blocks: bfloat16 [96, 25, 128, 128], P('rows', None, 'layers'), as said below
- block_mask: int32 [96, 25], P('rows'), may hold values from 0 to 1, as said below
- ham_slope: bfloat16 [96, 25, 128, 128], P('rows', None, 'layers'), may hold values from -0.0012207031 to 0.0012207031
- atom_owner: int32 [96, 128], P('rows'), may hold values from 0 to 63, never falling along the last dimension, each value on 1 to 4 neighbouring positions
Outputs:
- term_next: bfloat16 [96, 128, 2048], P('rows', 'layers', 'cols')
- grad_term: bfloat16 [96, 128, 2048], P('rows', 'layers', 'cols')
- forces: float32 [96, 64], P('rows')
Inputs may be any that keep to these rules, and one draw needn't show every extreme that they name: ham_blocks[i, d] is the transpose of ham_blocks[(i + d - 12) mod 96, 24 - d]: H is symmetric. block_mask[i, d] equals block_mask[(i + d - 12) mod 96, 24 - d], and block_mask[i, 12] is 1. Each row of atom_owner never falls; each atom owns 1 to 4 consecutive row orbitals.
All inputs are finite; a program needn't handle non-finite values.
Results may differ from a plain program's by a relative error of at most 0.005.
Values may be sent and summed in bfloat16 or wider, within the bound.
No kernel may reach another device: no remote copies, remote signals or barrier semaphores. Data moves between devices by JAX's collectives and lax.ppermute only.
A program may use at most 128 MiB of HBM per device.

v0:
```python
import jax
import jax.numpy as jnp
from jax import lax
from jax.sharding import PartitionSpec as P

APB = 64


def extended_2(cells, sides, width):
    for axis, dim in sides:
        count = lax.axis_size(axis)
        head = lax.slice_in_dim(cells, 0, width, axis=dim)
        tail = lax.slice_in_dim(cells, cells.shape[dim] - width, cells.shape[dim], axis=dim)
        cells = jnp.concatenate(
            [
                lax.ppermute(tail, axis, [(i, (i + 1) % count) for i in range(count)]),
                cells,
                lax.ppermute(head, axis, [((i + 1) % count, i) for i in range(count)]),
            ],
            axis=dim,
        )
    return cells


def from_behind(value, axis, steps):
    count = lax.axis_size(axis)
    pairs = [(source, (source + steps) % count) for source in range(count)]
    return lax.ppermute(value, axis, pairs)


def apply_blocks(ham_blocks, block_mask, extended, rows_dev):

    def apply_advance(offset, summed):
        blocks = lax.dynamic_index_in_dim(ham_blocks, offset, 1, keepdims=False)
        kept_mask = lax.dynamic_index_in_dim(block_mask, offset, 1, keepdims=False)
        masked = blocks * kept_mask.astype(jnp.bfloat16)[:, None, None]
        window = lax.dynamic_slice_in_dim(extended, offset, rows_dev, 0)
        return summed + jnp.einsum(
            "bnm,bnc->bmc", masked, window, preferred_element_type=jnp.float32
        )

    initial = jnp.zeros((rows_dev, ham_blocks.shape[3], extended.shape[2]), jnp.float32)
    return lax.fori_loop(0, ham_blocks.shape[1], apply_advance, initial)


def push_blocks(ham_blocks, block_mask, cotangent, rows_dev):
    reach_rows = (ham_blocks.shape[1] - 1) // 2

    def push_advance(offset, summed):
        blocks = lax.dynamic_index_in_dim(ham_blocks, offset, 1, keepdims=False)
        kept_mask = lax.dynamic_index_in_dim(block_mask, offset, 1, keepdims=False)
        masked = blocks * kept_mask.astype(jnp.bfloat16)[:, None, None]
        sources = jnp.einsum("bnm,bmc->bnc", masked, cotangent, preferred_element_type=jnp.float32)
        window = lax.dynamic_slice_in_dim(summed, offset, rows_dev, 0)
        return lax.dynamic_update_slice_in_dim(summed, window + sources, offset, 0)

    initial = jnp.zeros(
        (rows_dev + 2 * reach_rows, ham_blocks.shape[2], cotangent.shape[2]), jnp.float32
    )
    return lax.fori_loop(0, ham_blocks.shape[1], push_advance, initial)


def force_rows(ham_slope, block_mask, extended, cotangent, rows_dev):

    def force_advance(offset, summed):
        kept_mask = lax.dynamic_index_in_dim(block_mask, offset, 1, keepdims=False).astype(
            jnp.float32
        )
        window = lax.dynamic_slice_in_dim(extended, offset, rows_dev, 0)
        pair_grads = jnp.einsum(
            "bnc,bmc->bnm", window, cotangent, preferred_element_type=jnp.float32
        )
        slope_block = lax.dynamic_index_in_dim(ham_slope, offset, 1, keepdims=False).astype(
            jnp.float32
        )
        return summed + 2.0 * kept_mask[:, None] * jnp.sum(pair_grads * slope_block, axis=1)

    initial = jnp.zeros((rows_dev, cotangent.shape[1]), jnp.float32)
    return lax.fori_loop(0, ham_slope.shape[1], force_advance, initial)


def local(term_now, term_prev, cotangent, ham_blocks, block_mask, ham_slope, atom_owner):
    rows_dev = ham_blocks.shape[0]
    reach_rows = (ham_blocks.shape[1] - 1) // 2
    ext_state = extended_2(term_now, (("rows", 0),), reach_rows)
    forward = lax.psum_scatter(
        apply_blocks(ham_blocks, block_mask, ext_state, rows_dev),
        "layers",
        scatter_dimension=1,
        tiled=True,
    )
    pushed = push_blocks(ham_blocks, block_mask, cotangent, rows_dev)
    from_above = from_behind(pushed[:reach_rows], "rows", -1)
    from_below = from_behind(pushed[rows_dev + reach_rows :], "rows", 1)
    backward = pushed[reach_rows : reach_rows + rows_dev]
    backward = backward.at[:reach_rows].add(from_below)
    backward = backward.at[rows_dev - reach_rows :].add(from_above)
    row_force = force_rows(ham_slope, block_mask, ext_state, cotangent, rows_dev)
    term_next = (2.0 * forward - term_prev.astype(jnp.float32)).astype(jnp.bfloat16)
    grad_term = (2.0 * backward).astype(jnp.bfloat16)
    atom_ids = lax.broadcasted_iota(jnp.int32, (1, 1, APB), 2)
    owners = (atom_owner[:, :, None] == atom_ids).astype(jnp.float32)
    partial_force = jnp.einsum("bm,bma->ba", row_force, owners)
    forces = lax.psum(partial_force, ("cols", "layers"))
    return (term_next, grad_term, forces)


def solution(mesh):
    return jax.shard_map(
        local,
        mesh=mesh,
        in_specs=(
            P("rows", "layers", "cols"),
            P("rows", "layers", "cols"),
            P("rows", None, "cols"),
            P("rows", None, "layers", None),
            P("rows", None),
            P("rows", None, "layers", None),
            P("rows", None),
        ),
        out_specs=(P("rows", "layers", "cols"), P("rows", "layers", "cols"), P("rows", None)),
        check_vma=False,
    )
```

profile of v0, /device:TPU:0, one launch (start us, length us, event | category | flops | bytes accessed | tf_op | source)
XLA Modules:
  0.0 452.1 jit_solution(7391670305196008782)
XLA Ops:
  15.1 11.1 %copy.10 = bf16[24,25,64,128]{3,2,0,1:T(8,128)(2,1)} copy(bf16[24,25,64,128]{3,2,1,0:T(8,128)(2,1)} %param.20) | data formatting | bytes 19660800
  29.6 110.2 %while.43 = (s32[]{:T(128)}, f32[48,64,512]{2,1,0:T(8,128)}, bf16[24,25,64,128]{3,2,0,1:T(8,128)(2,1)}, s32[24,25]{0,1:T(8,128)S(1)}, bf16[24,128,512]{2,1,0:T(8,128)(2,1)S(1)}, /*index=5*/s32[]{:T(128)}) while((s32[]{:T(128)}, f32[48,64,512]{2,1,0:T(8,128)}, bf16[24,25,64,128]{3,2,0,1:T(8,128)(2,1)}, s32[24,25]{0,1:T(8,128)S(1)}, ...), condition=%wide.region_4.5_spmd, body=%wide.region_3.4_spmd.sunk | while | flops 202309664 | bytes 9831689 | solution.py:60
  130.9 4.5 add_dynamic-update-slice_fusion.3
  135.4 4.5 add_dynamic-update-slice_fusion.3
  155.4 180.2 %while.44 = (s32[]{:T(128)}, f32[24,128,512]{2,1,0:T(8,128)}, bf16[24,25,64,128]{3,2,0,1:T(8,128)(2,1)}, s32[24,25]{0,1:T(8,128)S(1)}, bf16[48,64,512]{2,1,0:T(8,128)(2,1)}, /*index=5*/s32[]{:T(128)}, s32[]{:T(128)}) while((s32[]{:T(128)}, f32[24,128,512]{2,1,0:T(8,128)}, bf16[24,25,64,128]{3,2,0,1:T(8,128)(2,1)}, ...), condition=%wide.region_1.2_spmd.clone, body=%wide.region_0.1_spmd.clone.sunk | while | flops 204668960 | bytes 14550299 | solution.py:43
  155.4 5.4 %select_add_fusion.4 = f32[24,128,512]{2,1,0:T(8,128)} fusion(f32[24,128,512]{2,1,0:T(8,128)} %get-tuple-element.525, pred[]{:T(512)S(6)} %compare.17, bf16[48,64,512]{2,1,0:T(8,128)(2,1)} %get-tuple-element.535, s32[]{:T(128)} %get-tuple-element.524, bf16[24,25,64,128]{3,2,0,1:T(8,128)(2,1)} %get-tuple-element.533, bf16[24]{0:T(256)(128)(2,1)S(1)} %fusion.42), kind=kOutput, calls=%fused_computation.8.clone.1 | convolution fusion | flops 204668928 | bytes 14550065 | tf_op jit(solution)/shard_map/while/body/eval_jaxpr/bnm,bnc->bmc/dot_general | solution.py:38
  160.8 7.3 %select_add_fusion.4 = f32[24,128,512]{2,1,0:T(8,128)} fusion(f32[24,128,512]{2,1,0:T(8,128)} %get-tuple-element.525, pred[]{:T(512)S(6)} %compare.17, bf16[48,64,512]{2,1,0:T(8,128)(2,1)} %get-tuple-element.535, s32[]{:T(128)} %get-tuple-element.524, bf16[24,25,64,128]{3,2,0,1:T(8,128)(2,1)} %get-tuple-element.533, bf16[24]{0:T(256)(128)(2,1)S(1)} %fusion.42), kind=kOutput, calls=%fused_computation.8.clone.1 | convolution fusion | flops 204668928 | bytes 14550065 | tf_op jit(solution)/shard_map/while/body/eval_jaxpr/bnm,bnc->bmc/dot_general | solution.py:38
  168.1 7.3 %select_add_fusion.4 = f32[24,128,512]{2,1,0:T(8,128)} fusion(f32[24,128,512]{2,1,0:T(8,128)} %get-tuple-element.525, pred[]{:T(512)S(6)} %compare.17, bf16[48,64,512]{2,1,0:T(8,128)(2,1)} %get-tuple-element.535, s32[]{:T(128)} %get-tuple-element.524, bf16[24,25,64,128]{3,2,0,1:T(8,128)(2,1)} %get-tuple-element.533, bf16[24]{0:T(256)(128)(2,1)S(1)} %fusion.42), kind=kOutput, calls=%fused_computation.8.clone.1 | convolution fusion | flops 204668928 | bytes 14550065 | tf_op jit(solution)/shard_map/while/body/eval_jaxpr/bnm,bnc->bmc/dot_general | solution.py:38
  175.4 7.3 %select_add_fusion.4 = f32[24,128,512]{2,1,0:T(8,128)} fusion(f32[24,128,512]{2,1,0:T(8,128)} %get-tuple-element.525, pred[]{:T(512)S(6)} %compare.17, bf16[48,64,512]{2,1,0:T(8,128)(2,1)} %get-tuple-element.535, s32[]{:T(128)} %get-tuple-element.524, bf16[24,25,64,128]{3,2,0,1:T(8,128)(2,1)} %get-tuple-element.533, bf16[24]{0:T(256)(128)(2,1)S(1)} %fusion.42), kind=kOutput, calls=%fused_computation.8.clone.1 | convolution fusion | flops 204668928 | bytes 14550065 | tf_op jit(solution)/shard_map/while/body/eval_jaxpr/bnm,bnc->bmc/dot_general | solution.py:38
  182.7 7.3 %select_add_fusion.4 = f32[24,128,512]{2,1,0:T(8,128)} fusion(f32[24,128,512]{2,1,0:T(8,128)} %get-tuple-element.525, pred[]{:T(512)S(6)} %compare.17, bf16[48,64,512]{2,1,0:T(8,128)(2,1)} %get-tuple-element.535, s32[]{:T(128)} %get-tuple-element.524, bf16[24,25,64,128]{3,2,0,1:T(8,128)(2,1)} %get-tuple-element.533, bf16[24]{0:T(256)(128)(2,1)S(1)} %fusion.42), kind=kOutput, calls=%fused_computation.8.clone.1 | convolution fusion | flops 204668928 | bytes 14550065 | tf_op jit(solution)/shard_map/while/body/eval_jaxpr/bnm,bnc->bmc/dot_general | solution.py:38
  190.0 7.3 %select_add_fusion.4 = f32[24,128,512]{2,1,0:T(8,128)} fusion(f32[24,128,512]{2,1,0:T(8,128)} %get-tuple-element.525, pred[]{:T(512)S(6)} %compare.17, bf16[48,64,512]{2,1,0:T(8,128)(2,1)} %get-tuple-element.535, s32[]{:T(128)} %get-tuple-element.524, bf16[24,25,64,128]{3,2,0,1:T(8,128)(2,1)} %get-tuple-element.533, bf16[24]{0:T(256)(128)(2,1)S(1)} %fusion.42), kind=kOutput, calls=%fused_computation.8.clone.1 | convolution fusion | flops 204668928 | bytes 14550065 | tf_op jit(solution)/shard_map/while/body/eval_jaxpr/bnm,bnc->bmc/dot_general | solution.py:38
  197.3 7.3 %select_add_fusion.4 = f32[24,128,512]{2,1,0:T(8,128)} fusion(f32[24,128,512]{2,1,0:T(8,128)} %get-tuple-element.525, pred[]{:T(512)S(6)} %compare.17, bf16[48,64,512]{2,1,0:T(8,128)(2,1)} %get-tuple-element.535, s32[]{:T(128)} %get-tuple-element.524, bf16[24,25,64,128]{3,2,0,1:T(8,128)(2,1)} %get-tuple-element.533, bf16[24]{0:T(256)(128)(2,1)S(1)} %fusion.42), kind=kOutput, calls=%fused_computation.8.clone.1 | convolution fusion | flops 204668928 | bytes 14550065 | tf_op jit(solution)/shard_map/while/body/eval_jaxpr/bnm,bnc->bmc/dot_general | solution.py:38
  204.6 7.3 %select_add_fusion.4 = f32[24,128,512]{2,1,0:T(8,128)} fusion(f32[24,128,512]{2,1,0:T(8,128)} %get-tuple-element.525, pred[]{:T(512)S(6)} %compare.17, bf16[48,64,512]{2,1,0:T(8,128)(2,1)} %get-tuple-element.535, s32[]{:T(128)} %get-tuple-element.524, bf16[24,25,64,128]{3,2,0,1:T(8,128)(2,1)} %get-tuple-element.533, bf16[24]{0:T(256)(128)(2,1)S(1)} %fusion.42), kind=kOutput, calls=%fused_computation.8.clone.1 | convolution fusion | flops 204668928 | bytes 14550065 | tf_op jit(solution)/shard_map/while/body/eval_jaxpr/bnm,bnc->bmc/dot_general | solution.py:38
  211.8 7.3 %select_add_fusion.4 = f32[24,128,512]{2,1,0:T(8,128)} fusion(f32[24,128,512]{2,1,0:T(8,128)} %get-tuple-element.525, pred[]{:T(512)S(6)} %compare.17, bf16[48,64,512]{2,1,0:T(8,128)(2,1)} %get-tuple-element.535, s32[]{:T(128)} %get-tuple-element.524, bf16[24,25,64,128]{3,2,0,1:T(8,128)(2,1)} %get-tuple-element.533, bf16[24]{0:T(256)(128)(2,1)S(1)} %fusion.42), kind=kOutput, calls=%fused_computation.8.clone.1 | convolution fusion | flops 204668928 | bytes 14550065 | tf_op jit(solution)/shard_map/while/body/eval_jaxpr/bnm,bnc->bmc/dot_general | solution.py:38
  219.1 7.3 %select_add_fusion.4 = f32[24,128,512]{2,1,0:T(8,128)} fusion(f32[24,128,512]{2,1,0:T(8,128)} %get-tuple-element.525, pred[]{:T(512)S(6)} %compare.17, bf16[48,64,512]{2,1,0:T(8,128)(2,1)} %get-tuple-element.535, s32[]{:T(128)} %get-tuple-element.524, bf16[24,25,64,128]{3,2,0,1:T(8,128)(2,1)} %get-tuple-element.533, bf16[24]{0:T(256)(128)(2,1)S(1)} %fusion.42), kind=kOutput, calls=%fused_computation.8.clone.1 | convolution fusion | flops 204668928 | bytes 14550065 | tf_op jit(solution)/shard_map/while/body/eval_jaxpr/bnm,bnc->bmc/dot_general | solution.py:38
  226.4 7.3 %select_add_fusion.4 = f32[24,128,512]{2,1,0:T(8,128)} fusion(f32[24,128,512]{2,1,0:T(8,128)} %get-tuple-element.525, pred[]{:T(512)S(6)} %compare.17, bf16[48,64,512]{2,1,0:T(8,128)(2,1)} %get-tuple-element.535, s32[]{:T(128)} %get-tuple-element.524, bf16[24,25,64,128]{3,2,0,1:T(8,128)(2,1)} %get-tuple-element.533, bf16[24]{0:T(256)(128)(2,1)S(1)} %fusion.42), kind=kOutput, calls=%fused_computation.8.clone.1 | convolution fusion | flops 204668928 | bytes 14550065 | tf_op jit(solution)/shard_map/while/body/eval_jaxpr/bnm,bnc->bmc/dot_general | solution.py:38
  233.7 7.3 %select_add_fusion.4 = f32[24,128,512]{2,1,0:T(8,128)} fusion(f32[24,128,512]{2,1,0:T(8,128)} %get-tuple-element.525, pred[]{:T(512)S(6)} %compare.17, bf16[48,64,512]{2,1,0:T(8,128)(2,1)} %get-tuple-element.535, s32[]{:T(128)} %get-tuple-element.524, bf16[24,25,64,128]{3,2,0,1:T(8,128)(2,1)} %get-tuple-element.533, bf16[24]{0:T(256)(128)(2,1)S(1)} %fusion.42), kind=kOutput, calls=%fused_computation.8.clone.1 | convolution fusion | flops 204668928 | bytes 14550065 | tf_op jit(solution)/shard_map/while/body/eval_jaxpr/bnm,bnc->bmc/dot_general | solution.py:38
  241.0 7.3 %select_add_fusion.4 = f32[24,128,512]{2,1,0:T(8,128)} fusion(f32[24,128,512]{2,1,0:T(8,128)} %get-tuple-element.525, pred[]{:T(512)S(6)} %compare.17, bf16[48,64,512]{2,1,0:T(8,128)(2,1)} %get-tuple-element.535, s32[]{:T(128)} %get-tuple-element.524, bf16[24,25,64,128]{3,2,0,1:T(8,128)(2,1)} %get-tuple-element.533, bf16[24]{0:T(256)(128)(2,1)S(1)} %fusion.42), kind=kOutput, calls=%fused_computation.8.clone.1 | convolution fusion | flops 204668928 | bytes 14550065 | tf_op jit(solution)/shard_map/while/body/eval_jaxpr/bnm,bnc->bmc/dot_general | solution.py:38
  248.3 7.3 %select_add_fusion.4 = f32[24,128,512]{2,1,0:T(8,128)} fusion(f32[24,128,512]{2,1,0:T(8,128)} %get-tuple-element.525, pred[]{:T(512)S(6)} %compare.17, bf16[48,64,512]{2,1,0:T(8,128)(2,1)} %get-tuple-element.535, s32[]{:T(128)} %get-tuple-element.524, bf16[24,25,64,128]{3,2,0,1:T(8,128)(2,1)} %get-tuple-element.533, bf16[24]{0:T(256)(128)(2,1)S(1)} %fusion.42), kind=kOutput, calls=%fused_computation.8.clone.1 | convolution fusion | flops 204668928 | bytes 14550065 | tf_op jit(solution)/shard_map/while/body/eval_jaxpr/bnm,bnc->bmc/dot_general | solution.py:38
  255.5 7.3 %select_add_fusion.4 = f32[24,128,512]{2,1,0:T(8,128)} fusion(f32[24,128,512]{2,1,0:T(8,128)} %get-tuple-element.525, pred[]{:T(512)S(6)} %compare.17, bf16[48,64,512]{2,1,0:T(8,128)(2,1)} %get-tuple-element.535, s32[]{:T(128)} %get-tuple-element.524, bf16[24,25,64,128]{3,2,0,1:T(8,128)(2,1)} %get-tuple-element.533, bf16[24]{0:T(256)(128)(2,1)S(1)} %fusion.42), kind=kOutput, calls=%fused_computation.8.clone.1 | convolution fusion | flops 204668928 | bytes 14550065 | tf_op jit(solution)/shard_map/while/body/eval_jaxpr/bnm,bnc->bmc/dot_general | solution.py:38
  262.8 7.3 %select_add_fusion.4 = f32[24,128,512]{2,1,0:T(8,128)} fusion(f32[24,128,512]{2,1,0:T(8,128)} %get-tuple-element.525, pred[]{:T(512)S(6)} %compare.17, bf16[48,64,512]{2,1,0:T(8,128)(2,1)} %get-tuple-element.535, s32[]{:T(128)} %get-tuple-element.524, bf16[24,25,64,128]{3,2,0,1:T(8,128)(2,1)} %get-tuple-element.533, bf16[24]{0:T(256)(128)(2,1)S(1)} %fusion.42), kind=kOutput, calls=%fused_computation.8.clone.1 | convolution fusion | flops 204668928 | bytes 14550065 | tf_op jit(solution)/shard_map/while/body/eval_jaxpr/bnm,bnc->bmc/dot_general | solution.py:38
  270.1 7.3 %select_add_fusion.4 = f32[24,128,512]{2,1,0:T(8,128)} fusion(f32[24,128,512]{2,1,0:T(8,128)} %get-tuple-element.525, pred[]{:T(512)S(6)} %compare.17, bf16[48,64,512]{2,1,0:T(8,128)(2,1)} %get-tuple-element.535, s32[]{:T(128)} %get-tuple-element.524, bf16[24,25,64,128]{3,2,0,1:T(8,128)(2,1)} %get-tuple-element.533, bf16[24]{0:T(256)(128)(2,1)S(1)} %fusion.42), kind=kOutput, calls=%fused_computation.8.clone.1 | convolution fusion | flops 204668928 | bytes 14550065 | tf_op jit(solution)/shard_map/while/body/eval_jaxpr/bnm,bnc->bmc/dot_general | solution.py:38
  277.4 7.3 %select_add_fusion.4 = f32[24,128,512]{2,1,0:T(8,128)} fusion(f32[24,128,512]{2,1,0:T(8,128)} %get-tuple-element.525, pred[]{:T(512)S(6)} %compare.17, bf16[48,64,512]{2,1,0:T(8,128)(2,1)} %get-tuple-element.535, s32[]{:T(128)} %get-tuple-element.524, bf16[24,25,64,128]{3,2,0,1:T(8,128)(2,1)} %get-tuple-element.533, bf16[24]{0:T(256)(128)(2,1)S(1)} %fusion.42), kind=kOutput, calls=%fused_computation.8.clone.1 | convolution fusion | flops 204668928 | bytes 14550065 | tf_op jit(solution)/shard_map/while/body/eval_jaxpr/bnm,bnc->bmc/dot_general | solution.py:38
  284.7 7.3 %select_add_fusion.4 = f32[24,128,512]{2,1,0:T(8,128)} fusion(f32[24,128,512]{2,1,0:T(8,128)} %get-tuple-element.525, pred[]{:T(512)S(6)} %compare.17, bf16[48,64,512]{2,1,0:T(8,128)(2,1)} %get-tuple-element.535, s32[]{:T(128)} %get-tuple-element.524, bf16[24,25,64,128]{3,2,0,1:T(8,128)(2,1)} %get-tuple-element.533, bf16[24]{0:T(256)(128)(2,1)S(1)} %fusion.42), kind=kOutput, calls=%fused_computation.8.clone.1 | convolution fusion | flops 204668928 | bytes 14550065 | tf_op jit(solution)/shard_map/while/body/eval_jaxpr/bnm,bnc->bmc/dot_general | solution.py:38
  292.0 7.3 %select_add_fusion.4 = f32[24,128,512]{2,1,0:T(8,128)} fusion(f32[24,128,512]{2,1,0:T(8,128)} %get-tuple-element.525, pred[]{:T(512)S(6)} %compare.17, bf16[48,64,512]{2,1,0:T(8,128)(2,1)} %get-tuple-element.535, s32[]{:T(128)} %get-tuple-element.524, bf16[24,25,64,128]{3,2,0,1:T(8,128)(2,1)} %get-tuple-element.533, bf16[24]{0:T(256)(128)(2,1)S(1)} %fusion.42), kind=kOutput, calls=%fused_computation.8.clone.1 | convolution fusion | flops 204668928 | bytes 14550065 | tf_op jit(solution)/shard_map/while/body/eval_jaxpr/bnm,bnc->bmc/dot_general | solution.py:38
  299.2 7.3 %select_add_fusion.4 = f32[24,128,512]{2,1,0:T(8,128)} fusion(f32[24,128,512]{2,1,0:T(8,128)} %get-tuple-element.525, pred[]{:T(512)S(6)} %compare.17, bf16[48,64,512]{2,1,0:T(8,128)(2,1)} %get-tuple-element.535, s32[]{:T(128)} %get-tuple-element.524, bf16[24,25,64,128]{3,2,0,1:T(8,128)(2,1)} %get-tuple-element.533, bf16[24]{0:T(256)(128)(2,1)S(1)} %fusion.42), kind=kOutput, calls=%fused_computation.8.clone.1 | convolution fusion | flops 204668928 | bytes 14550065 | tf_op jit(solution)/shard_map/while/body/eval_jaxpr/bnm,bnc->bmc/dot_general | solution.py:38
  306.5 7.3 %select_add_fusion.4 = f32[24,128,512]{2,1,0:T(8,128)} fusion(f32[24,128,512]{2,1,0:T(8,128)} %get-tuple-element.525, pred[]{:T(512)S(6)} %compare.17, bf16[48,64,512]{2,1,0:T(8,128)(2,1)} %get-tuple-element.535, s32[]{:T(128)} %get-tuple-element.524, bf16[24,25,64,128]{3,2,0,1:T(8,128)(2,1)} %get-tuple-element.533, bf16[24]{0:T(256)(128)(2,1)S(1)} %fusion.42), kind=kOutput, calls=%fused_computation.8.clone.1 | convolution fusion | flops 204668928 | bytes 14550065 | tf_op jit(solution)/shard_map/while/body/eval_jaxpr/bnm,bnc->bmc/dot_general | solution.py:38
  313.8 7.3 %select_add_fusion.4 = f32[24,128,512]{2,1,0:T(8,128)} fusion(f32[24,128,512]{2,1,0:T(8,128)} %get-tuple-element.525, pred[]{:T(512)S(6)} %compare.17, bf16[48,64,512]{2,1,0:T(8,128)(2,1)} %get-tuple-element.535, s32[]{:T(128)} %get-tuple-element.524, bf16[24,25,64,128]{3,2,0,1:T(8,128)(2,1)} %get-tuple-element.533, bf16[24]{0:T(256)(128)(2,1)S(1)} %fusion.42), kind=kOutput, calls=%fused_computation.8.clone.1 | convolution fusion | flops 204668928 | bytes 14550065 | tf_op jit(solution)/shard_map/while/body/eval_jaxpr/bnm,bnc->bmc/dot_general | solution.py:38
  321.1 7.3 %select_add_fusion.4 = f32[24,128,512]{2,1,0:T(8,128)} fusion(f32[24,128,512]{2,1,0:T(8,128)} %get-tuple-element.525, pred[]{:T(512)S(6)} %compare.17, bf16[48,64,512]{2,1,0:T(8,128)(2,1)} %get-tuple-element.535, s32[]{:T(128)} %get-tuple-element.524, bf16[24,25,64,128]{3,2,0,1:T(8,128)(2,1)} %get-tuple-element.533, bf16[24]{0:T(256)(128)(2,1)S(1)} %fusion.42), kind=kOutput, calls=%fused_computation.8.clone.1 | convolution fusion | flops 204668928 | bytes 14550065 | tf_op jit(solution)/shard_map/while/body/eval_jaxpr/bnm,bnc->bmc/dot_general | solution.py:38
  328.4 7.3 %select_add_fusion.4 = f32[24,128,512]{2,1,0:T(8,128)} fusion(f32[24,128,512]{2,1,0:T(8,128)} %get-tuple-element.525, pred[]{:T(512)S(6)} %compare.17, bf16[48,64,512]{2,1,0:T(8,128)(2,1)} %get-tuple-element.535, s32[]{:T(128)} %get-tuple-element.524, bf16[24,25,64,128]{3,2,0,1:T(8,128)(2,1)} %get-tuple-element.533, bf16[24]{0:T(256)(128)(2,1)S(1)} %fusion.42), kind=kOutput, calls=%fused_computation.8.clone.1 | convolution fusion | flops 204668928 | bytes 14550065 | tf_op jit(solution)/shard_map/while/body/eval_jaxpr/bnm,bnc->bmc/dot_general | solution.py:38
  335.7 69.7 %while.45 = (s32[]{:T(128)}, f32[24,128]{1,0:T(8,128)S(1)}, s32[24,25]{0,1:T(8,128)S(1)}, bf16[48,64,512]{2,1,0:T(8,128)(2,1)}, bf16[24,128,512]{2,1,0:T(8,128)(...) while((s32[]{:T(128)}, f32[24,128]{1,0:T(8,128)S(1)}, ...), condition=%wide.region_7.8_spmd.clone, body=%wide.region_5.7_spmd.clone.sunk | while | flops 201922608 | bytes 5162371 | solution.py:79
  406.2 24.9 %psum.7 = f32[24,64]{1,0:T(8,128)} all-reduce(f32[24,64]{1,0:T(8,128)S(1)} %bitcast.42), channel_id=1, replica_groups=mesh['rows'=4,'cols'=4,'layers'=2] {'cols','layers'}, use_global_device_ids=true, to_apply=%region_8.9 | all-reduce | flops 1536 | bytes 12288 | tf_op jit(solution)/shard_map/psum | solution.py:104
  (186 shorter events, 212.5 us)
Async XLA Ops:
  7.2 7.8 %copy-start.4 = (s32[24,25]{1,0:T(8,128)S(1)}, s32[24,25]{1,0:T(8,128)}, u32[]{:S(2)}) copy-start(s32[24,25]{1,0:T(8,128)} %param.21) | copy-start | bytes 7204
  7.2 434.5 %reduce-scatter.2.cloned.1.call-start = ((), (), s32[]{:S(2)}) async-start(), calls=%async_computation.1 | async-start | bytes 9437184 | tf_op jit(solution)/shard_map/reduce_scatter | solution.py:86
  9.9 140.0 %collective-permute-start = (bf16[12,64,512]{2,1,0:T(8,128)(2,1)}, bf16[12,64,512]{2,1,0:T(8,128)(2,1)}, u32[]{:S(2)}, u32[]{:S(2)}) collective-permute-start(bf16[12,64,512]{2,1,0:T(8,128)(2,1)} %get-tuple-element.417), channel_id=1, source_target_pairs={{0,8},{8,16},{16,24},{24,0},{1,9},{9,17},{17,25},{25,1},{2,10},{10... | collective-permute-start | bytes 2359304 | tf_op jit(solution)/shard_map/ppermute | solution.py:16
  12.9 139.6 %collective-permute-start.1 = (bf16[12,64,512]{2,1,0:T(8,128)(2,1)}, bf16[12,64,512]{2,1,0:T(8,128)(2,1)}, u32[]{:S(2)}, u32[]{:S(2)}) collective-permute-start(bf16[12,64,512]{2,1,0:T(8,128)(2,1)} %get-tuple-element.416), channel_id=1, source_target_pairs={{8,0},{16,8},{24,16},{0,24},{9,1},{17,9},{25,17},{1,25},{10,2},{18... | collective-permute-start | bytes 2359304 | tf_op jit(solution)/shard_map/ppermute | solution.py:18
  26.2 3.5 copy-start
  139.9 8.0 %copy-start.1 = (f32[48,64,512]{2,1,0:T(8,128)S(1)}, f32[48,64,512]{2,1,0:T(8,128)}, u32[]{:S(2)}) copy-start(f32[48,64,512]{2,1,0:T(8,128)} %get-tuple-element.325) | copy-start | bytes 18874372
  144.0 287.1 %collective-permute-start.2 = (f32[12,64,512]{2,1,0:T(8,128)}, f32[12,64,512]{2,1,0:T(8,128)}, u32[]{:S(2)}, u32[]{:S(2)}) collective-permute-start(f32[12,64,512]{2,1,0:T(8,128)} %get-tuple-element.415), channel_id=1, source_target_pairs={{0,8},{8,16},{16,24},{24,0},{1,9},{9,17},{17,25},{25,1},{2,10},{10... | collective-permute-start | bytes 4718600 | tf_op jit(solution)/shard_map/ppermute | solution.py:28
  144.0 290.5 %collective-permute-start.3 = (f32[12,64,512]{2,1,0:T(8,128)}, f32[12,64,512]{2,1,0:T(8,128)}, u32[]{:S(2)}, u32[]{:S(2)}) collective-permute-start(f32[12,64,512]{2,1,0:T(8,128)} %get-tuple-element.414), channel_id=1, source_target_pairs={{0,24},{8,0},{16,8},{24,16},{1,25},{9,1},{17,9},{25,17},{2,26},{10... | collective-permute-start | bytes 4718600 | tf_op jit(solution)/shard_map/ppermute | solution.py:28
  153.8 1.6 copy-start.2
  335.7 69.7 %copy-start.5 = (s32[24,128]{1,0:T(8,128)S(1)}, s32[24,128]{1,0:T(8,128)}, u32[]{:S(2)}) copy-start(s32[24,128]{1,0:T(8,128)} %param.23) | copy-start | bytes 36868
  438.0 3.6 copy-start.3
Sparse Core Ops, SparseCore 0:
  335.8 75.4 reduce-scatter.1
where the time goes:
time: 454 us; the launch traced here: 452 us
  matrix products  358 us (79%)
  local copies, waits for them, and re-layouts  29.1 us (6%)
  blocking collectives  24.9 us (5%)
  other arithmetic  16.7 us (4%)
  between operations  14.1 us (3%)
  starting transfers between devices  8.91 us (2%)
    dot_general x25, matrix products, apply_advance(): jnp.einsum('bnm,bnc->bmc', masked, window, preferred_element_type=jnp.flo...  180 us
    dot_general x25, matrix products, push_advance(): jnp.einsum('bnm,bmc->bnc', masked, cotangent, preferred_element_type=jnp....  110 us
    dot_general x25, matrix products, force_advance(): jnp.einsum('bnc,bmc->bnm', window, cotangent, preferred_element_type=jnp....  67 us
    psum x1, blocking collectives, local(): forces = lax.psum(partial_force, ('cols', 'layers'))  24.9 us
    unnamed x16, local copies, waits for them, and re-layouts  15.6 us
  transfers between devices with their start and end apart: 5, of which 0 were waited for; matrix products, arithmetic and copies ran while one was open for 87% of the time, Pallas kernels for 0%

commit v1 on v0

v1 whole, which is shorter than its diff:
```python
import functools

import jax
import jax.numpy as jnp
from jax import lax
from jax.experimental import pallas as pl
from jax.experimental.pallas import tpu as pltpu
from jax.sharding import PartitionSpec as P

APB = 64
VMEM_BYTES = 56 * 1024 * 1024
ARBITRARY = pltpu.GridDimensionSemantics.ARBITRARY


def shifted(value, axis, steps):
    count = lax.axis_size(axis)
    pairs = [(source, (source + steps) % count) for source in range(count)]
    return lax.ppermute(value, axis, pairs)


def swapped(value, axis, bit):
    count = lax.axis_size(axis)
    return lax.ppermute(value, axis, [(source, source ^ bit) for source in range(count)])


def keep_blocks(mask_ref, row, blocks, slots, share):
    parts = []
    for slot in range(slots):
        kept = mask_ref[row, slot] != 0
        block = blocks[slot * share : (slot + 1) * share]
        parts.append(jnp.where(kept, block, jnp.zeros_like(block)))
    return parts


def push_kernel(group, slots, share, mask_ref, ham_ref, cot_ref, low_ref, own_ref, high_ref, left, total):
    step = pl.program_id(0)
    orbitals = ham_ref.shape[2]
    columns = cot_ref.shape[2]
    spread = (slots + group - 1) * share

    @pl.when(step == 0)
    def _():
        total[...] = jnp.zeros_like(total)
        left[...] = jnp.zeros_like(left)

    for k in range(group):
        parts = keep_blocks(mask_ref, step * group + k, ham_ref[k], slots, share)
        for slot in range(slots):
            at = (slot + k) * share
            left[at : at + share, k * orbitals : (k + 1) * orbitals] = parts[slot]
    right = cot_ref[...].reshape(group * orbitals, columns)
    first = pl.multiple_of(step * (group * share), group * share)
    piece = 2 * share
    for at in range(0, spread, piece):
        size = min(piece, spread - at)
        total[pl.ds(first + at, size), :] += jnp.dot(
            left[at : at + size, :], right, preferred_element_type=jnp.float32
        )

    @pl.when(step == pl.num_programs(0) - 1)
    def _():
        halo = low_ref.shape[0]
        own = own_ref.shape[0]
        low_ref[...] = (2.0 * total[:halo, :]).astype(low_ref.dtype)
        own_ref[...] = 2.0 * total[halo : halo + own, :]
        high_ref[...] = (2.0 * total[halo + own :, :]).astype(high_ref.dtype)


def push(ham, mask, cotangent, share):
    rows, depth, orbitals = ham.shape
    columns = cotangent.shape[2]
    slots = depth // share
    reach = (slots - 1) // 2
    group = 2 if rows % 2 == 0 else 1
    kernel = functools.partial(push_kernel, group, slots, share)
    flops = 2 * rows * depth * orbitals * columns
    return pl.pallas_call(
        kernel,
        out_shape=(
            jax.ShapeDtypeStruct((reach * share, columns), jnp.bfloat16),
            jax.ShapeDtypeStruct((rows * share, columns), jnp.float32),
            jax.ShapeDtypeStruct((reach * share, columns), jnp.bfloat16),
        ),
        grid_spec=pltpu.PrefetchScalarGridSpec(
            num_scalar_prefetch=1,
            grid=(rows // group,),
            in_specs=[
                pl.BlockSpec((group, depth, orbitals), lambda i, m: (i, 0, 0)),
                pl.BlockSpec((group, orbitals, columns), lambda i, m: (i, 0, 0)),
            ],
            out_specs=[
                pl.BlockSpec((reach * share, columns), lambda i, m: (0, 0)),
                pl.BlockSpec((rows * share, columns), lambda i, m: (0, 0)),
                pl.BlockSpec((reach * share, columns), lambda i, m: (0, 0)),
            ],
            scratch_shapes=[
                pltpu.VMEM(((slots + group - 1) * share, group * orbitals), jnp.bfloat16),
                pltpu.VMEM(((rows + 2 * reach) * share, columns), jnp.float32),
            ],
        ),
        compiler_params=pltpu.CompilerParams(
            dimension_semantics=(ARBITRARY,), vmem_limit_bytes=VMEM_BYTES
        ),
        cost_estimate=pl.CostEstimate(flops=flops, bytes_accessed=ham.size * 2, transcendentals=0),
        name="push_blocks",
    )(mask, ham, cotangent)


def pull_kernel(
    first_row, slots, share, mask_ref, side_ref, ham_ref, slope_ref, cot_ref, prev_ref, head_ref, tail_ref,
    keep_ref, send_ref, force_ref, window, both, product,
):
    step = pl.program_id(0)
    orbitals = ham_ref.shape[1]
    side = side_ref[0]

    @pl.when(step == 0)
    def _():
        split = head_ref.shape[0]
        window[:split, :] = head_ref[...]
        window[split:, :] = tail_ref[...]

    row = first_row + step
    for slot in range(slots):
        kept = mask_ref[row, slot] != 0
        span = slice(slot * share, (slot + 1) * share)
        block = ham_ref[span, :]
        both[span, :orbitals] = jnp.where(kept, block, jnp.zeros_like(block))
        block = slope_ref[span, :]
        both[span, orbitals:] = jnp.where(kept, block, jnp.zeros_like(block))
    near = window[pl.ds(pl.multiple_of(step * share, share), slots * share), :]
    product[...] = lax.dot_general(
        both[...], near, (((0,), (0,)), ((), ())), preferred_element_type=jnp.float32
    )
    mine = pl.multiple_of(side * share, share)
    other = pl.multiple_of((1 - side) * share, share)
    keep_ref[...] = 2.0 * product[pl.ds(mine, share), :] - prev_ref[...].astype(jnp.float32)
    send_ref[...] = (2.0 * product[pl.ds(other, share), :]).astype(send_ref.dtype)
    work = product[orbitals:, :] * cot_ref[...].astype(jnp.float32)
    lanes = 128
    folded = work[:, :lanes]
    for at in range(lanes, work.shape[1], lanes):
        folded = folded + work[:, at : at + lanes]
    force_ref[...] = 2.0 * jnp.sum(folded.T, axis=0, keepdims=True)


def pull(ham, slope, mask, side, cotangent, previous, head, tail, share, first_row, rows):
    _, depth, orbitals = ham.shape
    columns = cotangent.shape[2]
    slots = depth // share
    kernel = functools.partial(pull_kernel, first_row, slots, share)
    flops = 4 * rows * depth * orbitals * columns
    row_block = lambda *dims: pl.BlockSpec((None,) + dims, lambda i, m, s: (i + first_row, 0, 0))
    whole = lambda a: pl.BlockSpec(a.shape, lambda i, m, s: (0, 0))
    out_block = lambda *dims: pl.BlockSpec((None,) + dims, lambda i, m, s: (i, 0, 0))
    return pl.pallas_call(
        kernel,
        out_shape=(
            jax.ShapeDtypeStruct((rows, share, columns), jnp.float32),
            jax.ShapeDtypeStruct((rows, share, columns), jnp.bfloat16),
            jax.ShapeDtypeStruct((rows, 1, orbitals), jnp.float32),
        ),
        grid_spec=pltpu.PrefetchScalarGridSpec(
            num_scalar_prefetch=2,
            grid=(rows,),
            in_specs=[
                row_block(depth, orbitals),
                row_block(depth, orbitals),
                row_block(orbitals, columns),
                row_block(share, columns),
                whole(head),
                whole(tail),
            ],
            out_specs=[
                out_block(share, columns),
                out_block(share, columns),
                out_block(1, orbitals),
            ],
            scratch_shapes=[
                pltpu.VMEM((head.shape[0] + tail.shape[0], columns), jnp.bfloat16),
                pltpu.VMEM((depth, 2 * orbitals), jnp.bfloat16),
                pltpu.VMEM((2 * orbitals, columns), jnp.float32),
            ],
        ),
        compiler_params=pltpu.CompilerParams(
            dimension_semantics=(ARBITRARY,), vmem_limit_bytes=VMEM_BYTES
        ),
        cost_estimate=pl.CostEstimate(
            flops=flops, bytes_accessed=4 * rows * depth * orbitals, transcendentals=0
        ),
        name="pull_blocks",
    )(mask, side, ham, slope, cotangent, previous, head, tail)


def local(term_now, term_prev, cotangent, ham_blocks, block_mask, ham_slope, atom_owner):
    rows, slots, share, orbitals = ham_blocks.shape
    columns = term_now.shape[2]
    reach = (slots - 1) // 2
    edge = reach * share
    half = rows // 2
    ham = ham_blocks.reshape(rows, slots * share, orbitals)
    slope = ham_slope.reshape(rows, slots * share, orbitals)
    term = term_now.reshape(rows * share, columns)
    side = lax.axis_index("layers").astype(jnp.int32).reshape(1)

    below = shifted(term[rows * share - edge :], "rows", 1)
    above = shifted(term[:edge], "rows", -1)

    to_below, own, to_above = push(ham, block_mask, cotangent, share)
    from_above = shifted(to_below, "rows", -1)
    from_below = shifted(to_above, "rows", 1)

    args = (ham, slope, block_mask, side, cotangent, term_prev)
    keep_a, send_a, force_a = pull(*args, below, term, share, 0, half)
    got_a = swapped(send_a, "layers", 1)
    keep_b, send_b, force_b = pull(*args, term, above, share, half, rows - half)
    got_b = swapped(send_b, "layers", 1)

    row_force = jnp.concatenate([force_a, force_b], axis=0).reshape(rows, orbitals)
    atom_ids = lax.broadcasted_iota(jnp.int32, (1, 1, APB), 2)
    owned = jnp.where(atom_owner[:, :, None] == atom_ids, row_force[:, :, None], 0.0)
    forces = jnp.sum(owned, axis=1)
    forces = forces + swapped(forces, "layers", 1)
    bit = 1
    while bit < lax.axis_size("cols"):
        forces = forces + swapped(forces, "cols", bit)
        bit *= 2

    term_next = jnp.concatenate(
        [keep_a + got_a.astype(jnp.float32), keep_b + got_b.astype(jnp.float32)], axis=0
    ).astype(jnp.bfloat16)
    own = own.reshape(rows, share, columns)
    got = jnp.concatenate([from_below, from_above], axis=0).reshape(rows, share, columns)
    grad_term = (own + got.astype(jnp.float32)).astype(jnp.bfloat16)
    return (term_next, grad_term, forces)


def solution(mesh):
    return jax.shard_map(
        local,
        mesh=mesh,
        in_specs=(
            P("rows", "layers", "cols"),
            P("rows", "layers", "cols"),
            P("rows", None, "cols"),
            P("rows", None, "layers", None),
            P("rows", None),
            P("rows", None, "layers", None),
            P("rows", None),
        ),
        out_specs=(P("rows", "layers", "cols"), P("rows", "layers", "cols"), P("rows", None)),
        check_vma=False,
    )
```

time: 454 us -> 101 us (0.22)
  the two profiles are of different devices: /device:TPU:0 before, /device:TPU:26 now
where the time goes in v1:
time: 101 us; the launch traced here: 100 us
  Pallas kernels  47.6 us (47%)
  waiting for transfers between devices  34.9 us (35%)
  starting transfers between devices  7.16 us (7%)
  other arithmetic  5.21 us (5%)
  local copies, waits for them, and re-layouts  4.44 us (4%)
    pallas_call x2, Pallas kernels, pull(): pl.pallas_call(kernel, out_shape=(jax.ShapeDtypeStruct((rows, share, colu...  31.2 us
    ppermute x5, waiting for transfers between devices, swapped(): lax.ppermute(value, axis, [(source, source ^ bit) for source in range(cou...  19.9 us
    pallas_call x1, Pallas kernels, push(): pl.pallas_call(kernel, out_shape=(jax.ShapeDtypeStruct((reach * share, co...  16.4 us
    ppermute x4, waiting for transfers between devices, shifted(): return lax.ppermute(value, axis, pairs)  15 us
    ppermute x4, starting transfers between devices, shifted(): return lax.ppermute(value, axis, pairs)  4.1 us
    ppermute x5, starting transfers between devices, swapped(): lax.ppermute(value, axis, [(source, source ^ bit) for source in range(cou...  3.06 us
    slice x1, local copies, waits for them, and re-layouts, local(): below = shifted(term[rows * share - edge:], 'rows', 1)  2.66 us
  transfers between devices with their start and end apart: 9, of which 5 were waited for; matrix products, arithmetic and copies ran while one was open for 4% of the time, Pallas kernels for 48%

profile of v1, /device:TPU:26, one launch (start us, length us, event | category | flops | bytes accessed | tf_op | source)
XLA Modules:
  0.0 100.1 jit_solution(3647381690238358452)
XLA Ops:
  0.6 2.7 %fusion = (bf16[12,64,512]{2,1,0:T(8,128)(2,1)}, bf16[12,64,512]{2,1,0:T(8,128)(2,1)}) fusion(bf16[24,64,512]{2,1,0:T(8,128)(2,1)} %param.7), kind=kLoop, calls=%fused_computation.7 | loop fusion | bytes 3145728 | tf_op jit(solution)/shard_map/slice | solution.py:206
  3.3 0.2 collective-permute-start
  3.5 1.8 %collective-permute-start.2 = (bf16[768,512]{1,0:T(8,128)(2,1)}, bf16[768,512]{1,0:T(8,128)(2,1)S(1)}, u32[]{:S(2)}, u32[]{:S(2)}) collective-permute-start(bf16[768,512]{1,0:T(8,128)(2,1)} %bitcast.5), channel_id=1, source_target_pairs={{0,24},{8,0},{16,8},{24,16},{1,25},{9,1},{17,9},{25,17},{2,26},{10... | collective-permute-start | bytes 2359304 | tf_op jit(solution)/shard_map/ppermute | solution.py:18
  5.3 16.4 %push_blocks.1 = (bf16[768,512]{1,0:T(8,128)(2,1)}, f32[1536,512]{1,0:T(8,128)}, bf16[768,512]{1,0:T(8,128)(2,1)}) custom-call(s32[24,25]{1,0:T(8,128)} %mask_ref.5, bf16[24,1600,128]{2,1,0:T(8,128)(2,1)} %bitcast.8, bf16[24,128,512]{2,1,0:T(8,128)(2,1)} %cot_ref.5), custom_call_target="tpu_custom_call" | custom-call | flops 5033164800 | bytes 9830400 | tf_op jit(solution)/shard_map/push_blocks/pallas_call | solution.py:77
  21.7 2.1 %collective-permute-start.4 = (bf16[768,512]{1,0:T(8,128)(2,1)}, bf16[768,512]{1,0:T(8,128)(2,1)S(1)}, u32[]{:S(2)}, u32[]{:S(2)}) collective-permute-start(bf16[768,512]{1,0:T(8,128)(2,1)} %get-tuple-element.17), channel_id=1, source_target_pairs={{0,8},{8,16},{16,24},{24,0},{1,9},{9,17},{17,25},{25,1},{2,10},{10... | collective-permute-start | bytes 2359304 | tf_op jit(solution)/shard_map/ppermute | solution.py:18
  23.8 0.0 collective-permute-start.5
  23.8 15.0 %collective-permute-done.head_ref = bf16[768,512]{1,0:T(8,128)(2,1)S(1)} collective-permute-done((bf16[768,512]{1,0:T(8,128)(2,1)}, bf16[768,512]{1,0:T(8,128)(2,1)S(1)}, u32[]{:S(2)}, u32[]{:S(2)}) %collective-permute-start) | collective-permute-done | bytes 786464 | tf_op jit(solution)/shard_map/ppermute | solution.py:18
  38.8 0.9 copy-done.4
  39.7 15.6 %pull_blocks.2 = (f32[12,64,512]{2,1,0:T(8,128)}, bf16[12,64,512]{2,1,0:T(8,128)(2,1)}, f32[12,1,128]{2,1,0:T(1,128)}) custom-call(s32[24,25]{1,0:T(8,128)} %mask_ref.5, s32[1]{0:T(128)} %bitcast.side_ref, bf16[24,1600,128]{2,1,0:T(8,128)(2,1)} %bitcast.9, bf16[24,1600,128]{2,1,0:T(8,128)(2,1)} %bitcast.11, bf16[24,128,512]{2,1,0:T(8,128)(2,1)} %cot_ref.5, ...), custom_call_target="tpu_custom_call" | custom-call | flops 5033164800 | bytes 9830400 | tf_op jit(solution)/shard_map/pull_blocks/pallas_call | solution.py:156
  55.2 0.0 copy-start.5
  55.3 1.7 %collective-permute-start.1 = (bf16[12,64,512]{2,1,0:T(8,128)(2,1)}, bf16[12,64,512]{2,1,0:T(8,128)(2,1)S(1)}, u32[]{:S(2)}, u32[]{:S(2)}) collective-permute-start(bf16[12,64,512]{2,1,0:T(8,128)(2,1)} %get-tuple-element.13), channel_id=1, source_target_pairs={{0,1},{1,0},{2,3},{3,2},{4,5},{5,4},{6,7},{7,6},{8,9},{9,8},{10,11... | collective-permute-start | bytes 2359304 | tf_op jit(solution)/shard_map/ppermute | solution.py:23
  56.9 0.0 collective-permute-done.2.tail_ref
  56.9 0.9 copy-done.3
  57.8 15.6 %pull_blocks.3 = (f32[12,64,512]{2,1,0:T(8,128)}, bf16[12,64,512]{2,1,0:T(8,128)(2,1)}, f32[12,1,128]{2,1,0:T(1,128)}) custom-call(s32[24,25]{1,0:T(8,128)} %mask_ref.5, s32[1]{0:T(128)} %bitcast.side_ref, bf16[24,1600,128]{2,1,0:T(8,128)(2,1)} %bitcast.10, bf16[24,1600,128]{2,1,0:T(8,128)(2,1)} %bitcast.12, bf16[24,128,512]{2,1,0:T(8,128)(2,1)} %cot_ref.5, ...), custom_call_target="tpu_custom_call" | custom-call | flops 5033164800 | bytes 9830400 | tf_op jit(solution)/shard_map/pull_blocks/pallas_call | solution.py:156
  73.4 0.7 pad_maximum_fusion.1
  74.2 0.4 select_reduce_fusion
  74.5 0.5 collective-permute-start.6
  75.0 3.3 %collective-permute-done.6 = f32[24,64]{1,0:T(8,128)S(1)} collective-permute-done((f32[24,64]{1,0:T(8,128)S(1)}, f32[24,64]{1,0:T(8,128)S(1)}, u32[]{:S(2)}, u32[]{:S(2)}) %collective-permute-start.6) | collective-permute-done | bytes 6176 | tf_op jit(solution)/shard_map/ppermute | solution.py:23
  78.3 0.0 collective-permute-start.7
  78.3 0.4 collective-permute-start.3
  78.7 0.7 collective-permute-done.7
  79.5 0.5 collective-permute-start.8
  79.9 0.0 collective-permute-done.4
  79.9 0.0 collective-permute-done.5
  80.0 1.7 %add_convert_fusion = bf16[1536,512]{1,0:T(8,128)(2,1)} fusion(f32[1536,512]{1,0:T(8,128)S(1)} %copy-done, bf16[768,512]{1,0:T(8,128)(2,1)S(1)} %collective-permute-done.5, bf16[768,512]{1,0:T(8,128)(2,1)S(1)} %collective-permute-done.4), kind=kLoop, calls=%fused_computation | loop fusion | flops 4718592 | bytes 6291456 | tf_op jit(solution)/shard_map/convert_element_type | solution.py:234
  81.6 1.5 %collective-permute-done.8 = f32[24,64]{1,0:T(8,128)S(1)} collective-permute-done((f32[24,64]{1,0:T(8,128)S(1)}, f32[24,64]{1,0:T(8,128)S(1)}, u32[]{:S(2)}, u32[]{:S(2)}) %collective-permute-start.8) | collective-permute-done | bytes 6176 | tf_op jit(solution)/shard_map/ppermute | solution.py:23
  83.2 0.6 add.24
  83.8 0.0 collective-permute-done.1
  83.8 0.3 add_convert_fusion.2
  84.0 14.4 %collective-permute-done.3 = bf16[12,64,512]{2,1,0:T(8,128)(2,1)S(1)} collective-permute-done((bf16[12,64,512]{2,1,0:T(8,128)(2,1)}, bf16[12,64,512]{2,1,0:T(8,128)(2,1)S(1)}, u32[]{:S(2)}, u32[]{:S(2)}) %collective-permute-start.3) | collective-permute-done | bytes 786464 | tf_op jit(solution)/shard_map/ppermute | solution.py:23
  98.5 0.3 add_convert_fusion.1
  98.8 1.3 %pad_maximum_fusion = bf16[24,64,512]{2,1,0:T(8,128)(2,1)} fusion(bf16[12,64,512]{2,1,0:T(8,128)(2,1)S(1)} %add_convert_fusion.1, bf16[12,64,512]{2,1,0:T(8,128)(2,1)S(1)} %add_convert_fusion.2), kind=kLoop, calls=%fused_computation.1 | loop fusion | flops 786432 | bytes 3145728 | tf_op jit(solution)/shard_map/concatenate | solution.py:229
  (13 shorter events, 0.0 us)
Async XLA Ops:
  3.3 35.5 %collective-permute-start = (bf16[768,512]{1,0:T(8,128)(2,1)}, bf16[768,512]{1,0:T(8,128)(2,1)S(1)}, u32[]{:S(2)}, u32[]{:S(2)}) collective-permute-start(bf16[768,512]{1,0:T(8,128)(2,1)} %bitcast.3), channel_id=1, source_target_pairs={{0,8},{8,16},{16,24},{24,0},{1,9},{9,17},{17,25},{25,1},{2,10},{10... | collective-permute-start | bytes 2359304 | tf_op jit(solution)/shard_map/ppermute | solution.py:18
  3.5 53.4 %collective-permute-start.2 = (bf16[768,512]{1,0:T(8,128)(2,1)}, bf16[768,512]{1,0:T(8,128)(2,1)S(1)}, u32[]{:S(2)}, u32[]{:S(2)}) collective-permute-start(bf16[768,512]{1,0:T(8,128)(2,1)} %bitcast.5), channel_id=1, source_target_pairs={{0,24},{8,0},{16,8},{24,16},{1,25},{9,1},{17,9},{25,17},{2,26},{10... | collective-permute-start | bytes 2359304 | tf_op jit(solution)/shard_map/ppermute | solution.py:18
  21.7 58.2 %collective-permute-start.4 = (bf16[768,512]{1,0:T(8,128)(2,1)}, bf16[768,512]{1,0:T(8,128)(2,1)S(1)}, u32[]{:S(2)}, u32[]{:S(2)}) collective-permute-start(bf16[768,512]{1,0:T(8,128)(2,1)} %get-tuple-element.17), channel_id=1, source_target_pairs={{0,8},{8,16},{16,24},{24,0},{1,9},{9,17},{17,25},{25,1},{2,10},{10... | collective-permute-start | bytes 2359304 | tf_op jit(solution)/shard_map/ppermute | solution.py:18
  23.8 56.1 %collective-permute-start.5 = (bf16[768,512]{1,0:T(8,128)(2,1)}, bf16[768,512]{1,0:T(8,128)(2,1)S(1)}, u32[]{:S(2)}, u32[]{:S(2)}) collective-permute-start(bf16[768,512]{1,0:T(8,128)(2,1)} %get-tuple-element.18), channel_id=1, source_target_pairs={{0,24},{8,0},{16,8},{24,16},{1,25},{9,1},{17,9},{25,17},{2,26},{10... | collective-permute-start | bytes 2359304 | tf_op jit(solution)/shard_map/ppermute | solution.py:18
  38.8 0.9 copy-start.4
  55.2 18.2 %copy-start.6 = (f32[12,1,128]{2,1,0:T(1,128)S(1)}, f32[12,1,128]{2,1,0:T(1,128)}, u32[]{:S(2)}) copy-start(f32[12,1,128]{2,1,0:T(1,128)} %get-tuple-element.19) | copy-start | bytes 18436
  55.2 18.9 %copy-start.5 = (s32[24,128]{1,0:T(8,128)S(1)}, s32[24,128]{1,0:T(8,128)}, u32[]{:S(2)}) copy-start(s32[24,128]{1,0:T(8,128)} %param.13) | copy-start | bytes 36868
  55.3 28.5 %collective-permute-start.1 = (bf16[12,64,512]{2,1,0:T(8,128)(2,1)}, bf16[12,64,512]{2,1,0:T(8,128)(2,1)S(1)}, u32[]{:S(2)}, u32[]{:S(2)}) collective-permute-start(bf16[12,64,512]{2,1,0:T(8,128)(2,1)} %get-tuple-element.13), channel_id=1, source_target_pairs={{0,1},{1,0},{2,3},{3,2},{4,5},{5,4},{6,7},{7,6},{8,9},{9,8},{10,11... | collective-permute-start | bytes 2359304 | tf_op jit(solution)/shard_map/ppermute | solution.py:23
  56.9 0.9 copy-start.3
  57.8 22.2 %copy-start = (f32[1536,512]{1,0:T(8,128)S(1)}, f32[1536,512]{1,0:T(8,128)}, u32[]{:S(2)}) copy-start(f32[1536,512]{1,0:T(8,128)} %get-tuple-element.16) | copy-start | bytes 9437188
  74.5 3.8 %collective-permute-start.6 = (f32[24,64]{1,0:T(8,128)S(1)}, f32[24,64]{1,0:T(8,128)S(1)}, u32[]{:S(2)}, u32[]{:S(2)}) collective-permute-start(f32[24,64]{1,0:T(8,128)S(1)} %select_reduce_fusion), channel_id=1, source_target_pairs={{0,1},{1,0},{2,3},{3,2},{4,5},{5,4},{6,7},{7,6},{8,9},{9,8},{10,11... | collective-permute-start | bytes 18440 | tf_op jit(solution)/shard_map/ppermute | solution.py:23
  78.3 1.2 %collective-permute-start.7 = (f32[24,64]{1,0:T(8,128)S(1)}, f32[24,64]{1,0:T(8,128)S(1)}, u32[]{:S(2)}, u32[]{:S(2)}) collective-permute-start(f32[24,64]{1,0:T(8,128)S(1)} %add.22), channel_id=1, source_target_pairs={{0,2},{2,0},{4,6},{6,4},{1,3},{3,1},{5,7},{7,5},{8,10},{10,8},{12,... | collective-permute-start | bytes 18440 | tf_op jit(solution)/shard_map/ppermute | solution.py:23
  78.3 20.2 %collective-permute-start.3 = (bf16[12,64,512]{2,1,0:T(8,128)(2,1)}, bf16[12,64,512]{2,1,0:T(8,128)(2,1)S(1)}, u32[]{:S(2)}, u32[]{:S(2)}) collective-permute-start(bf16[12,64,512]{2,1,0:T(8,128)(2,1)} %get-tuple-element.15), channel_id=1, source_target_pairs={{0,1},{1,0},{2,3},{3,2},{4,5},{5,4},{6,7},{7,6},{8,9},{9,8},{10,11... | collective-permute-start | bytes 2359304 | tf_op jit(solution)/shard_map/ppermute | solution.py:23
  79.5 3.7 %collective-permute-start.8 = (f32[24,64]{1,0:T(8,128)S(1)}, f32[24,64]{1,0:T(8,128)S(1)}, u32[]{:S(2)}, u32[]{:S(2)}) collective-permute-start(f32[24,64]{1,0:T(8,128)S(1)} %add.23), channel_id=1, source_target_pairs={{0,4},{2,6},{4,0},{6,2},{1,5},{3,7},{5,1},{7,3},{8,12},{10,14},{12... | collective-permute-start | bytes 18440 | tf_op jit(solution)/shard_map/ppermute | solution.py:23
  80.0 3.8 %copy-start.1 = (f32[12,64,512]{2,1,0:T(8,128)S(1)}, f32[12,64,512]{2,1,0:T(8,128)}, u32[]{:S(2)}) copy-start(f32[12,64,512]{2,1,0:T(8,128)} %get-tuple-element.12) | copy-start | bytes 4718596
  83.8 14.7 %copy-start.2 = (f32[12,64,512]{2,1,0:T(8,128)S(1)}, f32[12,64,512]{2,1,0:T(8,128)}, u32[]{:S(2)}) copy-start(f32[12,64,512]{2,1,0:T(8,128)} %get-tuple-element.14) | copy-start | bytes 4718596

commit v2 on v1

v2 whole, which is shorter than its diff:
```python
import functools

import jax
import jax.numpy as jnp
from jax import lax
from jax.experimental import pallas as pl
from jax.experimental.pallas import tpu as pltpu
from jax.sharding import PartitionSpec as P

APB = 64
VMEM_BYTES = 56 * 1024 * 1024
ARBITRARY = pltpu.GridDimensionSemantics.ARBITRARY


def shifted(value, axis, steps):
    count = lax.axis_size(axis)
    pairs = [(source, (source + steps) % count) for source in range(count)]
    return lax.ppermute(value, axis, pairs)


def swapped(value, axis, bit):
    count = lax.axis_size(axis)
    return lax.ppermute(value, axis, [(source, source ^ bit) for source in range(count)])


def push_kernel(
    group, sets, slots, share, mask_ref, ham_ref, cot_ref, edge_ref, low_ref, own_ref, high_ref, copy_ref, left, total
):
    step = pl.program_id(0)
    orbitals = ham_ref.shape[2]
    columns = cot_ref.shape[2]
    spread = (slots + group - 1) * share

    @pl.when(step == 0)
    def _():
        total[...] = jnp.zeros_like(total)
        left[...] = jnp.zeros_like(left)
        copy_ref[...] = edge_ref[...]

    for part in range(sets):
        base = part * group
        for k in range(group):
            row = step * (sets * group) + base + k
            for slot in range(slots):
                kept = mask_ref[row, slot] != 0
                block = ham_ref[base + k, slot * share : (slot + 1) * share, :]
                at = (slot + k) * share
                left[part, at : at + share, k * orbitals : (k + 1) * orbitals] = jnp.where(
                    kept, block, jnp.zeros_like(block)
                )
        right = cot_ref[base : base + group].reshape(group * orbitals, columns)
        first = pl.multiple_of((step * sets + part) * (group * share), group * share)
        piece = 2 * share
        for at in range(0, spread, piece):
            size = min(piece, spread - at)
            total[pl.ds(first + at, size), :] += jnp.dot(
                left[part, at : at + size, :], right, preferred_element_type=jnp.float32
            )

    @pl.when(step == pl.num_programs(0) - 1)
    def _():
        halo = low_ref.shape[0]
        own = own_ref.shape[0]
        low_ref[...] = (2.0 * total[:halo, :]).astype(low_ref.dtype)
        own_ref[...] = 2.0 * total[halo : halo + own, :]
        high_ref[...] = (2.0 * total[halo + own :, :]).astype(high_ref.dtype)


def largest_divisor(count, limit):
    return max(k for k in range(1, limit + 1) if count % k == 0)


def push(ham, mask, cotangent, term, share):
    rows, depth, orbitals = ham.shape
    columns = cotangent.shape[2]
    slots = depth // share
    reach = (slots - 1) // 2
    group = largest_divisor(rows, 2)
    sets = largest_divisor(rows // group, 2)
    each = group * sets
    kernel = functools.partial(push_kernel, group, sets, slots, share)
    flops = 2 * rows * depth * orbitals * columns
    edge = pl.BlockSpec((reach * share, columns), lambda i, m: (0, 0))
    return pl.pallas_call(
        kernel,
        out_shape=(
            jax.ShapeDtypeStruct((reach * share, columns), jnp.bfloat16),
            jax.ShapeDtypeStruct((rows * share, columns), jnp.float32),
            jax.ShapeDtypeStruct((reach * share, columns), jnp.bfloat16),
            jax.ShapeDtypeStruct((reach * share, columns), term.dtype),
        ),
        grid_spec=pltpu.PrefetchScalarGridSpec(
            num_scalar_prefetch=1,
            grid=(rows // each,),
            in_specs=[
                pl.BlockSpec((each, depth, orbitals), lambda i, m: (i, 0, 0)),
                pl.BlockSpec((each, orbitals, columns), lambda i, m: (i, 0, 0)),
                edge,
            ],
            out_specs=[edge, pl.BlockSpec((rows * share, columns), lambda i, m: (0, 0)), edge, edge],
            scratch_shapes=[
                pltpu.VMEM((sets, (slots + group - 1) * share, group * orbitals), jnp.bfloat16),
                pltpu.VMEM(((rows + 2 * reach) * share, columns), jnp.float32),
            ],
        ),
        compiler_params=pltpu.CompilerParams(
            dimension_semantics=(ARBITRARY,), vmem_limit_bytes=VMEM_BYTES
        ),
        cost_estimate=pl.CostEstimate(flops=flops, bytes_accessed=ham.size * 2, transcendentals=0),
        name="push_blocks",
    )(mask, ham, cotangent, term)


def pull_kernel(
    first_row, each, carried, slots, share, mask_ref, side_ref, ham_ref, slope_ref, cot_ref, prev_ref, head_ref, tail_ref, *rest,
):
    keep_ref, send_ref, force_ref = rest[carried : carried + 3]
    window, both, product = rest[-3:]
    step = pl.program_id(0)
    orbitals = ham_ref.shape[2]
    side = side_ref[0]

    @pl.when(step == 0)
    def _():
        split = head_ref.shape[0]
        window[:split, :] = head_ref[...]
        window[split:, :] = tail_ref[...]

    mine = pl.multiple_of(side * share, share)
    other = pl.multiple_of((1 - side) * share, share)
    for k in range(each):
        at = step * each + k
        row = first_row + at
        for slot in range(slots):
            kept = mask_ref[row, slot] != 0
            span = slice(slot * share, (slot + 1) * share)
            block = ham_ref[k, span, :]
            both[k, span, :orbitals] = jnp.where(kept, block, jnp.zeros_like(block))
            block = slope_ref[k, span, :]
            both[k, span, orbitals:] = jnp.where(kept, block, jnp.zeros_like(block))
        near = window[pl.ds(pl.multiple_of(at * share, share), slots * share), :]
        product[k] = lax.dot_general(
            both[k], near, (((0,), (0,)), ((), ())), preferred_element_type=jnp.float32
        )
        keep_ref[k] = 2.0 * product[k, pl.ds(mine, share), :] - prev_ref[k].astype(jnp.float32)
        send_ref[k] = (2.0 * product[k, pl.ds(other, share), :]).astype(send_ref.dtype)
        work = product[k, orbitals:, :] * cot_ref[k].astype(jnp.float32)
        lanes = 128
        folded = work[:, :lanes]
        for lane in range(lanes, work.shape[1], lanes):
            folded = folded + work[:, lane : lane + lanes]
        force_ref[k] = 2.0 * jnp.sum(folded.T, axis=0, keepdims=True)


def pull(ham, slope, mask, side, cotangent, previous, head, tail, share, first_row, rows, carried, keep):
    total_rows, depth, orbitals = ham.shape
    columns = cotangent.shape[2]
    slots = depth // share
    each = largest_divisor(rows, 3)
    skip = first_row // each
    assert skip * each == first_row
    held = tuple(carried) + ((keep,) if keep is not None else ())
    kernel = functools.partial(pull_kernel, first_row, each, len(held) + len(carried), slots, share)
    flops = 4 * rows * depth * orbitals * columns
    row_block = lambda *dims: pl.BlockSpec((each,) + dims, lambda i, m, s: (i + skip, 0, 0))
    whole = lambda a: pl.BlockSpec(a.shape, lambda i, m, s: (0, 0))
    out_block = lambda *dims: pl.BlockSpec((each,) + dims, lambda i, m, s: (i, 0, 0))
    anywhere = pl.BlockSpec(memory_space=pl.ANY)
    inputs = (mask, side, ham, slope, cotangent, previous, head, tail)
    aliases = {len(inputs) + k: k for k in range(len(held))}
    return pl.pallas_call(
        kernel,
        out_shape=tuple(jax.ShapeDtypeStruct(a.shape, a.dtype) for a in carried)
        + (
            jax.ShapeDtypeStruct((total_rows, share, columns), jnp.float32),
            jax.ShapeDtypeStruct((rows, share, columns), jnp.bfloat16),
            jax.ShapeDtypeStruct((rows, 1, orbitals), jnp.float32),
        ),
        grid_spec=pltpu.PrefetchScalarGridSpec(
            num_scalar_prefetch=2,
            grid=(rows // each,),
            in_specs=[
                row_block(depth, orbitals),
                row_block(depth, orbitals),
                row_block(orbitals, columns),
                row_block(share, columns),
                whole(head),
                whole(tail),
            ]
            + [anywhere] * len(held),
            out_specs=[anywhere] * len(carried)
            + [
                row_block(share, columns),
                out_block(share, columns),
                out_block(1, orbitals),
            ],
            scratch_shapes=[
                pltpu.VMEM((head.shape[0] + tail.shape[0], columns), jnp.bfloat16),
                pltpu.VMEM((each, depth, 2 * orbitals), jnp.bfloat16),
                pltpu.VMEM((each, 2 * orbitals, columns), jnp.float32),
            ],
        ),
        input_output_aliases=aliases,
        compiler_params=pltpu.CompilerParams(
            dimension_semantics=(ARBITRARY,), vmem_limit_bytes=VMEM_BYTES
        ),
        cost_estimate=pl.CostEstimate(
            flops=flops, bytes_accessed=4 * rows * depth * orbitals, transcendentals=0
        ),
        name="pull_blocks",
    )(*inputs, *held)


def local(term_now, term_prev, cotangent, ham_blocks, block_mask, ham_slope, atom_owner):
    rows, slots, share, orbitals = ham_blocks.shape
    columns = term_now.shape[2]
    reach = (slots - 1) // 2
    edge = reach * share
    half = rows // 2
    ham = ham_blocks.reshape(rows, slots * share, orbitals)
    slope = ham_slope.reshape(rows, slots * share, orbitals)
    term = term_now.reshape(rows * share, columns)
    side = lax.axis_index("layers").astype(jnp.int32).reshape(1)

    below = shifted(term[rows * share - edge :], "rows", 1)
    to_below, own, to_above, first_edge = push(ham, block_mask, cotangent, term, share)
    above = shifted(first_edge, "rows", -1)

    args = (ham, slope, block_mask, side, cotangent, term_prev)
    to_below, to_above, keep, send_a, force_a = pull(
        *args, below, term, share, 0, half, (to_below, to_above), None
    )
    from_above = shifted(to_below, "rows", -1)
    from_below = shifted(to_above, "rows", 1)
    got_a = swapped(send_a, "layers", 1)
    keep, send_b, force_b = pull(*args, term, above, share, half, rows - half, (), keep)
    got_b = swapped(send_b, "layers", 1)

    row_force = jnp.concatenate([force_a, force_b], axis=0).reshape(rows, orbitals)
    atom_ids = lax.broadcasted_iota(jnp.int32, (1, 1, APB), 2)
    owned = jnp.where(atom_owner[:, :, None] == atom_ids, row_force[:, :, None], 0.0)
    forces = jnp.sum(owned, axis=1)
    forces = forces + swapped(forces, "layers", 1)
    bit = 1
    while bit < lax.axis_size("cols"):
        forces = forces + swapped(forces, "cols", bit)
        bit *= 2

    got = jnp.concatenate([got_a, got_b], axis=0)
    term_next = (keep + got.astype(jnp.float32)).astype(jnp.bfloat16)
    own = own.reshape(rows, share, columns)
    got = jnp.concatenate([from_below, from_above], axis=0).reshape(rows, share, columns)
    grad_term = (own + got.astype(jnp.float32)).astype(jnp.bfloat16)
    return (term_next, grad_term, forces)


def solution(mesh):
    return jax.shard_map(
        local,
        mesh=mesh,
        in_specs=(
            P("rows", "layers", "cols"),
            P("rows", "layers", "cols"),
            P("rows", None, "cols"),
            P("rows", None, "layers", None),
            P("rows", None),
            P("rows", None, "layers", None),
            P("rows", None),
        ),
        out_specs=(P("rows", "layers", "cols"), P("rows", "layers", "cols"), P("rows", None)),
        check_vma=False,
    )
```

time: 101 us -> 103 us (1.020)
  the two profiles are of different devices: /device:TPU:26 before, /device:TPU:0 now
where the time goes in v2:
time: 103 us; the launch traced here: 102 us
  Pallas kernels  39.4 us (38%)
  waiting for transfers between devices  38 us (37%)
  starting transfers between devices  14.1 us (14%)
  other arithmetic  7.11 us (7%)
  local copies, waits for them, and re-layouts  3.16 us (3%)
    ppermute x5, waiting for transfers between devices, swapped(): lax.ppermute(value, axis, [(source, source ^ bit) for source in range(cou...  31.6 us
    pallas_call x2, Pallas kernels, pull(): pl.pallas_call(kernel, out_shape=tuple((jax.ShapeDtypeStruct(a.shape, a.d...  24.5 us
    pallas_call x1, Pallas kernels, push(): pl.pallas_call(kernel, out_shape=(jax.ShapeDtypeStruct((reach * share, co...  14.9 us
    ppermute x4, starting transfers between devices, shifted(): return lax.ppermute(value, axis, pairs)  8.96 us
    ppermute x4, waiting for transfers between devices, shifted(): return lax.ppermute(value, axis, pairs)  6.33 us
    ppermute x5, starting transfers between devices, swapped(): lax.ppermute(value, axis, [(source, source ^ bit) for source in range(cou...  5.17 us
    convert_element_type x1, other arithmetic, local(): term_next = (keep + got.astype(jnp.float32)).astype(jnp.bfloat16)  3.77 us
  transfers between devices with their start and end apart: 9, of which 5 were waited for; matrix products, arithmetic and copies ran while one was open for 5% of the time, Pallas kernels for 26%

profile of v2, /device:TPU:0, one launch (start us, length us, event | category | flops | bytes accessed | tf_op | source)
XLA Modules:
  0.0 102.4 jit_solution(1401821526419082263)
XLA Ops:
  0.6 1.2 %slice.6 = bf16[12,64,512]{2,1,0:T(8,128)(2,1)S(1)} slice(bf16[24,64,512]{2,1,0:T(8,128)(2,1)} %param.7), slice={[12:24], [0:64], [0:512]} | slice | bytes 1572864 | tf_op jit(solution)/shard_map/slice | solution.py:225
  1.8 3.1 %collective-permute-start.1 = (bf16[768,512]{1,0:T(8,128)(2,1)S(1)}, bf16[768,512]{1,0:T(8,128)(2,1)S(1)}, u32[]{:S(2)}, u32[]{:S(2)}) collective-permute-start(bf16[768,512]{1,0:T(8,128)(2,1)S(1)} %bitcast.16), channel_id=1, source_target_pairs={{0,8},{8,16},{16,24},{24,0},{1,9},{9,17},{17,25},{25,1},{2,10},{10... | collective-permute-start | bytes 2359304 | tf_op jit(solution)/shard_map/ppermute | solution.py:18
  4.9 14.9 %push_blocks.1 = (bf16[768,512]{1,0:T(8,128)(2,1)}, f32[1536,512]{1,0:T(8,128)}, bf16[768,512]{1,0:T(8,128)(2,1)}, bf16[768,512]{1,0:T(8,128)(2,1)}) custom-call(s32[24,25]{1,0:T(8,128)} %mask_ref.5, bf16[24,1600,128]{2,1,0:T(8,128)(2,1)} %bitcast.7, bf16[24,128,512]{2,1,0:T(8,128)(2,1)} %cot_ref.5, bf16[1536,512]{1,0:T(8,128)(2,1)} %bitcast.12), custom_call_target="tpu_custom_call" | custom-call | flops 5033164800 | bytes 9830400 | tf_op jit(solution)/shard_map/push_blocks/pallas_call | solution.py:84
  19.8 2.1 %collective-permute-start = (bf16[768,512]{1,0:T(8,128)(2,1)}, bf16[768,512]{1,0:T(8,128)(2,1)S(1)}, u32[]{:S(2)}, u32[]{:S(2)}) collective-permute-start(bf16[768,512]{1,0:T(8,128)(2,1)} %get-tuple-element.15), channel_id=1, source_target_pairs={{0,24},{8,0},{16,8},{24,16},{1,25},{9,1},{17,9},{25,17},{2,26},{10... | collective-permute-start | bytes 2359304 | tf_op jit(solution)/shard_map/ppermute | solution.py:18
  21.8 2.9 %collective-permute-done.1.head_ref = bf16[768,512]{1,0:T(8,128)(2,1)S(1)} collective-permute-done((bf16[768,512]{1,0:T(8,128)(2,1)S(1)}, bf16[768,512]{1,0:T(8,128)(2,1)S(1)}, u32[]{:S(2)}, u32[]{:S(2)}) %collective-permute-start.1) | collective-permute-done | bytes 786464 | tf_op jit(solution)/shard_map/ppermute | solution.py:18
  24.7 1.0 copy-done.1
  25.7 12.2 %pull_blocks.2 = (bf16[768,512]{1,0:T(8,128)(2,1)}, bf16[768,512]{1,0:T(8,128)(2,1)}, f32[24,64,512]{2,1,0:T(8,128)}, bf16[12,64,512]{2,1,0:T(8,128)(2,1)}, f32[12,1,128]{2,1,0:T(1,128)}) custom-call(s32[24,25]{1,0:T(8,128)} %mask_ref.5, s32[1]{0:T(128)} %bitcast.side_ref, ...), custom_call_target="tpu_custom_call", output_to_operand_aliasing={{0}: (8, {}), {1}: (9, {})} | custom-call | flops 5033164800 | bytes 9830400 | tf_op jit(solution)/shard_map/pull_blocks/pallas_call | solution.py:171
  37.9 3.4 %collective-permute-done.tail_ref = bf16[768,512]{1,0:T(8,128)(2,1)S(1)} collective-permute-done((bf16[768,512]{1,0:T(8,128)(2,1)}, bf16[768,512]{1,0:T(8,128)(2,1)S(1)}, u32[]{:S(2)}, u32[]{:S(2)}) %collective-permute-start) | collective-permute-done | bytes 786464 | tf_op jit(solution)/shard_map/ppermute | solution.py:18
  41.3 1.0 copy-done.4
  42.3 0.0 copy-start.5
  42.3 12.3 %pull_blocks.3 = (f32[24,64,512]{2,1,0:T(8,128)}, bf16[12,64,512]{2,1,0:T(8,128)(2,1)}, f32[12,1,128]{2,1,0:T(1,128)}) custom-call(s32[24,25]{1,0:T(8,128)} %mask_ref.5, s32[1]{0:T(128)} %bitcast.side_ref, bf16[24,1600,128]{2,1,0:T(8,128)(2,1)} %bitcast.9, bf16[24,1600,128]{2,1,0:T(8,128)(2,1)} %bitcast.11, ...), custom_call_target="tpu_custom_call", output_to_operand_aliasing={{0}: (8, {})} | custom-call | flops 5033164800 | bytes 9830400 | tf_op jit(solution)/shard_map/pull_blocks/pallas_call | solution.py:171
  54.6 1.6 %collective-permute-start.3 = (bf16[12,64,512]{2,1,0:T(8,128)(2,1)}, bf16[12,64,512]{2,1,0:T(8,128)(2,1)S(1)}, u32[]{:S(2)}, u32[]{:S(2)}) collective-permute-start(bf16[12,64,512]{2,1,0:T(8,128)(2,1)} %get-tuple-element.21), channel_id=1, source_target_pairs={{0,1},{1,0},{2,3},{3,2},{4,5},{5,4},{6,7},{7,6},{8,9},{9,8},{10,11... | collective-permute-start | bytes 2359304 | tf_op jit(solution)/shard_map/ppermute | solution.py:23
  56.2 0.0 copy-done.7
  56.2 0.5 collective-permute-start.2
  56.7 0.0 copy-done.3
  56.7 0.6 collective-permute-start.4
  57.3 3.3 %collective-permute-start.5 = (bf16[768,512]{1,0:T(8,128)(2,1)S(1)}, bf16[768,512]{1,0:T(8,128)(2,1)S(1)}, u32[]{:S(2)}, u32[]{:S(2)}) collective-permute-start(bf16[768,512]{1,0:T(8,128)(2,1)S(1)} %copy-done.2), channel_id=1, source_target_pairs={{0,24},{8,0},{16,8},{24,16},{1,25},{9,1},{17,9},{25,17},{2,26},{10... | collective-permute-start | bytes 2359304 | tf_op jit(solution)/shard_map/ppermute | solution.py:18
  60.6 0.7 pad_maximum_fusion
  61.3 0.4 select_reduce_fusion
  61.6 1.6 %collective-permute-start.6 = (f32[24,64]{1,0:T(8,128)S(1)}, f32[24,64]{1,0:T(8,128)S(1)}, u32[]{:S(2)}, u32[]{:S(2)}) collective-permute-start(f32[24,64]{1,0:T(8,128)S(1)} %select_reduce_fusion), channel_id=1, source_target_pairs={{0,1},{1,0},{2,3},{3,2},{4,5},{5,4},{6,7},{7,6},{8,9},{9,8},{10,11... | collective-permute-start | bytes 18440 | tf_op jit(solution)/shard_map/ppermute | solution.py:23
  63.2 28.3 %collective-permute-done.6 = f32[24,64]{1,0:T(8,128)S(1)} collective-permute-done((f32[24,64]{1,0:T(8,128)S(1)}, f32[24,64]{1,0:T(8,128)S(1)}, u32[]{:S(2)}, u32[]{:S(2)}) %collective-permute-start.6) | collective-permute-done | bytes 6176 | tf_op jit(solution)/shard_map/ppermute | solution.py:23
  91.5 0.0 collective-permute-start.7
  91.5 1.2 %collective-permute-done.7 = f32[24,64]{1,0:T(8,128)S(1)} collective-permute-done((f32[24,64]{1,0:T(8,128)S(1)}, f32[24,64]{1,0:T(8,128)S(1)}, u32[]{:S(2)}, u32[]{:S(2)}) %collective-permute-start.7) | collective-permute-done | bytes 6176 | tf_op jit(solution)/shard_map/ppermute | solution.py:23
  92.7 1.5 %collective-permute-start.8 = (f32[24,64]{1,0:T(8,128)S(1)}, f32[24,64]{1,0:T(8,128)S(1)}, u32[]{:S(2)}, u32[]{:S(2)}) collective-permute-start(f32[24,64]{1,0:T(8,128)S(1)} %add.19), channel_id=1, source_target_pairs={{0,4},{2,6},{4,0},{6,2},{1,5},{3,7},{5,1},{7,3},{8,12},{10,14},{12... | collective-permute-start | bytes 18440 | tf_op jit(solution)/shard_map/ppermute | solution.py:23
  94.2 2.2 %collective-permute-done.8 = f32[24,64]{1,0:T(8,128)S(1)} collective-permute-done((f32[24,64]{1,0:T(8,128)S(1)}, f32[24,64]{1,0:T(8,128)S(1)}, u32[]{:S(2)}, u32[]{:S(2)}) %collective-permute-start.8) | collective-permute-done | bytes 6176 | tf_op jit(solution)/shard_map/ppermute | solution.py:23
  96.4 0.6 add.20
  97.0 0.0 collective-permute-done.3
  97.0 0.0 collective-permute-done.2
  97.0 3.8 %add_convert_fusion.1 = bf16[24,64,512]{2,1,0:T(8,128)(2,1)} fusion(f32[24,64,512]{2,1,0:T(8,128)} %get-tuple-element.19, bf16[12,64,512]{2,1,0:T(8,128)(2,1)S(1)} %collective-permute-done.3, bf16[12,64,512]{2,1,0:T(8,128)(2,1)S(1)} %collective-permute-done.2), kind=kLoop, calls=%fused_computation.1 | loop fusion | flops 3145728 | bytes 6291456 | tf_op jit(solution)/shard_map/convert_element_type | solution.py:250
  100.7 0.0 collective-permute-done.4
  100.8 0.0 collective-permute-done.5
  100.8 1.7 %add_convert_fusion = bf16[1536,512]{1,0:T(8,128)(2,1)} fusion(f32[1536,512]{1,0:T(8,128)S(1)} %copy-done, bf16[768,512]{1,0:T(8,128)(2,1)S(1)} %collective-permute-done.5, bf16[768,512]{1,0:T(8,128)(2,1)S(1)} %collective-permute-done.4), kind=kLoop, calls=%fused_computation | loop fusion | flops 4718592 | bytes 6291456 | tf_op jit(solution)/shard_map/convert_element_type | solution.py:253
  (13 shorter events, 0.0 us)
Async XLA Ops:
  1.8 22.9 %collective-permute-start.1 = (bf16[768,512]{1,0:T(8,128)(2,1)S(1)}, bf16[768,512]{1,0:T(8,128)(2,1)S(1)}, u32[]{:S(2)}, u32[]{:S(2)}) collective-permute-start(bf16[768,512]{1,0:T(8,128)(2,1)S(1)} %bitcast.16), channel_id=1, source_target_pairs={{0,8},{8,16},{16,24},{24,0},{1,9},{9,17},{17,25},{25,1},{2,10},{10... | collective-permute-start | bytes 2359304 | tf_op jit(solution)/shard_map/ppermute | solution.py:18
  19.8 21.6 %collective-permute-start = (bf16[768,512]{1,0:T(8,128)(2,1)}, bf16[768,512]{1,0:T(8,128)(2,1)S(1)}, u32[]{:S(2)}, u32[]{:S(2)}) collective-permute-start(bf16[768,512]{1,0:T(8,128)(2,1)} %get-tuple-element.15), channel_id=1, source_target_pairs={{0,24},{8,0},{16,8},{24,16},{1,25},{9,1},{17,9},{25,17},{2,26},{10... | collective-permute-start | bytes 2359304 | tf_op jit(solution)/shard_map/ppermute | solution.py:18
  24.7 1.0 copy-start.1
  41.3 1.0 copy-start.4
  42.3 13.9 %copy-start.7 = (bf16[12,64,512]{2,1,0:T(8,128)(2,1)S(1)}, bf16[12,64,512]{2,1,0:T(8,128)(2,1)}, u32[]{:S(2)}) copy-start(bf16[12,64,512]{2,1,0:T(8,128)(2,1)} %get-tuple-element.20) | copy-start | bytes 2359300
  42.3 14.4 %copy-start.3 = (bf16[768,512]{1,0:T(8,128)(2,1)S(1)}, bf16[768,512]{1,0:T(8,128)(2,1)}, u32[]{:S(2)}) copy-start(bf16[768,512]{1,0:T(8,128)(2,1)} %get-tuple-element.23) | copy-start | bytes 2359300
  42.3 15.0 %copy-start.2 = (bf16[768,512]{1,0:T(8,128)(2,1)S(1)}, bf16[768,512]{1,0:T(8,128)(2,1)}, u32[]{:S(2)}) copy-start(bf16[768,512]{1,0:T(8,128)(2,1)} %get-tuple-element.24) | copy-start | bytes 2359300
  42.3 18.2 %copy-start.6 = (f32[12,1,128]{2,1,0:T(1,128)S(1)}, f32[12,1,128]{2,1,0:T(1,128)}, u32[]{:S(2)}) copy-start(f32[12,1,128]{2,1,0:T(1,128)} %get-tuple-element.25) | copy-start | bytes 18436
  42.3 18.9 %copy-start.5 = (s32[24,128]{1,0:T(8,128)S(1)}, s32[24,128]{1,0:T(8,128)}, u32[]{:S(2)}) copy-start(s32[24,128]{1,0:T(8,128)} %param.13) | copy-start | bytes 36868
  54.6 42.3 %collective-permute-start.3 = (bf16[12,64,512]{2,1,0:T(8,128)(2,1)}, bf16[12,64,512]{2,1,0:T(8,128)(2,1)S(1)}, u32[]{:S(2)}, u32[]{:S(2)}) collective-permute-start(bf16[12,64,512]{2,1,0:T(8,128)(2,1)} %get-tuple-element.21), channel_id=1, source_target_pairs={{0,1},{1,0},{2,3},{3,2},{4,5},{5,4},{6,7},{7,6},{8,9},{9,8},{10,11... | collective-permute-start | bytes 2359304 | tf_op jit(solution)/shard_map/ppermute | solution.py:23
  56.2 40.8 %collective-permute-start.2 = (bf16[12,64,512]{2,1,0:T(8,128)(2,1)S(1)}, bf16[12,64,512]{2,1,0:T(8,128)(2,1)S(1)}, u32[]{:S(2)}, u32[]{:S(2)}) collective-permute-start(bf16[12,64,512]{2,1,0:T(8,128)(2,1)S(1)} %copy-done.7), channel_id=1, source_target_pairs={{0,1},{1,0},{2,3},{3,2},{4,5},{5,4},{6,7},{7,6},{8,9},{9,8},{10,11... | collective-permute-start | bytes 2359304 | tf_op jit(solution)/shard_map/ppermute | solution.py:23
  56.7 44.0 %collective-permute-start.4 = (bf16[768,512]{1,0:T(8,128)(2,1)S(1)}, bf16[768,512]{1,0:T(8,128)(2,1)S(1)}, u32[]{:S(2)}, u32[]{:S(2)}) collective-permute-start(bf16[768,512]{1,0:T(8,128)(2,1)S(1)} %copy-done.3), channel_id=1, source_target_pairs={{0,8},{8,16},{16,24},{24,0},{1,9},{9,17},{17,25},{25,1},{2,10},{10... | collective-permute-start | bytes 2359304 | tf_op jit(solution)/shard_map/ppermute | solution.py:18
  57.3 43.5 %collective-permute-start.5 = (bf16[768,512]{1,0:T(8,128)(2,1)S(1)}, bf16[768,512]{1,0:T(8,128)(2,1)S(1)}, u32[]{:S(2)}, u32[]{:S(2)}) collective-permute-start(bf16[768,512]{1,0:T(8,128)(2,1)S(1)} %copy-done.2), channel_id=1, source_target_pairs={{0,24},{8,0},{16,8},{24,16},{1,25},{9,1},{17,9},{25,17},{2,26},{10... | collective-permute-start | bytes 2359304 | tf_op jit(solution)/shard_map/ppermute | solution.py:18
  61.6 29.8 %collective-permute-start.6 = (f32[24,64]{1,0:T(8,128)S(1)}, f32[24,64]{1,0:T(8,128)S(1)}, u32[]{:S(2)}, u32[]{:S(2)}) collective-permute-start(f32[24,64]{1,0:T(8,128)S(1)} %select_reduce_fusion), channel_id=1, source_target_pairs={{0,1},{1,0},{2,3},{3,2},{4,5},{5,4},{6,7},{7,6},{8,9},{9,8},{10,11... | collective-permute-start | bytes 18440 | tf_op jit(solution)/shard_map/ppermute | solution.py:23
  91.5 1.2 %collective-permute-start.7 = (f32[24,64]{1,0:T(8,128)S(1)}, f32[24,64]{1,0:T(8,128)S(1)}, u32[]{:S(2)}, u32[]{:S(2)}) collective-permute-start(f32[24,64]{1,0:T(8,128)S(1)} %add.18), channel_id=1, source_target_pairs={{0,2},{2,0},{4,6},{6,4},{1,3},{3,1},{5,7},{7,5},{8,10},{10,8},{12,... | collective-permute-start | bytes 18440 | tf_op jit(solution)/shard_map/ppermute | solution.py:23
  92.7 3.7 %collective-permute-start.8 = (f32[24,64]{1,0:T(8,128)S(1)}, f32[24,64]{1,0:T(8,128)S(1)}, u32[]{:S(2)}, u32[]{:S(2)}) collective-permute-start(f32[24,64]{1,0:T(8,128)S(1)} %add.19), channel_id=1, source_target_pairs={{0,4},{2,6},{4,0},{6,2},{1,5},{3,7},{5,1},{7,3},{8,12},{10,14},{12... | collective-permute-start | bytes 18440 | tf_op jit(solution)/shard_map/ppermute | solution.py:23
  97.0 3.8 %copy-start = (f32[1536,512]{1,0:T(8,128)S(1)}, f32[1536,512]{1,0:T(8,128)}, u32[]{:S(2)}) copy-start(f32[1536,512]{1,0:T(8,128)} %get-tuple-element.22) | copy-start | bytes 9437188

commit v3 on v2

--- a/solution.py
+++ b/solution.py
@@ -233,19 +233,25 @@
     from_above = shifted(to_below, "rows", -1)
     from_below = shifted(to_above, "rows", 1)
     got_a = swapped(send_a, "layers", 1)
-    keep, send_b, force_b = pull(*args, term, above, share, half, rows - half, (), keep)
+    paired = 2 if lax.axis_size("cols") % 2 == 0 else 1
+    if paired == 2:
+        force_a = force_a + swapped(force_a, "cols", 1)
+    force_a, keep, send_b, force_b = pull(
+        *args, term, above, share, half, rows - half, (force_a,), keep
+    )
     got_b = swapped(send_b, "layers", 1)
 
+    force_b, got_a = lax.optimization_barrier((force_b, got_a))
     row_force = jnp.concatenate([force_a, force_b], axis=0).reshape(rows, orbitals)
     atom_ids = lax.broadcasted_iota(jnp.int32, (1, 1, APB), 2)
     owned = jnp.where(atom_owner[:, :, None] == atom_ids, row_force[:, :, None], 0.0)
     forces = jnp.sum(owned, axis=1)
+    gathered = lax.all_gather(forces, "cols")
+    forces = jnp.concatenate(
+        [jnp.sum(gathered[::paired, :half], axis=0), jnp.sum(gathered[:, half:], axis=0)], axis=0
+    )
     forces = forces + swapped(forces, "layers", 1)
-    bit = 1
-    while bit < lax.axis_size("cols"):
-        forces = forces + swapped(forces, "cols", bit)
-        bit *= 2
-
+    got_b, from_below, from_above, forces = lax.optimization_barrier((got_b, from_below, from_above, forces))
     got = jnp.concatenate([got_a, got_b], axis=0)
     term_next = (keep + got.astype(jnp.float32)).astype(jnp.bfloat16)
     own = own.reshape(rows, share, columns)

time: 103 us -> 83.3 us (0.81)
  waiting for transfers between devices: 38 us -> 14.3 us
  blocking collectives: 0 us -> 5.23 us
  starting transfers between devices: 14.1 us -> 12.7 us
    ppermute x5 -> x4, waiting for transfers between devices: 31.6 us -> 11.4 us  [swapped(): lax.ppermute(value, axis, [(source, source ^ bit) for source in range(cou...]
    all_gather x0 -> x1, blocking collectives: none -> 5.23 us  [local(): gathered = lax.all_gather(forces, 'cols')]
    ppermute x4, waiting for transfers between devices: 6.33 us -> 2.91 us  [shifted(): return lax.ppermute(value, axis, pairs)]
    convert_element_type x1, other arithmetic: 3.77 us -> 1.7 us  [local(): term_next = (keep + got.astype(jnp.float32)).astype(jnp.bfloat16)]
    ppermute x5 -> x4, starting transfers between devices: 5.17 us -> 3.69 us  [swapped(): lax.ppermute(value, axis, [(source, source ^ bit) for source in range(cou...]
    unnamed x16 -> x10, local copies, waits for them, and re-layouts: 1.95 us -> 2.71 us
  transfers between devices with their start and end apart: 9 -> 8, of which waited for: 5 -> 2; matrix products, arithmetic and copies ran while one was open for 5% -> 4% of each run, Pallas kernels for 26% -> 48%
where the time goes in v3:
time: 83.3 us; the launch traced here: 82.6 us
  Pallas kernels  39.4 us (47%)
  waiting for transfers between devices  14.3 us (17%)
  starting transfers between devices  12.7 us (15%)
  other arithmetic  6.4 us (8%)
  blocking collectives  5.23 us (6%)
  local copies, waits for them, and re-layouts  3.92 us (5%)
    pallas_call x2, Pallas kernels, pull(): pl.pallas_call(kernel, out_shape=tuple((jax.ShapeDtypeStruct(a.shape, a.d...  24.5 us
    pallas_call x1, Pallas kernels, push(): pl.pallas_call(kernel, out_shape=(jax.ShapeDtypeStruct((reach * share, co...  14.9 us
    ppermute x4, waiting for transfers between devices, swapped(): lax.ppermute(value, axis, [(source, source ^ bit) for source in range(cou...  11.4 us
    ppermute x4, starting transfers between devices, shifted(): return lax.ppermute(value, axis, pairs)  8.96 us
    all_gather x1, blocking collectives, local(): gathered = lax.all_gather(forces, 'cols')  5.23 us
    ppermute x4, starting transfers between devices, swapped(): lax.ppermute(value, axis, [(source, source ^ bit) for source in range(cou...  3.69 us
    ppermute x4, waiting for transfers between devices, shifted(): return lax.ppermute(value, axis, pairs)  2.91 us
    unnamed x10, local copies, waits for them, and re-layouts  2.71 us
  transfers between devices with their start and end apart: 8, of which 2 were waited for; matrix products, arithmetic and copies ran while one was open for 4% of the time, Pallas kernels for 48%

profile of v3, /device:TPU:0, one launch (start us, length us, event | category | flops | bytes accessed | tf_op | source)
XLA Modules:
  0.0 82.6 jit_solution(13937444210876496503)
XLA Ops:
  0.6 1.2 %slice.12 = bf16[12,64,512]{2,1,0:T(8,128)(2,1)S(1)} slice(bf16[24,64,512]{2,1,0:T(8,128)(2,1)} %param.7), slice={[12:24], [0:64], [0:512]} | slice | bytes 1572864 | tf_op jit(solution)/shard_map/slice | solution.py:225
  1.8 3.1 %collective-permute-start.1 = (bf16[768,512]{1,0:T(8,128)(2,1)S(1)}, bf16[768,512]{1,0:T(8,128)(2,1)S(1)}, u32[]{:S(2)}, u32[]{:S(2)}) collective-permute-start(bf16[768,512]{1,0:T(8,128)(2,1)S(1)} %bitcast.17), channel_id=1, source_target_pairs={{0,8},{8,16},{16,24},{24,0},{1,9},{9,17},{17,25},{25,1},{2,10},{10... | collective-permute-start | bytes 2359304 | tf_op jit(solution)/shard_map/ppermute | solution.py:18
  4.9 14.9 %push_blocks.1 = (bf16[768,512]{1,0:T(8,128)(2,1)}, f32[1536,512]{1,0:T(8,128)}, bf16[768,512]{1,0:T(8,128)(2,1)}, bf16[768,512]{1,0:T(8,128)(2,1)}) custom-call(s32[24,25]{1,0:T(8,128)} %mask_ref.5, bf16[24,1600,128]{2,1,0:T(8,128)(2,1)} %bitcast.8, bf16[24,128,512]{2,1,0:T(8,128)(2,1)} %cot_ref.5, bf16[1536,512]{1,0:T(8,128)(2,1)} %bitcast.13), custom_call_target="tpu_custom_call" | custom-call | flops 5033164800 | bytes 9830400 | tf_op jit(solution)/shard_map/push_blocks/pallas_call | solution.py:84
  19.8 2.1 %collective-permute-start = (bf16[768,512]{1,0:T(8,128)(2,1)}, bf16[768,512]{1,0:T(8,128)(2,1)S(1)}, u32[]{:S(2)}, u32[]{:S(2)}) collective-permute-start(bf16[768,512]{1,0:T(8,128)(2,1)} %get-tuple-element.22), channel_id=1, source_target_pairs={{0,24},{8,0},{16,8},{24,16},{1,25},{9,1},{17,9},{25,17},{2,26},{10... | collective-permute-start | bytes 2359304 | tf_op jit(solution)/shard_map/ppermute | solution.py:18
  21.8 2.9 %collective-permute-done.1.head_ref = bf16[768,512]{1,0:T(8,128)(2,1)S(1)} collective-permute-done((bf16[768,512]{1,0:T(8,128)(2,1)S(1)}, bf16[768,512]{1,0:T(8,128)(2,1)S(1)}, u32[]{:S(2)}, u32[]{:S(2)}) %collective-permute-start.1) | collective-permute-done | bytes 786464 | tf_op jit(solution)/shard_map/ppermute | solution.py:18
  24.7 1.0 %copy-done.2 = bf16[768,512]{1,0:T(8,128)(2,1)} copy-done((bf16[768,512]{1,0:T(8,128)(2,1)}, bf16[768,512]{1,0:T(8,128)(2,1)S(1)}, u32[]{:S(2)}) %copy-start.2) | copy-done | bytes 786456
  25.7 12.2 %pull_blocks.2 = (bf16[768,512]{1,0:T(8,128)(2,1)}, bf16[768,512]{1,0:T(8,128)(2,1)}, f32[24,64,512]{2,1,0:T(8,128)}, bf16[12,64,512]{2,1,0:T(8,128)(2,1)}, f32[12,1,128]{2,1,0:T(1,128)}) custom-call(s32[24,25]{1,0:T(8,128)} %mask_ref.5, s32[1]{0:T(128)} %bitcast.side_ref, ...), custom_call_target="tpu_custom_call", output_to_operand_aliasing={{0}: (8, {}), {1}: (9, {})} | custom-call | flops 5033164800 | bytes 9830400 | tf_op jit(solution)/shard_map/pull_blocks/pallas_call | solution.py:171
  37.9 1.5 %collective-permute-start.3 = (bf16[12,64,512]{2,1,0:T(8,128)(2,1)}, bf16[12,64,512]{2,1,0:T(8,128)(2,1)S(1)}, u32[]{:S(2)}, u32[]{:S(2)}) collective-permute-start(bf16[12,64,512]{2,1,0:T(8,128)(2,1)} %get-tuple-element.29), channel_id=1, source_target_pairs={{0,1},{1,0},{2,3},{3,2},{4,5},{5,4},{6,7},{7,6},{8,9},{9,8},{10,11... | collective-permute-start | bytes 2359304 | tf_op jit(solution)/shard_map/ppermute | solution.py:23
  39.5 0.0 collective-permute-start.2
  39.5 0.0 collective-permute-start.5
  39.5 3.8 %collective-permute-start.6 = (bf16[768,512]{1,0:T(8,128)(2,1)}, bf16[768,512]{1,0:T(8,128)(2,1)S(1)}, u32[]{:S(2)}, u32[]{:S(2)}) collective-permute-start(bf16[768,512]{1,0:T(8,128)(2,1)} %get-tuple-element.33), channel_id=1, source_target_pairs={{0,24},{8,0},{16,8},{24,16},{1,25},{9,1},{17,9},{25,17},{2,26},{10... | collective-permute-start | bytes 2359304 | tf_op jit(solution)/shard_map/ppermute | solution.py:18
  43.3 0.0 collective-permute-done.2
  43.3 1.3 %add.13.rest_0_ = f32[12,1,128]{2,1,0:T(1,128)} add(f32[12,1,128]{2,1,0:T(1,128)} %get-tuple-element.25, f32[12,1,128]{2,1,0:T(1,128)S(1)} %collective-permute-done.2) | non-fusion elementwise | flops 1536 | bytes 18432 | tf_op jit(solution)/shard_map/add | solution.py:238
  44.6 0.0 collective-permute-done.tail_ref
  44.6 1.0 %copy-done.3 = bf16[768,512]{1,0:T(8,128)(2,1)} copy-done((bf16[768,512]{1,0:T(8,128)(2,1)}, bf16[768,512]{1,0:T(8,128)(2,1)S(1)}, u32[]{:S(2)}) %copy-start.3) | copy-done | bytes 786456
  45.6 12.3 %pull_blocks.3 = (f32[12,1,128]{2,1,0:T(1,128)}, f32[24,64,512]{2,1,0:T(8,128)}, bf16[12,64,512]{2,1,0:T(8,128)(2,1)}, f32[12,1,128]{2,1,0:T(1,128)}) custom-call(s32[24,25]{1,0:T(8,128)} %mask_ref.5, s32[1]{0:T(128)} %bitcast.side_ref, bf16[24,1600,128]{2,1,0:T(8,128)(2,1)} %bitcast.10, ...), custom_call_target="tpu_custom_call", output_to_operand_aliasing={{0}: (8, {}), {1}: (9, {})} | custom-call | flops 5033164800 | bytes 9830400 | tf_op jit(solution)/shard_map/pull_blocks/pallas_call | solution.py:171
  57.9 0.6 collective-permute-start.4
  58.5 0.0 collective-permute-done.3
  58.5 0.7 pad_maximum_fusion
  59.2 0.4 select_reduce_fusion
  59.6 5.2 %all-gather = f32[96,64]{1,0:T(8,128)S(1)} all-gather(f32[24,64]{1,0:T(8,128)S(1)} %select_reduce_fusion), channel_id=2, replica_groups=mesh['rows'=4,'cols'=4,'layers'=2] {'cols'}, dimensions={0}, use_global_device_ids=true | all-gather | bytes 30720 | tf_op jit(solution)/shard_map/all_gather | solution.py:249
  64.8 1.5 %collective-permute-start.7 = (f32[24,64]{1,0:T(8,128)S(1)}, f32[24,64]{1,0:T(8,128)S(1)}, u32[]{:S(2)}, u32[]{:S(2)}) collective-permute-start(f32[24,64]{1,0:T(8,128)S(1)} %pad_maximum_fusion.1), channel_id=1, source_target_pairs={{0,1},{1,0},{2,3},{3,2},{4,5},{5,4},{6,7},{7,6},{8,9},{9,8},{10,11... | collective-permute-start | bytes 18440 | tf_op jit(solution)/shard_map/ppermute | solution.py:23
  66.4 11.4 %collective-permute-done.7 = f32[24,64]{1,0:T(8,128)S(1)} collective-permute-done((f32[24,64]{1,0:T(8,128)S(1)}, f32[24,64]{1,0:T(8,128)S(1)}, u32[]{:S(2)}, u32[]{:S(2)}) %collective-permute-start.7) | collective-permute-done | bytes 6176 | tf_op jit(solution)/shard_map/ppermute | solution.py:23
  77.8 0.6 fusion
  78.4 0.0 collective-permute-done.5
  78.4 0.0 collective-permute-done.6
  78.4 0.0 collective-permute-done.4
  78.4 0.0 copy-done.1
  78.4 0.0 copy-start
  78.4 1.7 %add_convert_fusion = bf16[1536,512]{1,0:T(8,128)(2,1)} fusion(f32[1536,512]{1,0:T(8,128)S(1)} %copy-done.1, bf16[768,512]{1,0:T(8,128)(2,1)S(1)} %collective-permute-done.6, bf16[768,512]{1,0:T(8,128)(2,1)S(1)} %collective-permute-done.5), kind=kLoop, calls=%fused_computation | loop fusion | flops 4718592 | bytes 6291456 | tf_op jit(solution)/shard_map/convert_element_type | solution.py:259
  80.1 0.8 copy-done
  80.9 1.7 %add_convert_fusion.1 = bf16[24,64,512]{2,1,0:T(8,128)(2,1)} fusion(f32[24,64,512]{2,1,0:T(8,128)S(1)} %copy-done, bf16[12,64,512]{2,1,0:T(8,128)(2,1)S(1)} %collective-permute-done.4, bf16[12,64,512]{2,1,0:T(8,128)(2,1)S(1)} %collective-permute-done.3), kind=kLoop, calls=%fused_computation.1 | loop fusion | flops 3145728 | bytes 6291456 | tf_op jit(solution)/shard_map/convert_element_type | solution.py:256
  (8 shorter events, 0.0 us)
Async XLA Ops:
  1.8 22.9 %collective-permute-start.1 = (bf16[768,512]{1,0:T(8,128)(2,1)S(1)}, bf16[768,512]{1,0:T(8,128)(2,1)S(1)}, u32[]{:S(2)}, u32[]{:S(2)}) collective-permute-start(bf16[768,512]{1,0:T(8,128)(2,1)S(1)} %bitcast.17), channel_id=1, source_target_pairs={{0,8},{8,16},{16,24},{24,0},{1,9},{9,17},{17,25},{25,1},{2,10},{10... | collective-permute-start | bytes 2359304 | tf_op jit(solution)/shard_map/ppermute | solution.py:18
  19.8 24.8 %collective-permute-start = (bf16[768,512]{1,0:T(8,128)(2,1)}, bf16[768,512]{1,0:T(8,128)(2,1)S(1)}, u32[]{:S(2)}, u32[]{:S(2)}) collective-permute-start(bf16[768,512]{1,0:T(8,128)(2,1)} %get-tuple-element.22), channel_id=1, source_target_pairs={{0,24},{8,0},{16,8},{24,16},{1,25},{9,1},{17,9},{25,17},{2,26},{10... | collective-permute-start | bytes 2359304 | tf_op jit(solution)/shard_map/ppermute | solution.py:18
  24.7 1.0 %copy-start.2 = (bf16[768,512]{1,0:T(8,128)(2,1)}, bf16[768,512]{1,0:T(8,128)(2,1)S(1)}, u32[]{:S(2)}) copy-start(bf16[768,512]{1,0:T(8,128)(2,1)S(1)} %collective-permute-done.1.head_ref) | copy-start | bytes 2359300
  37.9 20.5 %collective-permute-start.3 = (bf16[12,64,512]{2,1,0:T(8,128)(2,1)}, bf16[12,64,512]{2,1,0:T(8,128)(2,1)S(1)}, u32[]{:S(2)}, u32[]{:S(2)}) collective-permute-start(bf16[12,64,512]{2,1,0:T(8,128)(2,1)} %get-tuple-element.29), channel_id=1, source_target_pairs={{0,1},{1,0},{2,3},{3,2},{4,5},{5,4},{6,7},{7,6},{8,9},{9,8},{10,11... | collective-permute-start | bytes 2359304 | tf_op jit(solution)/shard_map/ppermute | solution.py:23
  39.5 3.8 %collective-permute-start.2 = (f32[12,1,128]{2,1,0:T(1,128)}, f32[12,1,128]{2,1,0:T(1,128)S(1)}, u32[]{:S(2)}, u32[]{:S(2)}) collective-permute-start(f32[12,1,128]{2,1,0:T(1,128)} %get-tuple-element.25), channel_id=1, source_target_pairs={{0,2},{2,0},{4,6},{6,4},{1,3},{3,1},{5,7},{7,5},{8,10},{10,8},{12,... | collective-permute-start | bytes 18440 | tf_op jit(solution)/shard_map/ppermute | solution.py:23
  39.5 38.9 %collective-permute-start.5 = (bf16[768,512]{1,0:T(8,128)(2,1)}, bf16[768,512]{1,0:T(8,128)(2,1)S(1)}, u32[]{:S(2)}, u32[]{:S(2)}) collective-permute-start(bf16[768,512]{1,0:T(8,128)(2,1)} %get-tuple-element.32), channel_id=1, source_target_pairs={{0,8},{8,16},{16,24},{24,0},{1,9},{9,17},{17,25},{25,1},{2,10},{10... | collective-permute-start | bytes 2359304 | tf_op jit(solution)/shard_map/ppermute | solution.py:18
  39.5 38.9 %collective-permute-start.6 = (bf16[768,512]{1,0:T(8,128)(2,1)}, bf16[768,512]{1,0:T(8,128)(2,1)S(1)}, u32[]{:S(2)}, u32[]{:S(2)}) collective-permute-start(bf16[768,512]{1,0:T(8,128)(2,1)} %get-tuple-element.33), channel_id=1, source_target_pairs={{0,24},{8,0},{16,8},{24,16},{1,25},{9,1},{17,9},{25,17},{2,26},{10... | collective-permute-start | bytes 2359304 | tf_op jit(solution)/shard_map/ppermute | solution.py:18
  44.6 1.0 %copy-start.3 = (bf16[768,512]{1,0:T(8,128)(2,1)}, bf16[768,512]{1,0:T(8,128)(2,1)S(1)}, u32[]{:S(2)}) copy-start(bf16[768,512]{1,0:T(8,128)(2,1)S(1)} %collective-permute-done.tail_ref) | copy-start | bytes 2359300
  45.6 13.6 %copy-start.4 = (s32[24,128]{1,0:T(8,128)S(1)}, s32[24,128]{1,0:T(8,128)}, u32[]{:S(2)}) copy-start(s32[24,128]{1,0:T(8,128)} %param.13) | copy-start | bytes 36868
  45.6 32.8 %copy-start.1 = (f32[1536,512]{1,0:T(8,128)S(1)}, f32[1536,512]{1,0:T(8,128)}, u32[]{:S(2)}) copy-start(f32[1536,512]{1,0:T(8,128)} %get-tuple-element.37) | copy-start | bytes 9437188
  57.9 20.5 %collective-permute-start.4 = (bf16[12,64,512]{2,1,0:T(8,128)(2,1)}, bf16[12,64,512]{2,1,0:T(8,128)(2,1)S(1)}, u32[]{:S(2)}, u32[]{:S(2)}) collective-permute-start(bf16[12,64,512]{2,1,0:T(8,128)(2,1)} %get-tuple-element.31), channel_id=1, source_target_pairs={{0,1},{1,0},{2,3},{3,2},{4,5},{5,4},{6,7},{7,6},{8,9},{9,8},{10,11... | collective-permute-start | bytes 2359304 | tf_op jit(solution)/shard_map/ppermute | solution.py:23
  64.8 12.9 %collective-permute-start.7 = (f32[24,64]{1,0:T(8,128)S(1)}, f32[24,64]{1,0:T(8,128)S(1)}, u32[]{:S(2)}, u32[]{:S(2)}) collective-permute-start(f32[24,64]{1,0:T(8,128)S(1)} %pad_maximum_fusion.1), channel_id=1, source_target_pairs={{0,1},{1,0},{2,3},{3,2},{4,5},{5,4},{6,7},{7,6},{8,9},{9,8},{10,11... | collective-permute-start | bytes 18440 | tf_op jit(solution)/shard_map/ppermute | solution.py:23
  78.4 2.5 %copy-start = (f32[24,64,512]{2,1,0:T(8,128)S(1)}, f32[24,64,512]{2,1,0:T(8,128)}, u32[]{:S(2)}) copy-start(f32[24,64,512]{2,1,0:T(8,128)} %get-tuple-element.27) | copy-start | bytes 9437188

commit v4 on v3

--- a/solution.py
+++ b/solution.py
@@ -211,6 +211,54 @@
     )(*inputs, *held)
 
 
+def add_kernel(steps, own_ref, first_ref, second_ref, *rest):
+    out_ref = rest[-1]
+    step = pl.program_id(0)
+
+    @pl.when(step < steps)
+    def _():
+        out_ref[...] = (own_ref[...] + first_ref[...].astype(jnp.float32)).astype(out_ref.dtype)
+
+    @pl.when(step >= steps)
+    def _():
+        out_ref[...] = (own_ref[...] + second_ref[...].astype(jnp.float32)).astype(out_ref.dtype)
+
+
+def add_parts(own, arrived, size, places, filled):
+    columns = own.shape[1]
+    steps = 2
+    piece = size // steps
+    (one, one_at), (two, two_at) = arrived
+
+    def spec(first_at, second_at, turn):
+        def place(i):
+            near = jnp.minimum(i, steps - 1) if turn == 0 else i
+            far = jnp.maximum(i - steps, 0)
+            if turn == 0:
+                return (first_at * steps + near, 0)
+            if turn == 1:
+                return (second_at * steps + far, 0)
+            return (jnp.where(i < steps, first_at * steps + i, second_at * steps + i - steps), 0)
+
+        return pl.BlockSpec((piece, columns), place)
+
+    held = () if filled is None else (filled,)
+    return pl.pallas_call(
+        functools.partial(add_kernel, steps),
+        out_shape=jax.ShapeDtypeStruct(own.shape, jnp.bfloat16),
+        grid=(2 * steps,),
+        in_specs=[spec(*places, 2), spec(one_at, 0, 0), spec(0, two_at, 1)]
+        + [pl.BlockSpec(memory_space=pl.ANY)] * len(held),
+        out_specs=spec(*places, 2),
+        input_output_aliases={3: 0} if held else {},
+        compiler_params=pltpu.CompilerParams(
+            dimension_semantics=(ARBITRARY,), vmem_limit_bytes=8 * 1024 * 1024
+        ),
+        cost_estimate=pl.CostEstimate(flops=0, bytes_accessed=0, transcendentals=0),
+        name="add_parts",
+    )(own, one, two, *held)
+
+
 def local(term_now, term_prev, cotangent, ham_blocks, block_mask, ham_slope, atom_owner):
     rows, slots, share, orbitals = ham_blocks.shape
     columns = term_now.shape[2]
@@ -227,21 +275,18 @@
     above = shifted(first_edge, "rows", -1)
 
     args = (ham, slope, block_mask, side, cotangent, term_prev)
-    to_below, to_above, keep, send_a, force_a = pull(
-        *args, below, term, share, 0, half, (to_below, to_above), None
-    )
-    from_above = shifted(to_below, "rows", -1)
+    to_above, keep, send_a, force_a = pull(*args, below, term, share, 0, half, (to_above,), None)
     from_below = shifted(to_above, "rows", 1)
     got_a = swapped(send_a, "layers", 1)
     paired = 2 if lax.axis_size("cols") % 2 == 0 else 1
     if paired == 2:
         force_a = force_a + swapped(force_a, "cols", 1)
-    force_a, keep, send_b, force_b = pull(
-        *args, term, above, share, half, rows - half, (force_a,), keep
+    force_a, to_below, keep, send_b, force_b = pull(
+        *args, term, above, share, half, rows - half, (force_a, to_below), keep
     )
     got_b = swapped(send_b, "layers", 1)
-
-    force_b, got_a = lax.optimization_barrier((force_b, got_a))
+    from_above = shifted(to_below, "rows", -1)
+
     row_force = jnp.concatenate([force_a, force_b], axis=0).reshape(rows, orbitals)
     atom_ids = lax.broadcasted_iota(jnp.int32, (1, 1, APB), 2)
     owned = jnp.where(atom_owner[:, :, None] == atom_ids, row_force[:, :, None], 0.0)
@@ -250,14 +295,23 @@
     forces = jnp.concatenate(
         [jnp.sum(gathered[::paired, :half], axis=0), jnp.sum(gathered[:, half:], axis=0)], axis=0
     )
-    forces = forces + swapped(forces, "layers", 1)
-    got_b, from_below, from_above, forces = lax.optimization_barrier((got_b, from_below, from_above, forces))
-    got = jnp.concatenate([got_a, got_b], axis=0)
-    term_next = (keep + got.astype(jnp.float32)).astype(jnp.bfloat16)
-    own = own.reshape(rows, share, columns)
-    got = jnp.concatenate([from_below, from_above], axis=0).reshape(rows, share, columns)
-    grad_term = (own + got.astype(jnp.float32)).astype(jnp.bfloat16)
-    return (term_next, grad_term, forces)
+    others = swapped(forces, "layers", 1)
+
+    keep = keep.reshape(rows * share, columns)
+    got_a = got_a.reshape(half * share, columns)
+    got_b = got_b.reshape((rows - half) * share, columns)
+    size = edge // 2
+    term_next = add_parts(keep, ((got_a, 0), (got_a, 1)), size, (0, 1), None)
+    from_below, term_next = lax.optimization_barrier((from_below, term_next))
+    grad_term = add_parts(own, ((from_below, 0), (from_below, 1)), size, (0, 1), None)
+    got_b, grad_term = lax.optimization_barrier((got_b, grad_term))
+    term_next = add_parts(keep, ((got_b, 0), (got_b, 1)), size, (2, 3), term_next)
+    others, term_next = lax.optimization_barrier((others, term_next))
+    forces = forces + others
+    from_above, term_next, forces = lax.optimization_barrier((from_above, term_next, forces))
+    grad_term = add_parts(own, ((from_above, 0), (from_above, 1)), size, (2, 3), grad_term)
+    shape = (rows, share, columns)
+    return (term_next.reshape(shape), grad_term.reshape(shape), forces)
 
 
 def solution(mesh):

time: 83.3 us -> 79.6 us (0.956)
  waiting for transfers between devices: 14.3 us -> 6.59 us
  Pallas kernels: 39.4 us -> 45.3 us
  other arithmetic: 6.4 us -> 3 us
  local copies, waits for them, and re-layouts: 3.92 us -> 5.63 us
    ppermute x4, waiting for transfers between devices: 11.4 us -> 3.28 us  [swapped(): lax.ppermute(value, axis, [(source, source ^ bit) for source in range(cou...]
    pallas_call x0 -> x4, Pallas kernels: none -> 5.97 us  [add_parts(): pl.pallas_call(functools.partial(add_kernel, steps), out_shape=jax.ShapeD...]
    convert_element_type x2 -> x0, other arithmetic: 3.39 us -> none  [the longest x1 1.7 us: local(): term_next = (keep + got.astype(jnp.float32)).astype(jnp.bfloat16)]
    unnamed x10 -> x12, local copies, waits for them, and re-layouts: 2.71 us -> 4.42 us
    ppermute x4, starting transfers between devices: 8.96 us -> 7.54 us  [shifted(): return lax.ppermute(value, axis, pairs)]
    ppermute x4, starting transfers between devices: 3.69 us -> 4.75 us  [swapped(): lax.ppermute(value, axis, [(source, source ^ bit) for source in range(cou...]
  transfers between devices with their start and end apart: 8 -> 8, of which waited for: 2 -> 3; matrix products, arithmetic and copies ran while one was open for 4% -> 4% of each run, Pallas kernels for 48% -> 56%
where the time goes in v4:
time: 79.6 us; the launch traced here: 78.8 us
  Pallas kernels  45.3 us (57%)
  starting transfers between devices  12.3 us (15%)
  waiting for transfers between devices  6.59 us (8%)
  local copies, waits for them, and re-layouts  5.63 us (7%)
  blocking collectives  5.23 us (7%)
  other arithmetic  3 us (4%)
    pallas_call x2, Pallas kernels, pull(): pl.pallas_call(kernel, out_shape=tuple((jax.ShapeDtypeStruct(a.shape, a.d...  24.5 us
    pallas_call x1, Pallas kernels, push(): pl.pallas_call(kernel, out_shape=(jax.ShapeDtypeStruct((reach * share, co...  14.9 us
    ppermute x4, starting transfers between devices, shifted(): return lax.ppermute(value, axis, pairs)  7.54 us
    pallas_call x4, Pallas kernels, add_parts(): pl.pallas_call(functools.partial(add_kernel, steps), out_shape=jax.ShapeD...  5.97 us
    all_gather x1, blocking collectives, local(): gathered = lax.all_gather(forces, 'cols')  5.23 us
    ppermute x4, starting transfers between devices, swapped(): lax.ppermute(value, axis, [(source, source ^ bit) for source in range(cou...  4.75 us
    unnamed x12, local copies, waits for them, and re-layouts  4.42 us
    ppermute x4, waiting for transfers between devices, shifted(): return lax.ppermute(value, axis, pairs)  3.31 us
  transfers between devices with their start and end apart: 8, of which 3 were waited for; matrix products, arithmetic and copies ran while one was open for 4% of the time, Pallas kernels for 56%

profile of v4, /device:TPU:0, one launch (start us, length us, event | category | flops | bytes accessed | tf_op | source)
XLA Modules:
  0.0 78.8 jit_solution(3468189316998295113)
XLA Ops:
  0.6 1.2 %slice.12 = bf16[12,64,512]{2,1,0:T(8,128)(2,1)S(1)} slice(bf16[24,64,512]{2,1,0:T(8,128)(2,1)} %param.7), slice={[12:24], [0:64], [0:512]} | slice | bytes 1572864 | tf_op jit(solution)/shard_map/slice | solution.py:273
  1.8 3.1 %collective-permute-start.1 = (bf16[768,512]{1,0:T(8,128)(2,1)S(1)}, bf16[768,512]{1,0:T(8,128)(2,1)S(1)}, u32[]{:S(2)}, u32[]{:S(2)}) collective-permute-start(bf16[768,512]{1,0:T(8,128)(2,1)S(1)} %bitcast.28), channel_id=1, source_target_pairs={{0,8},{8,16},{16,24},{24,0},{1,9},{9,17},{17,25},{25,1},{2,10},{10... | collective-permute-start | bytes 2359304 | tf_op jit(solution)/shard_map/ppermute | solution.py:18
  4.9 14.9 %push_blocks.1 = (bf16[768,512]{1,0:T(8,128)(2,1)}, f32[1536,512]{1,0:T(8,128)}, bf16[768,512]{1,0:T(8,128)(2,1)}, bf16[768,512]{1,0:T(8,128)(2,1)}) custom-call(s32[24,25]{1,0:T(8,128)} %mask_ref.5, bf16[24,1600,128]{2,1,0:T(8,128)(2,1)} %bitcast.18, bf16[24,128,512]{2,1,0:T(8,128)(2,1)} %cot_ref.5, bf16[1536,512]{1,0:T(8,128)(2,1)} %bitcast.23), custom_call_target="tpu_custom_call" | custom-call | flops 5033164800 | bytes 9830400 | tf_op jit(solution)/shard_map/push_blocks/pallas_call | solution.py:84
  19.8 2.1 %collective-permute-start = (bf16[768,512]{1,0:T(8,128)(2,1)}, bf16[768,512]{1,0:T(8,128)(2,1)S(1)}, u32[]{:S(2)}, u32[]{:S(2)}) collective-permute-start(bf16[768,512]{1,0:T(8,128)(2,1)} %get-tuple-element.25), channel_id=1, source_target_pairs={{0,24},{8,0},{16,8},{24,16},{1,25},{9,1},{17,9},{25,17},{2,26},{10... | collective-permute-start | bytes 2359304 | tf_op jit(solution)/shard_map/ppermute | solution.py:18
  21.9 2.9 %collective-permute-done.1.head_ref = bf16[768,512]{1,0:T(8,128)(2,1)S(1)} collective-permute-done((bf16[768,512]{1,0:T(8,128)(2,1)S(1)}, bf16[768,512]{1,0:T(8,128)(2,1)S(1)}, u32[]{:S(2)}, u32[]{:S(2)}) %collective-permute-start.1) | collective-permute-done | bytes 786464 | tf_op jit(solution)/shard_map/ppermute | solution.py:18
  24.7 1.0 %copy-done.3 = bf16[768,512]{1,0:T(8,128)(2,1)} copy-done((bf16[768,512]{1,0:T(8,128)(2,1)}, bf16[768,512]{1,0:T(8,128)(2,1)S(1)}, u32[]{:S(2)}) %copy-start.3) | copy-done | bytes 786456
  25.7 12.2 %pull_blocks.2 = (bf16[768,512]{1,0:T(8,128)(2,1)}, f32[24,64,512]{2,1,0:T(8,128)}, bf16[12,64,512]{2,1,0:T(8,128)(2,1)}, f32[12,1,128]{2,1,0:T(1,128)}) custom-call(s32[24,25]{1,0:T(8,128)} %mask_ref.5, s32[1]{0:T(128)} %bitcast.side_ref, bf16[24,1600,128]{2,1,0:T(8,128)(2,1)} %bitcast.19, ...), custom_call_target="tpu_custom_call", output_to_operand_aliasing={{0}: (8, {})} | custom-call | flops 5033164800 | bytes 9830400 | tf_op jit(solution)/shard_map/pull_blocks/pallas_call | solution.py:171
  37.9 0.1 collective-permute-start.2
  38.0 0.1 collective-permute-start.6
  38.1 1.6 %collective-permute-start.7 = (bf16[12,64,512]{2,1,0:T(8,128)(2,1)}, bf16[12,64,512]{2,1,0:T(8,128)(2,1)S(1)}, u32[]{:S(2)}, u32[]{:S(2)}) collective-permute-start(bf16[12,64,512]{2,1,0:T(8,128)(2,1)} %get-tuple-element.37), channel_id=1, source_target_pairs={{0,1},{1,0},{2,3},{3,2},{4,5},{5,4},{6,7},{7,6},{8,9},{9,8},{10,11... | collective-permute-start | bytes 2359304 | tf_op jit(solution)/shard_map/ppermute | solution.py:23
  39.6 0.0 collective-permute-done.2
  39.6 1.3 %add.6.rest_0_ = f32[12,1,128]{2,1,0:T(1,128)} add(f32[12,1,128]{2,1,0:T(1,128)} %get-tuple-element.27, f32[12,1,128]{2,1,0:T(1,128)S(1)} %collective-permute-done.2) | non-fusion elementwise | flops 1536 | bytes 18432 | tf_op jit(solution)/shard_map/add | solution.py:283
  40.9 0.4 collective-permute-done.tail_ref
  41.3 0.9 %copy-done.4 = bf16[768,512]{1,0:T(8,128)(2,1)} copy-done((bf16[768,512]{1,0:T(8,128)(2,1)}, bf16[768,512]{1,0:T(8,128)(2,1)S(1)}, u32[]{:S(2)}) %copy-start.4) | copy-done | bytes 786456
  42.2 12.3 %pull_blocks.3 = (f32[12,1,128]{2,1,0:T(1,128)}, bf16[768,512]{1,0:T(8,128)(2,1)}, f32[24,64,512]{2,1,0:T(8,128)}, bf16[12,64,512]{2,1,0:T(8,128)(2,1)}, f32[12,1,128]{2,1,0:T(1,128)}) custom-call(s32[24,25]{1,0:T(8,128)} %mask_ref.5, s32[1]{0:T(128)} %bitcast.side_ref, ...), custom_call_target="tpu_custom_call", output_to_operand_aliasing={{0}: (8, {}), {1}: (9, {}), {2}: (10, {})} | custom-call | flops 5033164800 | bytes 9830400 | tf_op jit(solution)/shard_map/pull_blocks/pallas_call | solution.py:171
  54.5 1.6 %collective-permute-start.5 = (bf16[12,64,512]{2,1,0:T(8,128)(2,1)}, bf16[12,64,512]{2,1,0:T(8,128)(2,1)S(1)}, u32[]{:S(2)}, u32[]{:S(2)}) collective-permute-start(bf16[12,64,512]{2,1,0:T(8,128)(2,1)} %get-tuple-element.34), channel_id=1, source_target_pairs={{0,1},{1,0},{2,3},{3,2},{4,5},{5,4},{6,7},{7,6},{8,9},{9,8},{10,11... | collective-permute-start | bytes 2359304 | tf_op jit(solution)/shard_map/ppermute | solution.py:23
  56.1 2.3 %collective-permute-start.3 = (bf16[768,512]{1,0:T(8,128)(2,1)}, bf16[768,512]{1,0:T(8,128)(2,1)S(1)}, u32[]{:S(2)}, u32[]{:S(2)}) collective-permute-start(bf16[768,512]{1,0:T(8,128)(2,1)} %get-tuple-element.30), channel_id=1, source_target_pairs={{0,24},{8,0},{16,8},{24,16},{1,25},{9,1},{17,9},{25,17},{2,26},{10... | collective-permute-start | bytes 2359304 | tf_op jit(solution)/shard_map/ppermute | solution.py:18
  58.4 0.7 pad_maximum_fusion
  59.1 0.4 select_reduce_fusion
  59.5 5.2 %all-gather = f32[96,64]{1,0:T(8,128)S(1)} all-gather(f32[24,64]{1,0:T(8,128)S(1)} %select_reduce_fusion), channel_id=2, replica_groups=mesh['rows'=4,'cols'=4,'layers'=2] {'cols'}, dimensions={0}, use_global_device_ids=true | all-gather | bytes 30720 | tf_op jit(solution)/shard_map/all_gather | solution.py:294
  64.8 1.5 %collective-permute-start.4 = (f32[24,64]{1,0:T(8,128)S(1)}, f32[24,64]{1,0:T(8,128)S(1)}, u32[]{:S(2)}, u32[]{:S(2)}) collective-permute-start(f32[24,64]{1,0:T(8,128)S(1)} %pad_maximum_fusion.1), channel_id=1, source_target_pairs={{0,1},{1,0},{2,3},{3,2},{4,5},{5,4},{6,7},{7,6},{8,9},{9,8},{10,11... | collective-permute-start | bytes 18440 | tf_op jit(solution)/shard_map/ppermute | solution.py:23
  66.3 0.0 collective-permute-done.7
  66.3 1.9 %copy-done = f32[24,64,512]{2,1,0:T(8,128)S(1)} copy-done((f32[24,64,512]{2,1,0:T(8,128)S(1)}, f32[24,64,512]{2,1,0:T(8,128)}, u32[]{:S(2)}) %copy-start) | copy-done | bytes 3145752
  68.2 1.5 %add_parts.4.rest_0_ = bf16[1536,512]{1,0:T(8,128)(2,1)} custom-call(f32[1536,512]{1,0:T(8,128)S(1)} %bitcast.12, bf16[768,512]{1,0:T(8,128)(2,1)S(1)} %bitcast.14, bf16[768,512]{1,0:T(8,128)(2,1)S(1)} %bitcast.15), custom_call_target="tpu_custom_call" | custom-call | tf_op jit(solution)/shard_map/add_parts/pallas_call | solution.py:246
  69.7 0.7 copy-done.2
  70.4 1.5 %add_parts.5.rest_0_ = bf16[1536,512]{1,0:T(8,128)(2,1)} custom-call(f32[1536,512]{1,0:T(8,128)S(1)} %copy-done.2, bf16[768,512]{1,0:T(8,128)(2,1)S(1)} %collective-permute-done.6.first_ref.second_ref, bf16[768,512]{1,0:T(8,128)(2,1)S(1)} %collective-permute-done.6.first_ref.second_ref), custom_call_target="tpu_custom_call" | custom-call | tf_op jit(solution)/shard_map/add_parts/pallas_call | solution.py:246
  71.9 3.3 %collective-permute-done.5 = bf16[12,64,512]{2,1,0:T(8,128)(2,1)S(1)} collective-permute-done((bf16[12,64,512]{2,1,0:T(8,128)(2,1)}, bf16[12,64,512]{2,1,0:T(8,128)(2,1)S(1)}, u32[]{:S(2)}, u32[]{:S(2)}) %collective-permute-start.5) | collective-permute-done | bytes 786464 | tf_op jit(solution)/shard_map/ppermute | solution.py:23
  75.2 1.5 %add_parts.6 = bf16[1536,512]{1,0:T(8,128)(2,1)} custom-call(f32[1536,512]{1,0:T(8,128)S(1)} %bitcast.13, bf16[768,512]{1,0:T(8,128)(2,1)S(1)} %bitcast.16, bf16[768,512]{1,0:T(8,128)(2,1)S(1)} %bitcast.17, bf16[1536,512]{1,0:T(8,128)(2,1)} %add_parts.4.rest_0_), custom_call_target="tpu_custom_call", output_to_operand_aliasing={{}: (3, {})} | custom-call | tf_op jit(solution)/shard_map/add_parts/pallas_call | solution.py:246
  76.6 0.0 collective-permute-done.4
  76.6 0.6 fusion
  77.3 0.0 collective-permute-done.3.first_ref.second_ref
  77.3 1.5 %add_parts.7 = bf16[1536,512]{1,0:T(8,128)(2,1)} custom-call(f32[1536,512]{1,0:T(8,128)S(1)} %copy-done.2, bf16[768,512]{1,0:T(8,128)(2,1)S(1)} %collective-permute-done.3.first_ref.second_ref, bf16[768,512]{1,0:T(8,128)(2,1)S(1)} %collective-permute-done.3.first_ref.second_ref, bf16[1536,512]{1,0:T(8,128)(2,1)} %add_parts.5.rest_0_), custom_call_target="tpu_custom_call", output_to_operand_aliasing={{}: (3, {})} | custom-call | tf_op jit(solution)/shard_map/add_parts/pallas_call | solution.py:246
  (12 shorter events, 0.0 us)
Async XLA Ops:
  1.8 22.9 %collective-permute-start.1 = (bf16[768,512]{1,0:T(8,128)(2,1)S(1)}, bf16[768,512]{1,0:T(8,128)(2,1)S(1)}, u32[]{:S(2)}, u32[]{:S(2)}) collective-permute-start(bf16[768,512]{1,0:T(8,128)(2,1)S(1)} %bitcast.28), channel_id=1, source_target_pairs={{0,8},{8,16},{16,24},{24,0},{1,9},{9,17},{17,25},{25,1},{2,10},{10... | collective-permute-start | bytes 2359304 | tf_op jit(solution)/shard_map/ppermute | solution.py:18
  19.8 21.6 %collective-permute-start = (bf16[768,512]{1,0:T(8,128)(2,1)}, bf16[768,512]{1,0:T(8,128)(2,1)S(1)}, u32[]{:S(2)}, u32[]{:S(2)}) collective-permute-start(bf16[768,512]{1,0:T(8,128)(2,1)} %get-tuple-element.25), channel_id=1, source_target_pairs={{0,24},{8,0},{16,8},{24,16},{1,25},{9,1},{17,9},{25,17},{2,26},{10... | collective-permute-start | bytes 2359304 | tf_op jit(solution)/shard_map/ppermute | solution.py:18
  24.7 1.0 %copy-start.3 = (bf16[768,512]{1,0:T(8,128)(2,1)}, bf16[768,512]{1,0:T(8,128)(2,1)S(1)}, u32[]{:S(2)}) copy-start(bf16[768,512]{1,0:T(8,128)(2,1)S(1)} %collective-permute-done.1.head_ref) | copy-start | bytes 2359300
  37.9 1.7 %collective-permute-start.2 = (f32[12,1,128]{2,1,0:T(1,128)}, f32[12,1,128]{2,1,0:T(1,128)S(1)}, u32[]{:S(2)}, u32[]{:S(2)}) collective-permute-start(f32[12,1,128]{2,1,0:T(1,128)} %get-tuple-element.27), channel_id=1, source_target_pairs={{0,2},{2,0},{4,6},{6,4},{1,3},{3,1},{5,7},{7,5},{8,10},{10,8},{12,... | collective-permute-start | bytes 18440 | tf_op jit(solution)/shard_map/ppermute | solution.py:23
  38.0 31.7 %collective-permute-start.6 = (bf16[768,512]{1,0:T(8,128)(2,1)}, bf16[768,512]{1,0:T(8,128)(2,1)S(1)}, u32[]{:S(2)}, u32[]{:S(2)}) collective-permute-start(bf16[768,512]{1,0:T(8,128)(2,1)} %get-tuple-element.36), channel_id=1, source_target_pairs={{0,8},{8,16},{16,24},{24,0},{1,9},{9,17},{17,25},{25,1},{2,10},{10... | collective-permute-start | bytes 2359304 | tf_op jit(solution)/shard_map/ppermute | solution.py:18
  38.1 28.2 %collective-permute-start.7 = (bf16[12,64,512]{2,1,0:T(8,128)(2,1)}, bf16[12,64,512]{2,1,0:T(8,128)(2,1)S(1)}, u32[]{:S(2)}, u32[]{:S(2)}) collective-permute-start(bf16[12,64,512]{2,1,0:T(8,128)(2,1)} %get-tuple-element.37), channel_id=1, source_target_pairs={{0,1},{1,0},{2,3},{3,2},{4,5},{5,4},{6,7},{7,6},{8,9},{9,8},{10,11... | collective-permute-start | bytes 2359304 | tf_op jit(solution)/shard_map/ppermute | solution.py:23
  41.3 0.9 %copy-start.4 = (bf16[768,512]{1,0:T(8,128)(2,1)}, bf16[768,512]{1,0:T(8,128)(2,1)S(1)}, u32[]{:S(2)}) copy-start(bf16[768,512]{1,0:T(8,128)(2,1)S(1)} %collective-permute-done.tail_ref) | copy-start | bytes 2359300
  42.2 16.9 %copy-start.5 = (s32[24,128]{1,0:T(8,128)S(1)}, s32[24,128]{1,0:T(8,128)}, u32[]{:S(2)}) copy-start(s32[24,128]{1,0:T(8,128)} %param.13) | copy-start | bytes 36868
  54.5 20.7 %collective-permute-start.5 = (bf16[12,64,512]{2,1,0:T(8,128)(2,1)}, bf16[12,64,512]{2,1,0:T(8,128)(2,1)S(1)}, u32[]{:S(2)}, u32[]{:S(2)}) collective-permute-start(bf16[12,64,512]{2,1,0:T(8,128)(2,1)} %get-tuple-element.34), channel_id=1, source_target_pairs={{0,1},{1,0},{2,3},{3,2},{4,5},{5,4},{6,7},{7,6},{8,9},{9,8},{10,11... | collective-permute-start | bytes 2359304 | tf_op jit(solution)/shard_map/ppermute | solution.py:23
  56.1 21.2 %collective-permute-start.3 = (bf16[768,512]{1,0:T(8,128)(2,1)}, bf16[768,512]{1,0:T(8,128)(2,1)S(1)}, u32[]{:S(2)}, u32[]{:S(2)}) collective-permute-start(bf16[768,512]{1,0:T(8,128)(2,1)} %get-tuple-element.30), channel_id=1, source_target_pairs={{0,24},{8,0},{16,8},{24,16},{1,25},{9,1},{17,9},{25,17},{2,26},{10... | collective-permute-start | bytes 2359304 | tf_op jit(solution)/shard_map/ppermute | solution.py:18
  64.8 11.9 %collective-permute-start.4 = (f32[24,64]{1,0:T(8,128)S(1)}, f32[24,64]{1,0:T(8,128)S(1)}, u32[]{:S(2)}, u32[]{:S(2)}) collective-permute-start(f32[24,64]{1,0:T(8,128)S(1)} %pad_maximum_fusion.1), channel_id=1, source_target_pairs={{0,1},{1,0},{2,3},{3,2},{4,5},{5,4},{6,7},{7,6},{8,9},{9,8},{10,11... | collective-permute-start | bytes 18440 | tf_op jit(solution)/shard_map/ppermute | solution.py:23
  66.3 1.9 %copy-start = (f32[24,64,512]{2,1,0:T(8,128)S(1)}, f32[24,64,512]{2,1,0:T(8,128)}, u32[]{:S(2)}) copy-start(f32[24,64,512]{2,1,0:T(8,128)} %get-tuple-element.33) | copy-start | bytes 9437188
  68.2 2.2 %copy-start.2 = (f32[1536,512]{1,0:T(8,128)S(1)}, f32[1536,512]{1,0:T(8,128)}, u32[]{:S(2)}) copy-start(f32[1536,512]{1,0:T(8,128)} %get-tuple-element.35.own_ref) | copy-start | bytes 9437188
  70.4 4.8 %copy-start.1 = (f32[24,64,512]{2,1,0:T(8,128)S(1)}, f32[24,64,512]{2,1,0:T(8,128)}, u32[]{:S(2)}) copy-start(f32[24,64,512]{2,1,0:T(8,128)} %get-tuple-element.33) | copy-start | bytes 9437188

commit v5 on v4

--- a/solution.py
+++ b/solution.py
@@ -8,7 +8,7 @@
 from jax.sharding import PartitionSpec as P
 
 APB = 64
-VMEM_BYTES = 56 * 1024 * 1024
+VMEM_BYTES = 62 * 1024 * 1024
 ARBITRARY = pltpu.GridDimensionSemantics.ARBITRARY
 
 
@@ -75,7 +75,7 @@
     columns = cotangent.shape[2]
     slots = depth // share
     reach = (slots - 1) // 2
-    group = largest_divisor(rows, 2)
+    group = largest_divisor(rows, 6)
     sets = largest_divisor(rows // group, 2)
     each = group * sets
     kernel = functools.partial(push_kernel, group, sets, slots, share)
@@ -226,7 +226,7 @@
 
 def add_parts(own, arrived, size, places, filled):
     columns = own.shape[1]
-    steps = 2
+    steps = 1
     piece = size // steps
     (one, one_at), (two, two_at) = arrived
 
@@ -279,11 +279,11 @@
     from_below = shifted(to_above, "rows", 1)
     got_a = swapped(send_a, "layers", 1)
     paired = 2 if lax.axis_size("cols") % 2 == 0 else 1
-    if paired == 2:
-        force_a = force_a + swapped(force_a, "cols", 1)
-    force_a, to_below, keep, send_b, force_b = pull(
-        *args, term, above, share, half, rows - half, (force_a, to_below), keep
+    other_a = swapped(force_a, "cols", 1) if paired == 2 else jnp.zeros_like(force_a)
+    other_a, to_below, keep, send_b, force_b = pull(
+        *args, term, above, share, half, rows - half, (other_a, to_below), keep
     )
+    force_a = force_a + other_a
     got_b = swapped(send_b, "layers", 1)
     from_above = shifted(to_below, "rows", -1)
 

time: 79.6 us -> 78.4 us (0.985)
  Pallas kernels: 45.3 us -> 44 us
    pallas_call x4, Pallas kernels: 5.97 us -> 3.85 us  [add_parts(): pl.pallas_call(functools.partial(add_kernel, steps), out_shape=jax.ShapeD...]
    ppermute x4, starting transfers between devices: 4.75 us -> 3.82 us  [swapped(): lax.ppermute(value, axis, [(source, source ^ bit) for source in range(cou...]
    pallas_call x1, Pallas kernels: 14.9 us -> 15.7 us  [push(): pl.pallas_call(kernel, out_shape=(jax.ShapeDtypeStruct((reach * share, co...]
    ppermute x4, starting transfers between devices: 7.54 us -> 8.36 us  [shifted(): return lax.ppermute(value, axis, pairs)]
    unnamed x12 -> x14, local copies, waits for them, and re-layouts: 4.42 us -> 4.65 us
  transfers between devices with their start and end apart: 8 -> 8, of which waited for: 3 -> 4; matrix products, arithmetic and copies ran while one was open for 4% -> 3% of each run, Pallas kernels for 56% -> 55%
where the time goes in v5:
time: 78.4 us; the launch traced here: 77.7 us
  Pallas kernels  44 us (56%)
  starting transfers between devices  12.2 us (16%)
  waiting for transfers between devices  7.33 us (9%)
  local copies, waits for them, and re-layouts  5.84 us (7%)
  blocking collectives  5.23 us (7%)
  other arithmetic  2.39 us (3%)
    pallas_call x2, Pallas kernels, pull(): pl.pallas_call(kernel, out_shape=tuple((jax.ShapeDtypeStruct(a.shape, a.d...  24.5 us
    pallas_call x1, Pallas kernels, push(): pl.pallas_call(kernel, out_shape=(jax.ShapeDtypeStruct((reach * share, co...  15.7 us
    ppermute x4, starting transfers between devices, shifted(): return lax.ppermute(value, axis, pairs)  8.36 us
    all_gather x1, blocking collectives, local(): gathered = lax.all_gather(forces, 'cols')  5.23 us
    unnamed x14, local copies, waits for them, and re-layouts  4.65 us
    ppermute x4, waiting for transfers between devices, shifted(): return lax.ppermute(value, axis, pairs)  4.03 us
    pallas_call x4, Pallas kernels, add_parts(): pl.pallas_call(functools.partial(add_kernel, steps), out_shape=jax.ShapeD...  3.85 us
    ppermute x4, starting transfers between devices, swapped(): lax.ppermute(value, axis, [(source, source ^ bit) for source in range(cou...  3.82 us
  transfers between devices with their start and end apart: 8, of which 4 were waited for; matrix products, arithmetic and copies ran while one was open for 3% of the time, Pallas kernels for 55%

profile of v5, /device:TPU:0, one launch (start us, length us, event | category | flops | bytes accessed | tf_op | source)
XLA Modules:
  0.0 77.7 jit_solution(3161990109492393996)
XLA Ops:
  0.6 1.2 %slice.12 = bf16[12,64,512]{2,1,0:T(8,128)(2,1)S(1)} slice(bf16[24,64,512]{2,1,0:T(8,128)(2,1)} %param.7), slice={[12:24], [0:64], [0:512]} | slice | bytes 1572864 | tf_op jit(solution)/shard_map/slice | solution.py:273
  1.8 3.1 %collective-permute-start.1 = (bf16[768,512]{1,0:T(8,128)(2,1)S(1)}, bf16[768,512]{1,0:T(8,128)(2,1)S(1)}, u32[]{:S(2)}, u32[]{:S(2)}) collective-permute-start(bf16[768,512]{1,0:T(8,128)(2,1)S(1)} %bitcast.28), channel_id=1, source_target_pairs={{0,8},{8,16},{16,24},{24,0},{1,9},{9,17},{17,25},{25,1},{2,10},{10... | collective-permute-start | bytes 2359304 | tf_op jit(solution)/shard_map/ppermute | solution.py:18
  4.9 15.7 %push_blocks.1 = (bf16[768,512]{1,0:T(8,128)(2,1)}, f32[1536,512]{1,0:T(8,128)}, bf16[768,512]{1,0:T(8,128)(2,1)}, bf16[768,512]{1,0:T(8,128)(2,1)}) custom-call(s32[24,25]{1,0:T(8,128)} %mask_ref.5, bf16[24,1600,128]{2,1,0:T(8,128)(2,1)} %bitcast.18, bf16[24,128,512]{2,1,0:T(8,128)(2,1)} %cot_ref.5, bf16[1536,512]{1,0:T(8,128)(2,1)} %bitcast.23), custom_call_target="tpu_custom_call" | custom-call | flops 5033164800 | bytes 9830400 | tf_op jit(solution)/shard_map/push_blocks/pallas_call | solution.py:84
  20.6 2.1 %collective-permute-start = (bf16[768,512]{1,0:T(8,128)(2,1)}, bf16[768,512]{1,0:T(8,128)(2,1)}, u32[]{:S(2)}, u32[]{:S(2)}) collective-permute-start(bf16[768,512]{1,0:T(8,128)(2,1)} %get-tuple-element.25), channel_id=1, source_target_pairs={{0,24},{8,0},{16,8},{24,16},{1,25},{9,1},{17,9},{25,17},{2,26},{10... | collective-permute-start | bytes 2359304 | tf_op jit(solution)/shard_map/ppermute | solution.py:18
  22.6 1.9 %collective-permute-done.1.head_ref = bf16[768,512]{1,0:T(8,128)(2,1)S(1)} collective-permute-done((bf16[768,512]{1,0:T(8,128)(2,1)S(1)}, bf16[768,512]{1,0:T(8,128)(2,1)S(1)}, u32[]{:S(2)}, u32[]{:S(2)}) %collective-permute-start.1) | collective-permute-done | bytes 786464 | tf_op jit(solution)/shard_map/ppermute | solution.py:18
  24.6 1.0 %copy-done.3 = bf16[768,512]{1,0:T(8,128)(2,1)} copy-done((bf16[768,512]{1,0:T(8,128)(2,1)}, bf16[768,512]{1,0:T(8,128)(2,1)S(1)}, u32[]{:S(2)}) %copy-start.3) | copy-done | bytes 786456
  25.5 12.2 %pull_blocks.2 = (bf16[768,512]{1,0:T(8,128)(2,1)}, f32[24,64,512]{2,1,0:T(8,128)}, bf16[12,64,512]{2,1,0:T(8,128)(2,1)}, f32[12,1,128]{2,1,0:T(1,128)}) custom-call(s32[24,25]{1,0:T(8,128)} %mask_ref.5, s32[1]{0:T(128)} %bitcast.side_ref, bf16[24,1600,128]{2,1,0:T(8,128)(2,1)} %bitcast.19, ...), custom_call_target="tpu_custom_call", output_to_operand_aliasing={{0}: (8, {})} | custom-call | flops 5033164800 | bytes 9830400 | tf_op jit(solution)/shard_map/pull_blocks/pallas_call | solution.py:171
  37.8 0.1 collective-permute-start.2
  37.9 0.1 collective-permute-start.6
  37.9 1.6 %collective-permute-start.7 = (bf16[12,64,512]{2,1,0:T(8,128)(2,1)}, bf16[12,64,512]{2,1,0:T(8,128)(2,1)S(1)}, u32[]{:S(2)}, u32[]{:S(2)}) collective-permute-start(bf16[12,64,512]{2,1,0:T(8,128)(2,1)} %get-tuple-element.37), channel_id=1, source_target_pairs={{0,1},{1,0},{2,3},{3,2},{4,5},{5,4},{6,7},{7,6},{8,9},{9,8},{10,11... | collective-permute-start | bytes 2359304 | tf_op jit(solution)/shard_map/ppermute | solution.py:23
  39.5 1.9 %collective-permute-done.tail_ref = bf16[768,512]{1,0:T(8,128)(2,1)} collective-permute-done((bf16[768,512]{1,0:T(8,128)(2,1)}, bf16[768,512]{1,0:T(8,128)(2,1)}, u32[]{:S(2)}, u32[]{:S(2)}) %collective-permute-start) | collective-permute-done | bytes 786464 | tf_op jit(solution)/shard_map/ppermute | solution.py:18
  41.4 0.6 copy-done.4
  42.0 12.3 %pull_blocks.3 = (f32[12,1,128]{2,1,0:T(1,128)}, bf16[768,512]{1,0:T(8,128)(2,1)}, f32[24,64,512]{2,1,0:T(8,128)}, bf16[12,64,512]{2,1,0:T(8,128)(2,1)}, f32[12,1,128]{2,1,0:T(1,128)}) custom-call(s32[24,25]{1,0:T(8,128)} %mask_ref.5, s32[1]{0:T(128)} %bitcast.side_ref, ...), custom_call_target="tpu_custom_call", output_to_operand_aliasing={{0}: (8, {}), {1}: (9, {}), {2}: (10, {})} | custom-call | flops 5033164800 | bytes 9830400 | tf_op jit(solution)/shard_map/pull_blocks/pallas_call | solution.py:171
  54.3 1.6 %collective-permute-start.5 = (bf16[12,64,512]{2,1,0:T(8,128)(2,1)}, bf16[12,64,512]{2,1,0:T(8,128)(2,1)S(1)}, u32[]{:S(2)}, u32[]{:S(2)}) collective-permute-start(bf16[12,64,512]{2,1,0:T(8,128)(2,1)} %get-tuple-element.34), channel_id=1, source_target_pairs={{0,1},{1,0},{2,3},{3,2},{4,5},{5,4},{6,7},{7,6},{8,9},{9,8},{10,11... | collective-permute-start | bytes 2359304 | tf_op jit(solution)/shard_map/ppermute | solution.py:23
  55.9 0.7 add.6
  56.6 3.2 %collective-permute-start.3 = (bf16[768,512]{1,0:T(8,128)(2,1)}, bf16[768,512]{1,0:T(8,128)(2,1)S(1)}, u32[]{:S(2)}, u32[]{:S(2)}) collective-permute-start(bf16[768,512]{1,0:T(8,128)(2,1)} %get-tuple-element.30), channel_id=1, source_target_pairs={{0,24},{8,0},{16,8},{24,16},{1,25},{9,1},{17,9},{25,17},{2,26},{10... | collective-permute-start | bytes 2359304 | tf_op jit(solution)/shard_map/ppermute | solution.py:18
  59.7 0.7 pad_maximum_fusion
  60.5 0.4 select_reduce_fusion
  60.8 5.2 %all-gather = f32[96,64]{1,0:T(8,128)S(1)} all-gather(f32[24,64]{1,0:T(8,128)S(1)} %select_reduce_fusion), channel_id=2, replica_groups=mesh['rows'=4,'cols'=4,'layers'=2] {'cols'}, dimensions={0}, use_global_device_ids=true | all-gather | bytes 30720 | tf_op jit(solution)/shard_map/all_gather | solution.py:294
  66.1 0.6 collective-permute-start.4
  66.7 0.0 collective-permute-done.7
  66.7 1.9 %copy-done = f32[24,64,512]{2,1,0:T(8,128)S(1)} copy-done((f32[24,64,512]{2,1,0:T(8,128)S(1)}, f32[24,64,512]{2,1,0:T(8,128)}, u32[]{:S(2)}) %copy-start) | copy-done | bytes 3145752
  68.6 1.0 %add_parts.4.rest_0_ = bf16[1536,512]{1,0:T(8,128)(2,1)} custom-call(f32[1536,512]{1,0:T(8,128)S(1)} %bitcast.12, bf16[768,512]{1,0:T(8,128)(2,1)S(1)} %bitcast.14, bf16[768,512]{1,0:T(8,128)(2,1)S(1)} %bitcast.15), custom_call_target="tpu_custom_call" | custom-call | tf_op jit(solution)/shard_map/add_parts/pallas_call | solution.py:246
  69.5 0.0 collective-permute-done.6.first_ref.second_ref
  69.5 1.2 %copy-done.2 = f32[1536,512]{1,0:T(8,128)S(1)} copy-done((f32[1536,512]{1,0:T(8,128)S(1)}, f32[1536,512]{1,0:T(8,128)}, u32[]{:S(2)}) %copy-start.2) | copy-done | bytes 3145752
  70.7 1.0 %add_parts.5.rest_0_ = bf16[1536,512]{1,0:T(8,128)(2,1)} custom-call(f32[1536,512]{1,0:T(8,128)S(1)} %copy-done.2, bf16[768,512]{1,0:T(8,128)(2,1)S(1)} %collective-permute-done.6.first_ref.second_ref, bf16[768,512]{1,0:T(8,128)(2,1)S(1)} %collective-permute-done.6.first_ref.second_ref), custom_call_target="tpu_custom_call" | custom-call | tf_op jit(solution)/shard_map/add_parts/pallas_call | solution.py:246
  71.7 3.3 %collective-permute-done.5 = bf16[12,64,512]{2,1,0:T(8,128)(2,1)S(1)} collective-permute-done((bf16[12,64,512]{2,1,0:T(8,128)(2,1)}, bf16[12,64,512]{2,1,0:T(8,128)(2,1)S(1)}, u32[]{:S(2)}, u32[]{:S(2)}) %collective-permute-start.5) | collective-permute-done | bytes 786464 | tf_op jit(solution)/shard_map/ppermute | solution.py:23
  75.0 0.9 %add_parts.6 = bf16[1536,512]{1,0:T(8,128)(2,1)} custom-call(f32[1536,512]{1,0:T(8,128)S(1)} %bitcast.13, bf16[768,512]{1,0:T(8,128)(2,1)S(1)} %bitcast.16, bf16[768,512]{1,0:T(8,128)(2,1)S(1)} %bitcast.17, bf16[1536,512]{1,0:T(8,128)(2,1)} %add_parts.4.rest_0_), custom_call_target="tpu_custom_call", output_to_operand_aliasing={{}: (3, {})} | custom-call | tf_op jit(solution)/shard_map/add_parts/pallas_call | solution.py:246
  75.9 0.0 collective-permute-done.4
  75.9 0.6 fusion
  76.6 0.2 collective-permute-done.3.first_ref.second_ref
  76.7 0.9 %add_parts.7 = bf16[1536,512]{1,0:T(8,128)(2,1)} custom-call(f32[1536,512]{1,0:T(8,128)S(1)} %copy-done.2, bf16[768,512]{1,0:T(8,128)(2,1)S(1)} %collective-permute-done.3.first_ref.second_ref, bf16[768,512]{1,0:T(8,128)(2,1)S(1)} %collective-permute-done.3.first_ref.second_ref, bf16[1536,512]{1,0:T(8,128)(2,1)} %add_parts.5.rest_0_), custom_call_target="tpu_custom_call", output_to_operand_aliasing={{}: (3, {})} | custom-call | tf_op jit(solution)/shard_map/add_parts/pallas_call | solution.py:246
  (14 shorter events, 0.0 us)
Async XLA Ops:
  1.8 22.8 %collective-permute-start.1 = (bf16[768,512]{1,0:T(8,128)(2,1)S(1)}, bf16[768,512]{1,0:T(8,128)(2,1)S(1)}, u32[]{:S(2)}, u32[]{:S(2)}) collective-permute-start(bf16[768,512]{1,0:T(8,128)(2,1)S(1)} %bitcast.28), channel_id=1, source_target_pairs={{0,8},{8,16},{16,24},{24,0},{1,9},{9,17},{17,25},{25,1},{2,10},{10... | collective-permute-start | bytes 2359304 | tf_op jit(solution)/shard_map/ppermute | solution.py:18
  20.6 20.8 %collective-permute-start = (bf16[768,512]{1,0:T(8,128)(2,1)}, bf16[768,512]{1,0:T(8,128)(2,1)}, u32[]{:S(2)}, u32[]{:S(2)}) collective-permute-start(bf16[768,512]{1,0:T(8,128)(2,1)} %get-tuple-element.25), channel_id=1, source_target_pairs={{0,24},{8,0},{16,8},{24,16},{1,25},{9,1},{17,9},{25,17},{2,26},{10... | collective-permute-start | bytes 2359304 | tf_op jit(solution)/shard_map/ppermute | solution.py:18
  24.6 1.0 %copy-start.3 = (bf16[768,512]{1,0:T(8,128)(2,1)}, bf16[768,512]{1,0:T(8,128)(2,1)S(1)}, u32[]{:S(2)}) copy-start(bf16[768,512]{1,0:T(8,128)(2,1)S(1)} %collective-permute-done.1.head_ref) | copy-start | bytes 2359300
  37.8 3.6 %collective-permute-start.2 = (f32[12,1,128]{2,1,0:T(1,128)}, f32[12,1,128]{2,1,0:T(1,128)S(1)}, u32[]{:S(2)}, u32[]{:S(2)}) collective-permute-start(f32[12,1,128]{2,1,0:T(1,128)} %get-tuple-element.27), channel_id=1, source_target_pairs={{0,2},{2,0},{4,6},{6,4},{1,3},{3,1},{5,7},{7,5},{8,10},{10,8},{12,... | collective-permute-start | bytes 18440 | tf_op jit(solution)/shard_map/ppermute | solution.py:23
  37.9 31.7 %collective-permute-start.6 = (bf16[768,512]{1,0:T(8,128)(2,1)}, bf16[768,512]{1,0:T(8,128)(2,1)S(1)}, u32[]{:S(2)}, u32[]{:S(2)}) collective-permute-start(bf16[768,512]{1,0:T(8,128)(2,1)} %get-tuple-element.36), channel_id=1, source_target_pairs={{0,8},{8,16},{16,24},{24,0},{1,9},{9,17},{17,25},{25,1},{2,10},{10... | collective-permute-start | bytes 2359304 | tf_op jit(solution)/shard_map/ppermute | solution.py:18
  37.9 28.7 %collective-permute-start.7 = (bf16[12,64,512]{2,1,0:T(8,128)(2,1)}, bf16[12,64,512]{2,1,0:T(8,128)(2,1)S(1)}, u32[]{:S(2)}, u32[]{:S(2)}) collective-permute-start(bf16[12,64,512]{2,1,0:T(8,128)(2,1)} %get-tuple-element.37), channel_id=1, source_target_pairs={{0,1},{1,0},{2,3},{3,2},{4,5},{5,4},{6,7},{7,6},{8,9},{9,8},{10,11... | collective-permute-start | bytes 2359304 | tf_op jit(solution)/shard_map/ppermute | solution.py:23
  41.4 0.6 copy-start.4
  42.0 13.8 %copy-start.6 = (f32[12,1,128]{2,1,0:T(1,128)S(1)}, f32[12,1,128]{2,1,0:T(1,128)}, u32[]{:S(2)}) copy-start(f32[12,1,128]{2,1,0:T(1,128)} %get-tuple-element.27) | copy-start | bytes 18436
  42.0 18.4 %copy-start.5 = (s32[24,128]{1,0:T(8,128)S(1)}, s32[24,128]{1,0:T(8,128)}, u32[]{:S(2)}) copy-start(s32[24,128]{1,0:T(8,128)} %param.13) | copy-start | bytes 36868
  54.3 20.7 %collective-permute-start.5 = (bf16[12,64,512]{2,1,0:T(8,128)(2,1)}, bf16[12,64,512]{2,1,0:T(8,128)(2,1)S(1)}, u32[]{:S(2)}, u32[]{:S(2)}) collective-permute-start(bf16[12,64,512]{2,1,0:T(8,128)(2,1)} %get-tuple-element.34), channel_id=1, source_target_pairs={{0,1},{1,0},{2,3},{3,2},{4,5},{5,4},{6,7},{7,6},{8,9},{9,8},{10,11... | collective-permute-start | bytes 2359304 | tf_op jit(solution)/shard_map/ppermute | solution.py:23
  56.6 20.2 %collective-permute-start.3 = (bf16[768,512]{1,0:T(8,128)(2,1)}, bf16[768,512]{1,0:T(8,128)(2,1)S(1)}, u32[]{:S(2)}, u32[]{:S(2)}) collective-permute-start(bf16[768,512]{1,0:T(8,128)(2,1)} %get-tuple-element.30), channel_id=1, source_target_pairs={{0,24},{8,0},{16,8},{24,16},{1,25},{9,1},{17,9},{25,17},{2,26},{10... | collective-permute-start | bytes 2359304 | tf_op jit(solution)/shard_map/ppermute | solution.py:18
  66.1 9.9 %collective-permute-start.4 = (f32[24,64]{1,0:T(8,128)S(1)}, f32[24,64]{1,0:T(8,128)S(1)}, u32[]{:S(2)}, u32[]{:S(2)}) collective-permute-start(f32[24,64]{1,0:T(8,128)S(1)} %pad_maximum_fusion.1), channel_id=1, source_target_pairs={{0,1},{1,0},{2,3},{3,2},{4,5},{5,4},{6,7},{7,6},{8,9},{9,8},{10,11... | collective-permute-start | bytes 18440 | tf_op jit(solution)/shard_map/ppermute | solution.py:23
  66.7 1.9 %copy-start = (f32[24,64,512]{2,1,0:T(8,128)S(1)}, f32[24,64,512]{2,1,0:T(8,128)}, u32[]{:S(2)}) copy-start(f32[24,64,512]{2,1,0:T(8,128)} %get-tuple-element.33) | copy-start | bytes 9437188
  68.5 2.2 %copy-start.2 = (f32[1536,512]{1,0:T(8,128)S(1)}, f32[1536,512]{1,0:T(8,128)}, u32[]{:S(2)}) copy-start(f32[1536,512]{1,0:T(8,128)} %get-tuple-element.35.own_ref) | copy-start | bytes 9437188
  70.7 4.3 %copy-start.1 = (f32[24,64,512]{2,1,0:T(8,128)S(1)}, f32[24,64,512]{2,1,0:T(8,128)}, u32[]{:S(2)}) copy-start(f32[24,64,512]{2,1,0:T(8,128)} %get-tuple-element.33) | copy-start | bytes 9437188

commit v6 on v5

--- a/solution.py
+++ b/solution.py
@@ -9,6 +9,7 @@
 
 APB = 64
 VMEM_BYTES = 62 * 1024 * 1024
+PULL_VMEM_BYTES = 51 * 1024 * 1024
 ARBITRARY = pltpu.GridDimensionSemantics.ARBITRARY
 
 
@@ -202,7 +203,7 @@
         ),
         input_output_aliases=aliases,
         compiler_params=pltpu.CompilerParams(
-            dimension_semantics=(ARBITRARY,), vmem_limit_bytes=VMEM_BYTES
+            dimension_semantics=(ARBITRARY,), vmem_limit_bytes=PULL_VMEM_BYTES
         ),
         cost_estimate=pl.CostEstimate(
             flops=flops, bytes_accessed=4 * rows * depth * orbitals, transcendentals=0

time: 78.4 us -> 77.2 us (0.985)
  waiting for transfers between devices: 7.33 us -> 9.04 us
  local copies, waits for them, and re-layouts: 5.84 us -> 4.28 us
  other arithmetic: 2.39 us -> 1.01 us
    unnamed x14 -> x12, local copies, waits for them, and re-layouts: 4.65 us -> 3.09 us
    ppermute x4, waiting for transfers between devices: 4.03 us -> 5.55 us  [shifted(): return lax.ppermute(value, axis, pairs)]
    ppermute x4, starting transfers between devices: 8.36 us -> 9.29 us  [shifted(): return lax.ppermute(value, axis, pairs)]
  transfers between devices with their start and end apart: 8 -> 8, of which waited for: 4 -> 4; matrix products, arithmetic and copies ran while one was open for 3% -> 1% of each run, Pallas kernels for 55% -> 56%
where the time goes in v6:
time: 77.2 us; the launch traced here: 76.7 us
  Pallas kernels  43.7 us (57%)
  starting transfers between devices  12.7 us (16%)
  waiting for transfers between devices  9.04 us (12%)
  blocking collectives  5.23 us (7%)
  local copies, waits for them, and re-layouts  4.28 us (6%)
  other arithmetic  1.01 us (1%)
    pallas_call x2, Pallas kernels, pull(): pl.pallas_call(kernel, out_shape=tuple((jax.ShapeDtypeStruct(a.shape, a.d...  24.1 us
    pallas_call x1, Pallas kernels, push(): pl.pallas_call(kernel, out_shape=(jax.ShapeDtypeStruct((reach * share, co...  15.8 us
    ppermute x4, starting transfers between devices, shifted(): return lax.ppermute(value, axis, pairs)  9.29 us
    ppermute x4, waiting for transfers between devices, shifted(): return lax.ppermute(value, axis, pairs)  5.55 us
    all_gather x1, blocking collectives, local(): gathered = lax.all_gather(forces, 'cols')  5.23 us
    pallas_call x4, Pallas kernels, add_parts(): pl.pallas_call(functools.partial(add_kernel, steps), out_shape=jax.ShapeD...  3.85 us
    ppermute x4, waiting for transfers between devices, swapped(): lax.ppermute(value, axis, [(source, source ^ bit) for source in range(cou...  3.49 us
    ppermute x4, starting transfers between devices, swapped(): lax.ppermute(value, axis, [(source, source ^ bit) for source in range(cou...  3.43 us
  transfers between devices with their start and end apart: 8, of which 4 were waited for; matrix products, arithmetic and copies ran while one was open for 1% of the time, Pallas kernels for 56%

profile of v6, /device:TPU:0, one launch (start us, length us, event | category | flops | bytes accessed | tf_op | source)
XLA Modules:
  0.0 76.7 jit_solution(10046122448514575112)
XLA Ops:
  0.6 1.2 %slice.12 = bf16[12,64,512]{2,1,0:T(8,128)(2,1)S(1)} slice(bf16[24,64,512]{2,1,0:T(8,128)(2,1)} %param.7), slice={[12:24], [0:64], [0:512]} | slice | bytes 1572864 | tf_op jit(solution)/shard_map/slice | solution.py:274
  1.8 3.1 %collective-permute-start.1 = (bf16[768,512]{1,0:T(8,128)(2,1)S(1)}, bf16[768,512]{1,0:T(8,128)(2,1)S(1)}, u32[]{:S(2)}, u32[]{:S(2)}) collective-permute-start(bf16[768,512]{1,0:T(8,128)(2,1)S(1)} %bitcast.28), channel_id=1, source_target_pairs={{0,8},{8,16},{16,24},{24,0},{1,9},{9,17},{17,25},{25,1},{2,10},{10... | collective-permute-start | bytes 2359304 | tf_op jit(solution)/shard_map/ppermute | solution.py:19
  4.9 15.8 %push_blocks.1 = (bf16[768,512]{1,0:T(8,128)(2,1)}, f32[1536,512]{1,0:T(8,128)}, bf16[768,512]{1,0:T(8,128)(2,1)}, bf16[768,512]{1,0:T(8,128)(2,1)}) custom-call(s32[24,25]{1,0:T(8,128)} %mask_ref.5, bf16[24,1600,128]{2,1,0:T(8,128)(2,1)} %bitcast.18, bf16[24,128,512]{2,1,0:T(8,128)(2,1)} %cot_ref.5, bf16[1536,512]{1,0:T(8,128)(2,1)} %bitcast.23), custom_call_target="tpu_custom_call" | custom-call | flops 5033164800 | bytes 9830400 | tf_op jit(solution)/shard_map/push_blocks/pallas_call | solution.py:85
  20.7 2.0 %collective-permute-start = (bf16[768,512]{1,0:T(8,128)(2,1)}, bf16[768,512]{1,0:T(8,128)(2,1)S(1)}, u32[]{:S(2)}, u32[]{:S(2)}) collective-permute-start(bf16[768,512]{1,0:T(8,128)(2,1)} %get-tuple-element.25), channel_id=1, source_target_pairs={{0,24},{8,0},{16,8},{24,16},{1,25},{9,1},{17,9},{25,17},{2,26},{10... | collective-permute-start | bytes 2359304 | tf_op jit(solution)/shard_map/ppermute | solution.py:19
  22.7 1.8 %collective-permute-done.1.head_ref = bf16[768,512]{1,0:T(8,128)(2,1)S(1)} collective-permute-done((bf16[768,512]{1,0:T(8,128)(2,1)S(1)}, bf16[768,512]{1,0:T(8,128)(2,1)S(1)}, u32[]{:S(2)}, u32[]{:S(2)}) %collective-permute-start.1) | collective-permute-done | bytes 786464 | tf_op jit(solution)/shard_map/ppermute | solution.py:19
  24.6 0.0 copy-done.4
  24.6 12.0 %pull_blocks.2 = (bf16[768,512]{1,0:T(8,128)(2,1)}, f32[24,64,512]{2,1,0:T(8,128)}, bf16[12,64,512]{2,1,0:T(8,128)(2,1)S(1)}, f32[12,1,128]{2,1,0:T(1,128)S(1)}) custom-call(s32[24,25]{1,0:T(8,128)S(1)} %copy-done.4, s32[1]{0:T(128)} %bitcast.side_ref, bf16[24,1600,128]{2,1,0:T(8,128)(2,1)} %bitcast.19, ...), custom_call_target="tpu_custom_call", output_to_operand_aliasing={{0}: (8, {})} | custom-call | flops 5033164800 | bytes 9830400 | tf_op jit(solution)/shard_map/pull_blocks/pallas_call | solution.py:172
  36.6 0.0 collective-permute-start.2
  36.6 0.0 collective-permute-start.6
  36.6 1.6 %collective-permute-start.7 = (bf16[12,64,512]{2,1,0:T(8,128)(2,1)S(1)}, bf16[12,64,512]{2,1,0:T(8,128)(2,1)S(1)}, u32[]{:S(2)}, u32[]{:S(2)}) collective-permute-start(bf16[12,64,512]{2,1,0:T(8,128)(2,1)S(1)} %get-tuple-element.37), channel_id=1, source_target_pairs={{0,1},{1,0},{2,3},{3,2},{4,5},{5,4},{6,7},{7,6},{8,9},{9,8},{10,11... | collective-permute-start | bytes 2359304 | tf_op jit(solution)/shard_map/ppermute | solution.py:24
  38.2 3.1 %collective-permute-done.tail_ref = bf16[768,512]{1,0:T(8,128)(2,1)S(1)} collective-permute-done((bf16[768,512]{1,0:T(8,128)(2,1)}, bf16[768,512]{1,0:T(8,128)(2,1)S(1)}, u32[]{:S(2)}, u32[]{:S(2)}) %collective-permute-start) | collective-permute-done | bytes 786464 | tf_op jit(solution)/shard_map/ppermute | solution.py:19
  41.3 0.0 collective-permute-done.2.rest_0_
  41.3 0.0 copy-done.3
  41.3 12.0 %pull_blocks.3 = (f32[12,1,128]{2,1,0:T(1,128)S(1)}, bf16[768,512]{1,0:T(8,128)(2,1)S(1)}, f32[24,64,512]{2,1,0:T(8,128)}, bf16[12,64,512]{2,1,0:T(8,128)(2,1)S(1)}, f32[12,1,128]{2,1,0:T(1,128)S(1)}) custom-call(s32[24,25]{1,0:T(8,128)S(1)} %copy-done.4, s32[1]{0:T(128)} %bitcast.side_ref, ...), custom_call_target="tpu_custom_call", output_to_operand_aliasing={{0}: (8, {}), {1}: (9, {}), {2}: (10, {})} | custom-call | flops 5033164800 | bytes 9830400 | tf_op jit(solution)/shard_map/pull_blocks/pallas_call | solution.py:172
  53.3 1.5 %collective-permute-start.5 = (bf16[12,64,512]{2,1,0:T(8,128)(2,1)S(1)}, bf16[12,64,512]{2,1,0:T(8,128)(2,1)S(1)}, u32[]{:S(2)}, u32[]{:S(2)}) collective-permute-start(bf16[12,64,512]{2,1,0:T(8,128)(2,1)S(1)} %get-tuple-element.34), channel_id=1, source_target_pairs={{0,1},{1,0},{2,3},{3,2},{4,5},{5,4},{6,7},{7,6},{8,9},{9,8},{10,11... | collective-permute-start | bytes 2359304 | tf_op jit(solution)/shard_map/ppermute | solution.py:24
  54.9 4.2 %collective-permute-start.3 = (bf16[768,512]{1,0:T(8,128)(2,1)S(1)}, bf16[768,512]{1,0:T(8,128)(2,1)S(1)}, u32[]{:S(2)}, u32[]{:S(2)}) collective-permute-start(bf16[768,512]{1,0:T(8,128)(2,1)S(1)} %get-tuple-element.30), channel_id=1, source_target_pairs={{0,24},{8,0},{16,8},{24,16},{1,25},{9,1},{17,9},{25,17},{2,26},{10... | collective-permute-start | bytes 2359304 | tf_op jit(solution)/shard_map/ppermute | solution.py:19
  59.1 0.0 copy-done.5
  59.1 0.4 select_reduce_fusion
  59.4 5.2 %all-gather = f32[96,64]{1,0:T(8,128)S(1)} all-gather(f32[24,64]{1,0:T(8,128)S(1)} %select_reduce_fusion), channel_id=2, replica_groups=mesh['rows'=4,'cols'=4,'layers'=2] {'cols'}, dimensions={0}, use_global_device_ids=true | all-gather | bytes 30720 | tf_op jit(solution)/shard_map/all_gather | solution.py:295
  64.7 0.3 collective-permute-start.4
  65.0 0.0 collective-permute-done.7
  65.0 1.9 %copy-done = f32[24,64,512]{2,1,0:T(8,128)S(1)} copy-done((f32[24,64,512]{2,1,0:T(8,128)S(1)}, f32[24,64,512]{2,1,0:T(8,128)}, u32[]{:S(2)}) %copy-start) | copy-done | bytes 3145752
  66.9 1.0 %add_parts.4.rest_0_ = bf16[1536,512]{1,0:T(8,128)(2,1)} custom-call(f32[1536,512]{1,0:T(8,128)S(1)} %bitcast.12, bf16[768,512]{1,0:T(8,128)(2,1)S(1)} %bitcast.14, bf16[768,512]{1,0:T(8,128)(2,1)S(1)} %bitcast.15), custom_call_target="tpu_custom_call" | custom-call | tf_op jit(solution)/shard_map/add_parts/pallas_call | solution.py:247
  67.9 0.0 collective-permute-done.6.first_ref.second_ref
  67.9 1.2 %copy-done.2 = f32[1536,512]{1,0:T(8,128)S(1)} copy-done((f32[1536,512]{1,0:T(8,128)S(1)}, f32[1536,512]{1,0:T(8,128)}, u32[]{:S(2)}) %copy-start.2) | copy-done | bytes 3145752
  69.1 1.0 %add_parts.5.rest_0_ = bf16[1536,512]{1,0:T(8,128)(2,1)} custom-call(f32[1536,512]{1,0:T(8,128)S(1)} %copy-done.2, bf16[768,512]{1,0:T(8,128)(2,1)S(1)} %collective-permute-done.6.first_ref.second_ref, bf16[768,512]{1,0:T(8,128)(2,1)S(1)} %collective-permute-done.6.first_ref.second_ref), custom_call_target="tpu_custom_call" | custom-call | tf_op jit(solution)/shard_map/add_parts/pallas_call | solution.py:247
  70.1 3.5 %collective-permute-done.5 = bf16[12,64,512]{2,1,0:T(8,128)(2,1)S(1)} collective-permute-done((bf16[12,64,512]{2,1,0:T(8,128)(2,1)S(1)}, bf16[12,64,512]{2,1,0:T(8,128)(2,1)S(1)}, u32[]{:S(2)}, u32[]{:S(2)}) %collective-permute-start.5) | collective-permute-done | bytes 786464 | tf_op jit(solution)/shard_map/ppermute | solution.py:24
  73.6 0.9 %add_parts.6 = bf16[1536,512]{1,0:T(8,128)(2,1)} custom-call(f32[1536,512]{1,0:T(8,128)S(1)} %bitcast.13, bf16[768,512]{1,0:T(8,128)(2,1)S(1)} %bitcast.16, bf16[768,512]{1,0:T(8,128)(2,1)S(1)} %bitcast.17, bf16[1536,512]{1,0:T(8,128)(2,1)} %add_parts.4.rest_0_), custom_call_target="tpu_custom_call", output_to_operand_aliasing={{}: (3, {})} | custom-call | tf_op jit(solution)/shard_map/add_parts/pallas_call | solution.py:247
  74.5 0.0 collective-permute-done.4
  74.5 0.6 fusion
  75.1 0.6 collective-permute-done.3.first_ref.second_ref
  75.8 0.9 %add_parts.7 = bf16[1536,512]{1,0:T(8,128)(2,1)} custom-call(f32[1536,512]{1,0:T(8,128)S(1)} %copy-done.2, bf16[768,512]{1,0:T(8,128)(2,1)S(1)} %collective-permute-done.3.first_ref.second_ref, bf16[768,512]{1,0:T(8,128)(2,1)S(1)} %collective-permute-done.3.first_ref.second_ref, bf16[1536,512]{1,0:T(8,128)(2,1)} %add_parts.5.rest_0_), custom_call_target="tpu_custom_call", output_to_operand_aliasing={{}: (3, {})} | custom-call | tf_op jit(solution)/shard_map/add_parts/pallas_call | solution.py:247
  (12 shorter events, 0.1 us)
Async XLA Ops:
  1.8 22.7 %collective-permute-start.1 = (bf16[768,512]{1,0:T(8,128)(2,1)S(1)}, bf16[768,512]{1,0:T(8,128)(2,1)S(1)}, u32[]{:S(2)}, u32[]{:S(2)}) collective-permute-start(bf16[768,512]{1,0:T(8,128)(2,1)S(1)} %bitcast.28), channel_id=1, source_target_pairs={{0,8},{8,16},{16,24},{24,0},{1,9},{9,17},{17,25},{25,1},{2,10},{10... | collective-permute-start | bytes 2359304 | tf_op jit(solution)/shard_map/ppermute | solution.py:19
  4.9 19.7 %copy-start.4 = (s32[24,25]{1,0:T(8,128)S(1)}, s32[24,25]{1,0:T(8,128)}, u32[]{:S(2)}) copy-start(s32[24,25]{1,0:T(8,128)} %mask_ref.5) | copy-start | bytes 7204
  20.7 20.6 %collective-permute-start = (bf16[768,512]{1,0:T(8,128)(2,1)}, bf16[768,512]{1,0:T(8,128)(2,1)S(1)}, u32[]{:S(2)}, u32[]{:S(2)}) collective-permute-start(bf16[768,512]{1,0:T(8,128)(2,1)} %get-tuple-element.25), channel_id=1, source_target_pairs={{0,24},{8,0},{16,8},{24,16},{1,25},{9,1},{17,9},{25,17},{2,26},{10... | collective-permute-start | bytes 2359304 | tf_op jit(solution)/shard_map/ppermute | solution.py:19
  24.6 16.8 %copy-start.3 = (bf16[768,512]{1,0:T(8,128)(2,1)S(1)}, bf16[768,512]{1,0:T(8,128)(2,1)}, u32[]{:S(2)}) copy-start(bf16[768,512]{1,0:T(8,128)(2,1)} %get-tuple-element.28.rest_1_) | copy-start | bytes 2359300
  36.6 4.7 %collective-permute-start.2 = (f32[12,1,128]{2,1,0:T(1,128)S(1)}, f32[12,1,128]{2,1,0:T(1,128)S(1)}, u32[]{:S(2)}, u32[]{:S(2)}) collective-permute-start(f32[12,1,128]{2,1,0:T(1,128)S(1)} %get-tuple-element.27), channel_id=1, source_target_pairs={{0,2},{2,0},{4,6},{6,4},{1,3},{3,1},{5,7},{7,5},{8,10},{10,8},{12,... | collective-permute-start | bytes 18440 | tf_op jit(solution)/shard_map/ppermute | solution.py:24
  36.6 31.3 %collective-permute-start.6 = (bf16[768,512]{1,0:T(8,128)(2,1)}, bf16[768,512]{1,0:T(8,128)(2,1)S(1)}, u32[]{:S(2)}, u32[]{:S(2)}) collective-permute-start(bf16[768,512]{1,0:T(8,128)(2,1)} %get-tuple-element.36), channel_id=1, source_target_pairs={{0,8},{8,16},{16,24},{24,0},{1,9},{9,17},{17,25},{25,1},{2,10},{10... | collective-permute-start | bytes 2359304 | tf_op jit(solution)/shard_map/ppermute | solution.py:19
  36.6 28.4 %collective-permute-start.7 = (bf16[12,64,512]{2,1,0:T(8,128)(2,1)S(1)}, bf16[12,64,512]{2,1,0:T(8,128)(2,1)S(1)}, u32[]{:S(2)}, u32[]{:S(2)}) collective-permute-start(bf16[12,64,512]{2,1,0:T(8,128)(2,1)S(1)} %get-tuple-element.37), channel_id=1, source_target_pairs={{0,1},{1,0},{2,3},{3,2},{4,5},{5,4},{6,7},{7,6},{8,9},{9,8},{10,11... | collective-permute-start | bytes 2359304 | tf_op jit(solution)/shard_map/ppermute | solution.py:24
  41.3 17.8 %copy-start.5 = (s32[24,128]{1,0:T(8,128)S(1)}, s32[24,128]{1,0:T(8,128)}, u32[]{:S(2)}) copy-start(s32[24,128]{1,0:T(8,128)} %param.13) | copy-start | bytes 36868
  53.3 20.2 %collective-permute-start.5 = (bf16[12,64,512]{2,1,0:T(8,128)(2,1)S(1)}, bf16[12,64,512]{2,1,0:T(8,128)(2,1)S(1)}, u32[]{:S(2)}, u32[]{:S(2)}) collective-permute-start(bf16[12,64,512]{2,1,0:T(8,128)(2,1)S(1)} %get-tuple-element.34), channel_id=1, source_target_pairs={{0,1},{1,0},{2,3},{3,2},{4,5},{5,4},{6,7},{7,6},{8,9},{9,8},{10,11... | collective-permute-start | bytes 2359304 | tf_op jit(solution)/shard_map/ppermute | solution.py:24
  54.9 20.9 %collective-permute-start.3 = (bf16[768,512]{1,0:T(8,128)(2,1)S(1)}, bf16[768,512]{1,0:T(8,128)(2,1)S(1)}, u32[]{:S(2)}, u32[]{:S(2)}) collective-permute-start(bf16[768,512]{1,0:T(8,128)(2,1)S(1)} %get-tuple-element.30), channel_id=1, source_target_pairs={{0,24},{8,0},{16,8},{24,16},{1,25},{9,1},{17,9},{25,17},{2,26},{10... | collective-permute-start | bytes 2359304 | tf_op jit(solution)/shard_map/ppermute | solution.py:19
  64.7 9.8 %collective-permute-start.4 = (f32[24,64]{1,0:T(8,128)S(1)}, f32[24,64]{1,0:T(8,128)S(1)}, u32[]{:S(2)}, u32[]{:S(2)}) collective-permute-start(f32[24,64]{1,0:T(8,128)S(1)} %pad_maximum_fusion.1), channel_id=1, source_target_pairs={{0,1},{1,0},{2,3},{3,2},{4,5},{5,4},{6,7},{7,6},{8,9},{9,8},{10,11... | collective-permute-start | bytes 18440 | tf_op jit(solution)/shard_map/ppermute | solution.py:24
  65.0 1.9 %copy-start = (f32[24,64,512]{2,1,0:T(8,128)S(1)}, f32[24,64,512]{2,1,0:T(8,128)}, u32[]{:S(2)}) copy-start(f32[24,64,512]{2,1,0:T(8,128)} %get-tuple-element.33) | copy-start | bytes 9437188
  66.9 2.2 %copy-start.2 = (f32[1536,512]{1,0:T(8,128)S(1)}, f32[1536,512]{1,0:T(8,128)}, u32[]{:S(2)}) copy-start(f32[1536,512]{1,0:T(8,128)} %get-tuple-element.35.own_ref) | copy-start | bytes 9437188
  69.1 4.5 %copy-start.1 = (f32[24,64,512]{2,1,0:T(8,128)S(1)}, f32[24,64,512]{2,1,0:T(8,128)}, u32[]{:S(2)}) copy-start(f32[24,64,512]{2,1,0:T(8,128)} %get-tuple-element.33) | copy-start | bytes 9437188

commit v7 on v6

--- a/solution.py
+++ b/solution.py
@@ -139,10 +139,13 @@
             both[k, span, :orbitals] = jnp.where(kept, block, jnp.zeros_like(block))
             block = slope_ref[k, span, :]
             both[k, span, orbitals:] = jnp.where(kept, block, jnp.zeros_like(block))
+    for k in range(each):
+        at = step * each + k
         near = window[pl.ds(pl.multiple_of(at * share, share), slots * share), :]
         product[k] = lax.dot_general(
             both[k], near, (((0,), (0,)), ((), ())), preferred_element_type=jnp.float32
         )
+    for k in range(each):
         keep_ref[k] = 2.0 * product[k, pl.ds(mine, share), :] - prev_ref[k].astype(jnp.float32)
         send_ref[k] = (2.0 * product[k, pl.ds(other, share), :]).astype(send_ref.dtype)
         work = product[k, orbitals:, :] * cot_ref[k].astype(jnp.float32)

time: 77.2 us -> 77.2 us (level)
  no operation moved by 1% of the time
where the time goes in v7:
time: 77.2 us; the launch traced here: 76.7 us
  Pallas kernels  43.9 us (57%)
  starting transfers between devices  12.7 us (16%)
  waiting for transfers between devices  8.87 us (11%)
  blocking collectives  5.23 us (7%)
  local copies, waits for them, and re-layouts  4.28 us (6%)
  other arithmetic  1.01 us (1%)
    pallas_call x2, Pallas kernels, pull(): pl.pallas_call(kernel, out_shape=tuple((jax.ShapeDtypeStruct(a.shape, a.d...  24.2 us
    pallas_call x1, Pallas kernels, push(): pl.pallas_call(kernel, out_shape=(jax.ShapeDtypeStruct((reach * share, co...  15.8 us
    ppermute x4, starting transfers between devices, shifted(): return lax.ppermute(value, axis, pairs)  9.29 us
    ppermute x4, waiting for transfers between devices, shifted(): return lax.ppermute(value, axis, pairs)  5.38 us
    all_gather x1, blocking collectives, local(): gathered = lax.all_gather(forces, 'cols')  5.23 us
    pallas_call x4, Pallas kernels, add_parts(): pl.pallas_call(functools.partial(add_kernel, steps), out_shape=jax.ShapeD...  3.85 us
    ppermute x4, waiting for transfers between devices, swapped(): lax.ppermute(value, axis, [(source, source ^ bit) for source in range(cou...  3.49 us
    ppermute x4, starting transfers between devices, swapped(): lax.ppermute(value, axis, [(source, source ^ bit) for source in range(cou...  3.43 us
  transfers between devices with their start and end apart: 8, of which 4 were waited for; matrix products, arithmetic and copies ran while one was open for 1% of the time, Pallas kernels for 56%

profile of v7, /device:TPU:0, one launch (start us, length us, event | category | flops | bytes accessed | tf_op | source)
XLA Modules:
  0.0 76.7 jit_solution(13880620126708573308)
XLA Ops:
  0.6 1.2 %slice.12 = bf16[12,64,512]{2,1,0:T(8,128)(2,1)S(1)} slice(bf16[24,64,512]{2,1,0:T(8,128)(2,1)} %param.7), slice={[12:24], [0:64], [0:512]} | slice | bytes 1572864 | tf_op jit(solution)/shard_map/slice | solution.py:277
  1.8 3.1 %collective-permute-start.1 = (bf16[768,512]{1,0:T(8,128)(2,1)S(1)}, bf16[768,512]{1,0:T(8,128)(2,1)S(1)}, u32[]{:S(2)}, u32[]{:S(2)}) collective-permute-start(bf16[768,512]{1,0:T(8,128)(2,1)S(1)} %bitcast.28), channel_id=1, source_target_pairs={{0,8},{8,16},{16,24},{24,0},{1,9},{9,17},{17,25},{25,1},{2,10},{10... | collective-permute-start | bytes 2359304 | tf_op jit(solution)/shard_map/ppermute | solution.py:19
  4.9 15.8 %push_blocks.1 = (bf16[768,512]{1,0:T(8,128)(2,1)}, f32[1536,512]{1,0:T(8,128)}, bf16[768,512]{1,0:T(8,128)(2,1)}, bf16[768,512]{1,0:T(8,128)(2,1)}) custom-call(s32[24,25]{1,0:T(8,128)} %mask_ref.5, bf16[24,1600,128]{2,1,0:T(8,128)(2,1)} %bitcast.18, bf16[24,128,512]{2,1,0:T(8,128)(2,1)} %cot_ref.5, bf16[1536,512]{1,0:T(8,128)(2,1)} %bitcast.23), custom_call_target="tpu_custom_call" | custom-call | flops 5033164800 | bytes 9830400 | tf_op jit(solution)/shard_map/push_blocks/pallas_call | solution.py:85
  20.7 2.0 %collective-permute-start = (bf16[768,512]{1,0:T(8,128)(2,1)}, bf16[768,512]{1,0:T(8,128)(2,1)S(1)}, u32[]{:S(2)}, u32[]{:S(2)}) collective-permute-start(bf16[768,512]{1,0:T(8,128)(2,1)} %get-tuple-element.25), channel_id=1, source_target_pairs={{0,24},{8,0},{16,8},{24,16},{1,25},{9,1},{17,9},{25,17},{2,26},{10... | collective-permute-start | bytes 2359304 | tf_op jit(solution)/shard_map/ppermute | solution.py:19
  22.7 1.8 %collective-permute-done.1.head_ref = bf16[768,512]{1,0:T(8,128)(2,1)S(1)} collective-permute-done((bf16[768,512]{1,0:T(8,128)(2,1)S(1)}, bf16[768,512]{1,0:T(8,128)(2,1)S(1)}, u32[]{:S(2)}, u32[]{:S(2)}) %collective-permute-start.1) | collective-permute-done | bytes 786464 | tf_op jit(solution)/shard_map/ppermute | solution.py:19
  24.6 0.0 copy-done.4
  24.6 12.1 %pull_blocks.2 = (bf16[768,512]{1,0:T(8,128)(2,1)}, f32[24,64,512]{2,1,0:T(8,128)}, bf16[12,64,512]{2,1,0:T(8,128)(2,1)S(1)}, f32[12,1,128]{2,1,0:T(1,128)S(1)}) custom-call(s32[24,25]{1,0:T(8,128)S(1)} %copy-done.4, s32[1]{0:T(128)} %bitcast.side_ref, bf16[24,1600,128]{2,1,0:T(8,128)(2,1)} %bitcast.19, ...), custom_call_target="tpu_custom_call", output_to_operand_aliasing={{0}: (8, {})} | custom-call | flops 5033164800 | bytes 9830400 | tf_op jit(solution)/shard_map/pull_blocks/pallas_call | solution.py:175
  36.7 0.0 collective-permute-start.2
  36.7 0.0 collective-permute-start.6
  36.7 1.6 %collective-permute-start.7 = (bf16[12,64,512]{2,1,0:T(8,128)(2,1)S(1)}, bf16[12,64,512]{2,1,0:T(8,128)(2,1)S(1)}, u32[]{:S(2)}, u32[]{:S(2)}) collective-permute-start(bf16[12,64,512]{2,1,0:T(8,128)(2,1)S(1)} %get-tuple-element.37), channel_id=1, source_target_pairs={{0,1},{1,0},{2,3},{3,2},{4,5},{5,4},{6,7},{7,6},{8,9},{9,8},{10,11... | collective-permute-start | bytes 2359304 | tf_op jit(solution)/shard_map/ppermute | solution.py:24
  38.3 3.0 %collective-permute-done.tail_ref = bf16[768,512]{1,0:T(8,128)(2,1)S(1)} collective-permute-done((bf16[768,512]{1,0:T(8,128)(2,1)}, bf16[768,512]{1,0:T(8,128)(2,1)S(1)}, u32[]{:S(2)}, u32[]{:S(2)}) %collective-permute-start) | collective-permute-done | bytes 786464 | tf_op jit(solution)/shard_map/ppermute | solution.py:19
  41.3 0.0 collective-permute-done.2.rest_0_
  41.3 0.0 copy-done.3
  41.3 12.1 %pull_blocks.3 = (f32[12,1,128]{2,1,0:T(1,128)S(1)}, bf16[768,512]{1,0:T(8,128)(2,1)S(1)}, f32[24,64,512]{2,1,0:T(8,128)}, bf16[12,64,512]{2,1,0:T(8,128)(2,1)S(1)}, f32[12,1,128]{2,1,0:T(1,128)S(1)}) custom-call(s32[24,25]{1,0:T(8,128)S(1)} %copy-done.4, s32[1]{0:T(128)} %bitcast.side_ref, ...), custom_call_target="tpu_custom_call", output_to_operand_aliasing={{0}: (8, {}), {1}: (9, {}), {2}: (10, {})} | custom-call | flops 5033164800 | bytes 9830400 | tf_op jit(solution)/shard_map/pull_blocks/pallas_call | solution.py:175
  53.4 1.5 %collective-permute-start.5 = (bf16[12,64,512]{2,1,0:T(8,128)(2,1)S(1)}, bf16[12,64,512]{2,1,0:T(8,128)(2,1)S(1)}, u32[]{:S(2)}, u32[]{:S(2)}) collective-permute-start(bf16[12,64,512]{2,1,0:T(8,128)(2,1)S(1)} %get-tuple-element.34), channel_id=1, source_target_pairs={{0,1},{1,0},{2,3},{3,2},{4,5},{5,4},{6,7},{7,6},{8,9},{9,8},{10,11... | collective-permute-start | bytes 2359304 | tf_op jit(solution)/shard_map/ppermute | solution.py:24
  55.0 4.2 %collective-permute-start.3 = (bf16[768,512]{1,0:T(8,128)(2,1)S(1)}, bf16[768,512]{1,0:T(8,128)(2,1)S(1)}, u32[]{:S(2)}, u32[]{:S(2)}) collective-permute-start(bf16[768,512]{1,0:T(8,128)(2,1)S(1)} %get-tuple-element.30), channel_id=1, source_target_pairs={{0,24},{8,0},{16,8},{24,16},{1,25},{9,1},{17,9},{25,17},{2,26},{10... | collective-permute-start | bytes 2359304 | tf_op jit(solution)/shard_map/ppermute | solution.py:19
  59.2 0.0 copy-done.5
  59.2 0.4 select_reduce_fusion
  59.5 5.2 %all-gather = f32[96,64]{1,0:T(8,128)S(1)} all-gather(f32[24,64]{1,0:T(8,128)S(1)} %select_reduce_fusion), channel_id=2, replica_groups=mesh['rows'=4,'cols'=4,'layers'=2] {'cols'}, dimensions={0}, use_global_device_ids=true | all-gather | bytes 30720 | tf_op jit(solution)/shard_map/all_gather | solution.py:298
  64.8 0.3 collective-permute-start.4
  65.1 0.0 collective-permute-done.7
  65.1 1.9 %copy-done = f32[24,64,512]{2,1,0:T(8,128)S(1)} copy-done((f32[24,64,512]{2,1,0:T(8,128)S(1)}, f32[24,64,512]{2,1,0:T(8,128)}, u32[]{:S(2)}) %copy-start) | copy-done | bytes 3145752
  67.0 1.0 %add_parts.4.rest_0_ = bf16[1536,512]{1,0:T(8,128)(2,1)} custom-call(f32[1536,512]{1,0:T(8,128)S(1)} %bitcast.12, bf16[768,512]{1,0:T(8,128)(2,1)S(1)} %bitcast.14, bf16[768,512]{1,0:T(8,128)(2,1)S(1)} %bitcast.15), custom_call_target="tpu_custom_call" | custom-call | tf_op jit(solution)/shard_map/add_parts/pallas_call | solution.py:250
  68.0 0.0 collective-permute-done.6.first_ref.second_ref
  68.0 1.2 %copy-done.2 = f32[1536,512]{1,0:T(8,128)S(1)} copy-done((f32[1536,512]{1,0:T(8,128)S(1)}, f32[1536,512]{1,0:T(8,128)}, u32[]{:S(2)}) %copy-start.2) | copy-done | bytes 3145752
  69.2 1.0 %add_parts.5.rest_0_ = bf16[1536,512]{1,0:T(8,128)(2,1)} custom-call(f32[1536,512]{1,0:T(8,128)S(1)} %copy-done.2, bf16[768,512]{1,0:T(8,128)(2,1)S(1)} %collective-permute-done.6.first_ref.second_ref, bf16[768,512]{1,0:T(8,128)(2,1)S(1)} %collective-permute-done.6.first_ref.second_ref), custom_call_target="tpu_custom_call" | custom-call | tf_op jit(solution)/shard_map/add_parts/pallas_call | solution.py:250
  70.2 3.5 %collective-permute-done.5 = bf16[12,64,512]{2,1,0:T(8,128)(2,1)S(1)} collective-permute-done((bf16[12,64,512]{2,1,0:T(8,128)(2,1)S(1)}, bf16[12,64,512]{2,1,0:T(8,128)(2,1)S(1)}, u32[]{:S(2)}, u32[]{:S(2)}) %collective-permute-start.5) | collective-permute-done | bytes 786464 | tf_op jit(solution)/shard_map/ppermute | solution.py:24
  73.6 0.9 %add_parts.6 = bf16[1536,512]{1,0:T(8,128)(2,1)} custom-call(f32[1536,512]{1,0:T(8,128)S(1)} %bitcast.13, bf16[768,512]{1,0:T(8,128)(2,1)S(1)} %bitcast.16, bf16[768,512]{1,0:T(8,128)(2,1)S(1)} %bitcast.17, bf16[1536,512]{1,0:T(8,128)(2,1)} %add_parts.4.rest_0_), custom_call_target="tpu_custom_call", output_to_operand_aliasing={{}: (3, {})} | custom-call | tf_op jit(solution)/shard_map/add_parts/pallas_call | solution.py:250
  74.6 0.0 collective-permute-done.4
  74.6 0.6 fusion
  75.2 0.5 collective-permute-done.3.first_ref.second_ref
  75.8 0.9 %add_parts.7 = bf16[1536,512]{1,0:T(8,128)(2,1)} custom-call(f32[1536,512]{1,0:T(8,128)S(1)} %copy-done.2, bf16[768,512]{1,0:T(8,128)(2,1)S(1)} %collective-permute-done.3.first_ref.second_ref, bf16[768,512]{1,0:T(8,128)(2,1)S(1)} %collective-permute-done.3.first_ref.second_ref, bf16[1536,512]{1,0:T(8,128)(2,1)} %add_parts.5.rest_0_), custom_call_target="tpu_custom_call", output_to_operand_aliasing={{}: (3, {})} | custom-call | tf_op jit(solution)/shard_map/add_parts/pallas_call | solution.py:250
  (12 shorter events, 0.1 us)
Async XLA Ops:
  1.8 22.7 %collective-permute-start.1 = (bf16[768,512]{1,0:T(8,128)(2,1)S(1)}, bf16[768,512]{1,0:T(8,128)(2,1)S(1)}, u32[]{:S(2)}, u32[]{:S(2)}) collective-permute-start(bf16[768,512]{1,0:T(8,128)(2,1)S(1)} %bitcast.28), channel_id=1, source_target_pairs={{0,8},{8,16},{16,24},{24,0},{1,9},{9,17},{17,25},{25,1},{2,10},{10... | collective-permute-start | bytes 2359304 | tf_op jit(solution)/shard_map/ppermute | solution.py:19
  4.9 19.7 %copy-start.4 = (s32[24,25]{1,0:T(8,128)S(1)}, s32[24,25]{1,0:T(8,128)}, u32[]{:S(2)}) copy-start(s32[24,25]{1,0:T(8,128)} %mask_ref.5) | copy-start | bytes 7204
  20.7 20.6 %collective-permute-start = (bf16[768,512]{1,0:T(8,128)(2,1)}, bf16[768,512]{1,0:T(8,128)(2,1)S(1)}, u32[]{:S(2)}, u32[]{:S(2)}) collective-permute-start(bf16[768,512]{1,0:T(8,128)(2,1)} %get-tuple-element.25), channel_id=1, source_target_pairs={{0,24},{8,0},{16,8},{24,16},{1,25},{9,1},{17,9},{25,17},{2,26},{10... | collective-permute-start | bytes 2359304 | tf_op jit(solution)/shard_map/ppermute | solution.py:19
  24.6 16.8 %copy-start.3 = (bf16[768,512]{1,0:T(8,128)(2,1)S(1)}, bf16[768,512]{1,0:T(8,128)(2,1)}, u32[]{:S(2)}) copy-start(bf16[768,512]{1,0:T(8,128)(2,1)} %get-tuple-element.28.rest_1_) | copy-start | bytes 2359300
  36.7 4.6 %collective-permute-start.2 = (f32[12,1,128]{2,1,0:T(1,128)S(1)}, f32[12,1,128]{2,1,0:T(1,128)S(1)}, u32[]{:S(2)}, u32[]{:S(2)}) collective-permute-start(f32[12,1,128]{2,1,0:T(1,128)S(1)} %get-tuple-element.27), channel_id=1, source_target_pairs={{0,2},{2,0},{4,6},{6,4},{1,3},{3,1},{5,7},{7,5},{8,10},{10,8},{12,... | collective-permute-start | bytes 18440 | tf_op jit(solution)/shard_map/ppermute | solution.py:24
  36.7 31.3 %collective-permute-start.6 = (bf16[768,512]{1,0:T(8,128)(2,1)}, bf16[768,512]{1,0:T(8,128)(2,1)S(1)}, u32[]{:S(2)}, u32[]{:S(2)}) collective-permute-start(bf16[768,512]{1,0:T(8,128)(2,1)} %get-tuple-element.36), channel_id=1, source_target_pairs={{0,8},{8,16},{16,24},{24,0},{1,9},{9,17},{17,25},{25,1},{2,10},{10... | collective-permute-start | bytes 2359304 | tf_op jit(solution)/shard_map/ppermute | solution.py:19
  36.7 28.4 %collective-permute-start.7 = (bf16[12,64,512]{2,1,0:T(8,128)(2,1)S(1)}, bf16[12,64,512]{2,1,0:T(8,128)(2,1)S(1)}, u32[]{:S(2)}, u32[]{:S(2)}) collective-permute-start(bf16[12,64,512]{2,1,0:T(8,128)(2,1)S(1)} %get-tuple-element.37), channel_id=1, source_target_pairs={{0,1},{1,0},{2,3},{3,2},{4,5},{5,4},{6,7},{7,6},{8,9},{9,8},{10,11... | collective-permute-start | bytes 2359304 | tf_op jit(solution)/shard_map/ppermute | solution.py:24
  41.3 17.8 %copy-start.5 = (s32[24,128]{1,0:T(8,128)S(1)}, s32[24,128]{1,0:T(8,128)}, u32[]{:S(2)}) copy-start(s32[24,128]{1,0:T(8,128)} %param.13) | copy-start | bytes 36868
  53.4 20.2 %collective-permute-start.5 = (bf16[12,64,512]{2,1,0:T(8,128)(2,1)S(1)}, bf16[12,64,512]{2,1,0:T(8,128)(2,1)S(1)}, u32[]{:S(2)}, u32[]{:S(2)}) collective-permute-start(bf16[12,64,512]{2,1,0:T(8,128)(2,1)S(1)} %get-tuple-element.34), channel_id=1, source_target_pairs={{0,1},{1,0},{2,3},{3,2},{4,5},{5,4},{6,7},{7,6},{8,9},{9,8},{10,11... | collective-permute-start | bytes 2359304 | tf_op jit(solution)/shard_map/ppermute | solution.py:24
  55.0 20.8 %collective-permute-start.3 = (bf16[768,512]{1,0:T(8,128)(2,1)S(1)}, bf16[768,512]{1,0:T(8,128)(2,1)S(1)}, u32[]{:S(2)}, u32[]{:S(2)}) collective-permute-start(bf16[768,512]{1,0:T(8,128)(2,1)S(1)} %get-tuple-element.30), channel_id=1, source_target_pairs={{0,24},{8,0},{16,8},{24,16},{1,25},{9,1},{17,9},{25,17},{2,26},{10... | collective-permute-start | bytes 2359304 | tf_op jit(solution)/shard_map/ppermute | solution.py:19
  64.8 9.8 %collective-permute-start.4 = (f32[24,64]{1,0:T(8,128)S(1)}, f32[24,64]{1,0:T(8,128)S(1)}, u32[]{:S(2)}, u32[]{:S(2)}) collective-permute-start(f32[24,64]{1,0:T(8,128)S(1)} %pad_maximum_fusion.1), channel_id=1, source_target_pairs={{0,1},{1,0},{2,3},{3,2},{4,5},{5,4},{6,7},{7,6},{8,9},{9,8},{10,11... | collective-permute-start | bytes 18440 | tf_op jit(solution)/shard_map/ppermute | solution.py:24
  65.1 1.9 %copy-start = (f32[24,64,512]{2,1,0:T(8,128)S(1)}, f32[24,64,512]{2,1,0:T(8,128)}, u32[]{:S(2)}) copy-start(f32[24,64,512]{2,1,0:T(8,128)} %get-tuple-element.33) | copy-start | bytes 9437188
  67.0 2.2 %copy-start.2 = (f32[1536,512]{1,0:T(8,128)S(1)}, f32[1536,512]{1,0:T(8,128)}, u32[]{:S(2)}) copy-start(f32[1536,512]{1,0:T(8,128)} %get-tuple-element.35.own_ref) | copy-start | bytes 9437188
  69.2 4.5 %copy-start.1 = (f32[24,64,512]{2,1,0:T(8,128)S(1)}, f32[24,64,512]{2,1,0:T(8,128)}, u32[]{:S(2)}) copy-start(f32[24,64,512]{2,1,0:T(8,128)} %get-tuple-element.33) | copy-start | bytes 9437188
